TPU v7x, 32 devices: a whole 2x2x4 slice. The times are simulated.
32 devices in a mesh: member: 8 (over y, x, core), tile: 4 (over z).
Axes of the slice: x: 2, y: 2, z: 4, core: 2. Of those that a mesh axis runs over, the one named last changes fastest.
Arguments:
- perturbations: bfloat16 [64, 2, 5, 8, 8, 512], P('member', None, None, None, None, 'tile'), may hold values from -6 to 6
- gradient_store: float32 [2, 5, 8, 8, 512], P(None, None, None, 'member', 'tile'), may hold values from -6 to 6
- diffusivity: float32 [8, 8, 512], P(None, None, 'tile'), may hold values from 0.2 to 0.4
- slab_owner: int32 [8], replicated, may hold values from 0 to 7, each once
Outputs:
- increment_store: float32 [2, 5, 8, 8, 512], P(None, None, None, 'member', 'tile')
Inputs may be any that keep to these rules, and one draw needn't show every extreme that they name: `slab_owner`: each member index holds exactly one slab.
All inputs are finite; a program needn't handle non-finite values.
Results may differ from a plain program's by a relative error of at most 0.0003.
Values sent between devices are 32-bit elements; how exact they have to be, the bound alone decides.
No kernel may reach another device: no remote copies, remote signals or barrier semaphores. Data moves between devices by JAX's collectives and lax.ppermute only.
A program may use at most 128 MiB of HBM per device.

v0:
```python
import math

import jax
import jax.numpy as jnp
from jax import lax
from jax.experimental import pallas as pl
from jax.experimental.pallas import tpu as pltpu
from jax.sharding import PartitionSpec as P

SWEEPS = 10
GROUPS = 4
ANCHOR_WORK = 10**10
VMEM_LIMIT = 16 * 1024 * 1024


def lane_roll(value, shift):
    shift = shift % value.shape[-1]
    return value if shift == 0 else pltpu.roll(value, shift, 1)


def lane_index(shape):
    return lax.broadcasted_iota(jnp.int32, shape, 1)


def spread(row, rows=8):
    return jnp.broadcast_to(row, (rows, row.shape[-1]))


def whole(memory_space=pltpu.VMEM):
    return pl.BlockSpec(memory_space=memory_space)


def mirrors(level, row, levels, rows):
    return [
        (far_level, far_row)
        for far_level in (level, levels - 1 - level)
        for far_row in (row, rows - 1 - row)
    ]


def group_index(shape, start):
    part = shape[-1] // GROUPS
    return (lane_index(shape) + start) % shape[-1] // part


def own_strips(values):
    part = values[0].shape[-1] // GROUPS
    rolled = [lane_roll(value, part * g) for g, value in enumerate(values)]
    both = []
    for start in (SWEEPS, part - SWEEPS):
        group = group_index(values[0].shape, start)
        strip = rolled[0]
        for g in range(1, GROUPS):
            strip = jnp.where(group == g, rolled[g], strip)
        both.append(strip)
    return both


def packed_edges(first, second):
    part = first.shape[-1] // GROUPS
    place = lane_index(first.shape) % part
    moved = lane_roll(second, part // 2)
    to_right = jnp.where(place >= part // 2, first, moved)
    to_left = jnp.where(place < part // 2, first, moved)
    return to_right, to_left


def joined_strip(own, edge, index, is_left):
    part = own.shape[-1] // GROUPS
    place = lane_index(own.shape) % part
    edge = lane_roll(edge, -(index % 2) * (part // 2))
    return jnp.where(place >= part - SWEEPS if is_left else place < SWEEPS, edge, own)


def row_mirrored(value, start):
    part = value.shape[-1] // GROUPS
    group = group_index(value.shape, start)
    return jnp.where(group % 2 == 0, lane_roll(value, -part), lane_roll(value, part))


def total(terms):
    terms = list(terms)
    while len(terms) > 1:
        terms = [
            terms[i] + terms[i + 1] if i + 1 < len(terms) else terms[i]
            for i in range(0, len(terms), 2)
        ]
    return terms[0]


def around(planes, level, row, start=None):
    levels, rows = len(planes), len(planes[level])
    here = planes[level][row]
    terms = [lane_roll(here, 1), lane_roll(here, -1)]
    if row > 0:
        terms.append(planes[level][row - 1])
    if row < rows - 1:
        terms.append(planes[level][row + 1])
    elif start is not None:
        terms.append(row_mirrored(here, start))
    if level > 0:
        terms.append(planes[level - 1][row])
    if level < levels - 1:
        terms.append(planes[level + 1][row])
    elif start is not None:
        terms.append(lane_roll(here, here.shape[-1] // 2))
    return total(terms)


def sweep(source, target, keep_at, square_at, start=None):
    levels, rows = source.shape[0], source.shape[1]
    planes = [[source[level, row] for row in range(rows)] for level in range(levels)]
    for level in range(levels):
        for row in range(rows):
            target[level, row] = keep_at(level, row) * planes[level][row] + square_at(
                level, row
            ) * around(planes, level, row, start)


def anchor_kernel(out_ref):
    out_ref[...] = jnp.zeros_like(out_ref)


def weigh_kernel(
    owner_ref,
    gathered_ref,
    pert_ref,
    coeff_ref,
    anchor_ref,
    field_ref,
    left_ref,
    right_ref,
    coeff_left_ref,
    coeff_right_ref,
    to_right_ref,
    to_left_ref,
    grad_ref,
):
    members, terms, levels, rows, lanes = pert_ref.shape
    slab_rows = gathered_ref.shape[2]
    strip_levels, strip_rows = left_ref.shape[:2]
    for slab in range(rows // slab_rows):
        owner = owner_ref[slab]
        for term in range(terms):
            for inner in range(slab_rows):
                row = slab * slab_rows + inner
                grad_ref[pl.ds(term * levels * rows + row, levels, stride=rows), :] = gathered_ref[
                    owner, term, inner
                ]

    for level in range(levels):
        base = level * rows
        coeff = coeff_ref[level]
        gradients = [
            coeff * grad_ref[pl.ds(term * levels * rows + base, rows), :] for term in range(terms)
        ]
        for member in range(members):
            field_ref[pl.ds(base * members + member, rows, stride=members), :] = total(
                pert_ref[member, term, level].astype(jnp.float32) * gradients[term]
                for term in range(terms)
            )

    pairs = strip_levels * strip_rows // 2
    fields, coeffs = [], []
    for level in range(strip_levels):
        for row in range(strip_rows):
            index = level * strip_rows + row
            cells = mirrors(level, row, levels, rows)
            field = own_strips(
                [field_ref[pl.ds((l * rows + r) * members, members), :] for l, r in cells]
            )
            coeff = own_strips([spread(coeff_ref[l, pl.ds(r, 1), :]) for l, r in cells])
            left_ref[level, row], right_ref[level, row] = field
            coeff_left_ref[pl.ds(index, 1), :] = coeff[0][0:1]
            coeff_right_ref[pl.ds(index, 1), :] = coeff[1][0:1]
            fields.append(field[0])
            coeffs.append(coeff[0])
    for pair in range(pairs):
        edges = packed_edges(fields[2 * pair], fields[2 * pair + 1])
        coeff_edges = packed_edges(coeffs[2 * pair], coeffs[2 * pair + 1])
        for ref, edge, coeff_edge in zip((to_right_ref, to_left_ref), edges, coeff_edges):
            ref[pl.ds(pair * members, members), :] = edge
            ref[pl.ds(pairs * members + pair, 1), :] = coeff_edge[0:1]


def interior_kernel(
    field_ref, coeff_ref, pert_ref, out_ref, ends_ref, other_ref, keep_ref, square_ref, inverse_ref
):
    levels, rows, members, lanes = field_ref.shape
    terms = pert_ref.shape[1]
    width = lanes // levels
    slot = lane_index((rows, lanes)) // width

    def pack_ends(member):
        for term in range(terms):
            ends = None
            for index, level in enumerate(level_slots(levels)):
                value = pert_ref[member, term, level].astype(jnp.float32)
                moved = lane_roll(value, width * (index + 1))
                ends = moved if ends is None else jnp.where(slot == index, moved, ends)
            ends_ref[member, term] = ends

    row_index = lax.broadcasted_iota(jnp.int32, (rows, lanes), 0)
    for level in range(levels):
        here = coeff_ref[level]
        beside = [
            lane_roll(here, 1),
            lane_roll(here, -1),
            jnp.where(row_index > 0, pltpu.roll(here, 1, 0), 0.0),
            jnp.where(row_index < rows - 1, pltpu.roll(here, rows - 1, 0), 0.0),
        ]
        if level > 0:
            beside.append(coeff_ref[level - 1])
        if level < levels - 1:
            beside.append(coeff_ref[level + 1])
        keep_ref[level] = 1.0 - here * total(beside)
        square_ref[level] = here * here
        inverse_ref[level] = 1.0 / here

    def keep_at(level, row):
        return keep_ref[level, pl.ds(row, 1), :]

    def square_at(level, row):
        return square_ref[level, pl.ds(row, 1), :]

    sweep(field_ref, other_ref, keep_at, square_at)
    sweep(other_ref, out_ref, keep_at, square_at)

    pairs = SWEEPS // 2 - 1
    share = members // pairs

    def pair(index, carry):
        sweep(out_ref, other_ref, keep_at, square_at)
        sweep(other_ref, out_ref, keep_at, square_at)
        for extra in range(share):
            pack_ends(index * share + extra)
        return carry

    lax.fori_loop(0, pairs, pair, 0)
    for member in range(pairs * share, members):
        pack_ends(member)
    for level in range(levels):
        for row in range(rows):
            out_ref[level, row] = out_ref[level, row] * inverse_ref[level, pl.ds(row, 1), :]


def swept_strips(strip_ref, coeff_ref, edge_ref, is_left, keep_ref, square_ref):
    strip_levels, strip_rows, members, lanes = strip_ref.shape
    part = lanes // GROUPS
    start = SWEEPS if is_left else part - SWEEPS
    pairs = strip_levels * strip_rows // 2
    planes, coeffs = [], []
    for level in range(strip_levels):
        plane, coeff_plane = [], []
        for row in range(strip_rows):
            index = level * strip_rows + row
            edge = edge_ref[pl.ds(index // 2 * members, members), :]
            coeff_edge = spread(edge_ref[pl.ds(pairs * members + index // 2, 1), :])
            plane.append(joined_strip(strip_ref[level, row], edge, index, is_left))
            coeff_plane.append(
                joined_strip(spread(coeff_ref[pl.ds(index, 1), :]), coeff_edge, index, is_left)
            )
        planes.append(plane)
        coeffs.append(coeff_plane)
    for level in range(strip_levels):
        for row in range(strip_rows):
            here = coeffs[level][row]
            keep_ref[level, row] = 1.0 - here * around(coeffs, level, row, start)
            square_ref[level, row] = here * here
    for _ in range(SWEEPS):
        planes = [
            [
                keep_ref[level, row] * planes[level][row]
                + square_ref[level, row] * around(planes, level, row, start)
                for row in range(strip_rows)
            ]
            for level in range(strip_levels)
        ]
    for level in range(strip_levels):
        for row in range(strip_rows):
            coeff = spread(coeff_ref[pl.ds(level * strip_rows + row, 1), :])
            planes[level][row] = planes[level][row] / jnp.where(coeff > 0.0, coeff, 1.0)
    return planes


def level_slots(levels):
    near = list(range(levels // 2))
    return near + [levels - 1 - level for level in near]


def partial_kernel(
    pert_ref, interior_ref, strip_ref, coeff_ref, edge_ref, out_ref, local_ref, keep_ref, square_ref
):
    members, terms, levels, rows, lanes = pert_ref.shape
    part = lanes // GROUPS
    planes = swept_strips(strip_ref, coeff_ref, edge_ref, True, keep_ref, square_ref)
    lane = lane_index((members, lanes))
    for level, plane in enumerate(planes):
        for row, final in enumerate(plane):
            for g, (l, r) in enumerate(mirrors(level, row, levels, rows)):
                local_ref[pl.ds((l * rows + r) * members, members), :] = jnp.where(
                    lane < SWEEPS, lane_roll(final, -part * g), interior_ref[l, r]
                )

    for level in range(levels):
        base = level * rows
        fields = [
            local_ref[pl.ds(base * members + member, rows, stride=members), :]
            for member in range(members)
        ]
        for term in range(terms):
            out_ref[pl.ds(term * levels * rows + base, rows), :] = total(
                pert_ref[member, term, level].astype(jnp.float32) * fields[member]
                for member in range(members)
            )


def finish_kernel(
    owner_ref,
    ends_ref,
    partial_ref,
    strip_ref,
    coeff_ref,
    edge_ref,
    out_ref,
    local_ref,
    sum_ref,
    keep_ref,
    square_ref,
):
    members, terms, rows, lanes = ends_ref.shape
    slab_rows, levels = out_ref.shape[2], out_ref.shape[3]
    part, half, width = lanes // GROUPS, lanes // 2, lanes // levels
    planes = swept_strips(strip_ref, coeff_ref, edge_ref, False, keep_ref, square_ref)
    strip_levels, strip_rows = len(planes), len(planes[0])
    slot = lane_index((members, lanes)) % half // width
    for row in range(strip_rows):
        for mirror in range(2):
            ends = None
            for level in range(strip_levels):
                moved = lane_roll(planes[level][row], width * (level + 1) - part * mirror)
                ends = moved if ends is None else jnp.where(slot == level, moved, ends)
            target = rows - 1 - row if mirror else row
            local_ref[pl.ds(target, members, stride=rows), :] = ends
    fields = [local_ref[pl.ds(member * rows, rows), :] for member in range(members)]
    lane = lane_index((rows, lanes))
    for term in range(terms):
        added = total(ends_ref[member, term] * fields[member] for member in range(members))
        for index, level in enumerate(level_slots(levels)):
            place = pl.ds((term * levels + level) * rows, rows)
            sum_ref[place, :] = jnp.where(
                lane >= lanes - SWEEPS, lane_roll(added, -width * (index + 1)), partial_ref[place, :]
            )
    for slab in range(rows // slab_rows):
        owner = owner_ref[slab]
        for term in range(terms):
            for inner in range(slab_rows):
                row = slab * slab_rows + inner
                out_ref[owner, term, inner] = sum_ref[
                    pl.ds(term * levels * rows + row, levels, stride=rows), :
                ]


def local_call(kernel, name, outs, scratch, operands, places, work):
    def shape_of(out):
        return out if isinstance(out, jax.ShapeDtypeStruct) else jax.ShapeDtypeStruct(out, jnp.float32)

    shapes = tuple(shape_of(out) for out in outs)
    specs = tuple(whole() for _ in outs)
    moved = sum(math.prod(x.shape) * x.dtype.itemsize for x in tuple(operands) + shapes)
    single = len(outs) == 1
    return pl.pallas_call(
        kernel,
        out_shape=shapes[0] if single else shapes,
        in_specs=[whole(place) for place in places],
        out_specs=specs[0] if single else specs,
        scratch_shapes=[
            pltpu.VMEM(item, jnp.float32) if isinstance(item, tuple) else item for item in scratch
        ],
        compiler_params=pltpu.CompilerParams(vmem_limit_bytes=VMEM_LIMIT),
        cost_estimate=pl.CostEstimate(flops=work, bytes_accessed=moved, transcendentals=0),
        name=name,
    )(*operands)


def body(perturbations, gradient_store, diffusivity, slab_owner):
    members, slots, variables, levels, rows, lanes = perturbations.shape
    terms = slots * variables
    n_member = lax.axis_size("member")
    n_tile = lax.axis_size("tile")
    slab_rows = gradient_store.shape[3]
    cells = levels * rows * lanes
    strip_levels, strip_rows = levels // 2, rows // 2
    strips = strip_levels * strip_rows
    wide_strip = (strip_levels, strip_rows, members, lanes)
    coeff_wide_strip = (strip_levels, strip_rows, 8, lanes)
    strip_scratch = [coeff_wide_strip, coeff_wide_strip]
    coeff_strip = (strips, lanes)
    wide_field = (levels, rows, members, lanes)
    flat_field = (levels * rows * members, lanes)
    field_coeff = (levels, rows, lanes)
    edge_shape = (strips // 2 * (members + 1), lanes)
    grad_shape = (terms * levels * rows, lanes)
    vmem, smem = pltpu.VMEM, pltpu.SMEM

    pert = perturbations.reshape(members, terms, levels, rows, lanes)
    slab = gradient_store.reshape(terms, levels, slab_rows, lanes).swapaxes(1, 2)
    anchor = local_call(anchor_kernel, "anchor", [(8, lanes)], [], (), (), ANCHOR_WORK)
    gathered = lax.all_gather(slab, "member", axis=0, tiled=False)

    field, left, right, coeff_left, coeff_right, to_right, to_left = local_call(
        weigh_kernel,
        "weigh",
        [flat_field, wide_strip, wide_strip, coeff_strip, coeff_strip, edge_shape, edge_shape],
        [grad_shape],
        (slab_owner, gathered, pert, diffusivity, anchor),
        (smem, vmem, vmem, vmem, vmem),
        2 * terms * members * cells,
    )
    up = [(i, i + 1) for i in range(n_tile - 1)]
    down = [(i + 1, i) for i in range(n_tile - 1)]
    from_left = lax.ppermute(to_right, "tile", up)
    from_right = lax.ppermute(to_left, "tile", down)

    interior, ends = local_call(
        interior_kernel,
        "interior",
        [wide_field, (members, terms, rows, lanes)],
        [wide_field, field_coeff, field_coeff, field_coeff],
        (field.reshape(wide_field), diffusivity, pert),
        (vmem,) * 3,
        8 * SWEEPS * members * cells,
    )
    partial = local_call(
        partial_kernel,
        "partial",
        [grad_shape],
        [flat_field] + strip_scratch,
        (pert, interior, left, coeff_left, from_left),
        (vmem,) * 5,
        2 * SWEEPS * members * cells,
    )
    sums = local_call(
        finish_kernel,
        "finish",
        [(n_member, terms, slab_rows, levels, lanes)],
        [(members * rows, lanes), grad_shape] + strip_scratch,
        (slab_owner, ends, partial, right, coeff_right, from_right),
        (smem,) + (vmem,) * 5,
        2 * terms * members * cells,
    )
    received = lax.all_to_all(sums, "member", 0, 0, tiled=True)
    norm_factor = 1.0 / (members * n_member - 1)
    owned = jnp.sum(received, axis=0) * norm_factor
    return owned.swapaxes(1, 2).reshape(slots, variables, levels, slab_rows, lanes)


def solution(mesh):
    in_specs = (
        P("member", None, None, None, None, "tile"),
        P(None, None, None, "member", "tile"),
        P(None, None, "tile"),
        P(),
    )
    out_specs = P(None, None, None, "member", "tile")
    return jax.shard_map(body, mesh=mesh, in_specs=in_specs, out_specs=out_specs, check_vma=False)
```

profile of v0, /device:TPU:0, one launch (start us, length us, event | category | flops | bytes accessed | tf_op | source)
XLA Modules:
  0.0 34.7 jit_solution(3859656204627254193)
XLA Ops:
  0.0 0.0 copy-start.3
  0.0 0.0 copy-start.2
  0.0 0.0 copy-start.1
  0.0 0.0 copy-start
  0.0 0.8 %copy-done.3 = f32[2,5,8,1,128]{4,3,2,1,0:T(1,128)S(1)} copy-done((f32[2,5,8,1,128]{4,3,2,1,0:T(1,128)S(1)}, f32[2,5,8,1,128]{4,3,2,1,0:T(1,128)}, u32[]{:S(2)}) %copy-start.3) | copy-done | bytes 40984
  0.8 10.9 %all_gather.3.gathered_ref = f32[8,10,1,8,128]{4,3,2,1,0:T(8,128)S(1)} all-gather(f32[1,10,1,8,128]{4,3,2,1,0:T(8,128)S(1)} %bitcast.8), channel_id=1, replica_groups=mesh['member'=8,'tile'=4] {'member'}, dimensions={0}, use_global_device_ids=true | all-gather | bytes 368640 | tf_op jit(solution)/shard_map/all_gather | solution.py:409
  11.7 0.0 copy-done.2
  11.7 0.0 copy-done.1
  11.7 0.0 copy-done
  11.7 1.1 %weigh.1 = (f32[512,128]{1,0:T(8,128)S(1)}, f32[4,4,8,128]{3,2,1,0:T(8,128)S(1)}, f32[4,4,8,128]{3,2,1,0:T(8,128)S(1)}, f32[16,128]{1,0:T(8,128)S(1)}, f32[16,12...) custom-call(s32[8]{0:T(128)S(1)} %copy-done.2, f32[8,10,1,8,128]{4,3,2,1,0:T(8,128)S(1)} %all_gather.3.gathered_ref, ...), custom_call_target="tpu_custom_call" | custom-call | flops 1310720 | bytes 2158624 | tf_op jit(solution)/shard_map/weigh/pallas_call | solution.py:372
  12.8 3.5 %collective-permute-start = (f32[72,128]{1,0:T(8,128)S(1)}, f32[72,128]{1,0:T(8,128)S(1)}, u32[]{:S(2)}, u32[]{:S(2)}) collective-permute-start(f32[72,128]{1,0:T(8,128)S(1)} %get-tuple-element.19), channel_id=1, source_target_pairs={{0,1},{1,2},{2,3},{4,5},{5,6},{6,7},{8,9},{9,10},{10,11},{12,13},{... | collective-permute-start | bytes 110600 | tf_op jit(solution)/shard_map/ppermute | solution.py:422
  16.3 1.3 %collective-permute-start.1 = (f32[72,128]{1,0:T(8,128)S(1)}, f32[72,128]{1,0:T(8,128)S(1)}, u32[]{:S(2)}, u32[]{:S(2)}) collective-permute-start(f32[72,128]{1,0:T(8,128)S(1)} %get-tuple-element.22), channel_id=1, source_target_pairs={{1,0},{2,1},{3,2},{5,4},{6,5},{7,6},{9,8},{10,9},{11,10},{13,12},{... | collective-permute-start | bytes 110600 | tf_op jit(solution)/shard_map/ppermute | solution.py:423
  17.6 2.1 %interior.1 = (f32[8,8,8,128]{3,2,1,0:T(8,128)S(1)}, f32[8,10,8,128]{3,2,1,0:T(8,128)S(1)}) custom-call(f32[8,8,8,128]{3,2,1,0:T(8,128)S(1)} %bitcast.7, f32[8,8,128]{2,1,0:T(8,128)S(1)} %copy-done.1, bf16[8,10,8,8,128]{4,3,2,1,0:T(8,128)(2,1)S(1)} %bitcast.5), custom_call_target="tpu_custom_call" | custom-call | flops 5242880 | bytes 2195456 | tf_op jit(solution)/shard_map/interior/pallas_call | solution.py:372
  19.6 0.0 collective-permute-done.edge_ref
  19.6 1.3 %partial.1.partial_ref = f32[640,128]{1,0:T(8,128)S(1)} custom-call(bf16[8,10,8,8,128]{4,3,2,1,0:T(8,128)(2,1)S(1)} %bitcast.6, f32[8,8,8,128]{3,2,1,0:T(8,128)S(1)} %get-tuple-element.16.interior_ref, f32[4,4,8,128]{3,2,1,0:T(8,128)S(1)} %get-tuple-element.17.strip_ref, f32[16,128]{1,0:T(8,128)S(1)} %get-tuple-element.18.coeff_ref, ...), custom_call_target="tpu_custom_call" | custom-call | flops 1310720 | bytes 2011136 | tf_op jit(solution)/shard_map/partial/pallas_call | solution.py:372
  21.0 1.2 %collective-permute-done.1.edge_ref = f32[72,128]{1,0:T(8,128)S(1)} collective-permute-done((f32[72,128]{1,0:T(8,128)S(1)}, f32[72,128]{1,0:T(8,128)S(1)}, u32[]{:S(2)}, u32[]{:S(2)}) %collective-permute-start.1) | collective-permute-done | bytes 36896 | tf_op jit(solution)/shard_map/ppermute | solution.py:423
  22.1 1.8 %finish.1 = f32[8,10,1,8,128]{4,3,2,1,0:T(8,128)S(1)} custom-call(s32[8]{0:T(128)S(1)} %copy-done.2, f32[8,10,8,128]{3,2,1,0:T(8,128)S(1)} %get-tuple-element.15.ends_ref, f32[640,128]{1,0:T(8,128)S(1)} %partial.1.partial_ref, f32[4,4,8,128]{3,2,1,0:T(8,128)S(1)} %get-tuple-element.20.strip_ref, f32[16,128]{1,0:T(8,128)S(1)} %get-tuple-element.21.coeff_ref, ...), custom_call_target="tpu_custom_call" | custom-call | flops 1310720 | bytes 1093664 | tf_op jit(solution)/shard_map/finish/pallas_call | solution.py:372
  23.9 10.2 %all_to_all.5 = f32[8,10,1,8,128]{4,3,2,1,0:T(8,128)S(1)} all-to-all(f32[8,10,1,8,128]{4,3,2,1,0:T(8,128)S(1)} %finish.1), channel_id=1, replica_groups=mesh['member'=8,'tile'=4] {'member'}, dimensions={0} | all-to-all | bytes 655360 | tf_op jit(solution)/shard_map/all_to_all | solution.py:452
  34.1 0.6 %broadcast_multiply_fusion = f32[10,8,128]{2,1,0:T(8,128)} fusion(f32[10,8,128]{2,1,0:T(8,128)S(1)} %reduce_sum.9), kind=kLoop, calls=%fused_computation | loop fusion | flops 10240 | bytes 81920 | tf_op jit(solution)/shard_map/mul | solution.py:454
  (2 shorter events, 0.0 us)
Async XLA Ops:
  0.0 0.8 %copy-start.3 = (f32[2,5,8,1,128]{4,3,2,1,0:T(1,128)S(1)}, f32[2,5,8,1,128]{4,3,2,1,0:T(1,128)}, u32[]{:S(2)}) copy-start(f32[2,5,8,1,128]{4,3,2,1,0:T(1,128)} %param.5) | copy-start | bytes 122884
  0.0 11.7 %copy-start.2 = (s32[8]{0:T(128)S(1)}, s32[8]{0:T(128)}, u32[]{:S(2)}) copy-start(s32[8]{0:T(128)} %owner_ref.3) | copy-start | bytes 100
  0.0 11.7 %copy-start.1 = (f32[8,8,128]{2,1,0:T(8,128)S(1)}, f32[8,8,128]{2,1,0:T(8,128)}, u32[]{:S(2)}) copy-start(f32[8,8,128]{2,1,0:T(8,128)} %coeff_ref.3) | copy-start | bytes 98308
  0.0 11.7 %copy-start = (bf16[8,2,5,8,8,128]{5,4,3,2,1,0:T(8,128)(2,1)S(1)}, bf16[8,2,5,8,8,128]{5,4,3,2,1,0:T(8,128)(2,1)}, u32[]{:S(2)}) copy-start(bf16[8,2,5,8,8,128]{5,4,3,2,1,0:T(8,128)(2,1)} %param.4) | copy-start | bytes 3932164
  12.8 6.9 %collective-permute-start = (f32[72,128]{1,0:T(8,128)S(1)}, f32[72,128]{1,0:T(8,128)S(1)}, u32[]{:S(2)}, u32[]{:S(2)}) collective-permute-start(f32[72,128]{1,0:T(8,128)S(1)} %get-tuple-element.19), channel_id=1, source_target_pairs={{0,1},{1,2},{2,3},{4,5},{5,6},{6,7},{8,9},{9,10},{10,11},{12,13},{... | collective-permute-start | bytes 110600 | tf_op jit(solution)/shard_map/ppermute | solution.py:422
  16.3 5.9 %collective-permute-start.1 = (f32[72,128]{1,0:T(8,128)S(1)}, f32[72,128]{1,0:T(8,128)S(1)}, u32[]{:S(2)}, u32[]{:S(2)}) collective-permute-start(f32[72,128]{1,0:T(8,128)S(1)} %get-tuple-element.22), channel_id=1, source_target_pairs={{1,0},{2,1},{3,2},{5,4},{6,5},{7,6},{9,8},{10,9},{11,10},{13,12},{... | collective-permute-start | bytes 110600 | tf_op jit(solution)/shard_map/ppermute | solution.py:423
where the time goes:
time: 35 us; the launch traced here: 34.7 us
  blocking collectives  21.1 us (60%)
  Pallas kernels  6.2 us (18%)
  starting transfers between devices  4.79 us (14%)
  waiting for transfers between devices  1.15 us (3%)
  local copies, waits for them, and re-layouts  0.78 us (2%)
  other arithmetic  0.64 us (2%)
    all_gather x1, blocking collectives, body(): gathered = lax.all_gather(slab, 'member', axis=0, tiled=False)  10.9 us
    all_to_all x1, blocking collectives, body(): received = lax.all_to_all(sums, 'member', 0, 0, tiled=True)  10.2 us
    pallas_call x5, Pallas kernels, local_call(): pl.pallas_call(kernel, out_shape=shapes[0] if single else shapes, in_spec...  6.2 us
    ppermute x1, starting transfers between devices, body(): from_left = lax.ppermute(to_right, 'tile', up)  3.5 us
    ppermute x1, starting transfers between devices, body(): from_right = lax.ppermute(to_left, 'tile', down)  1.29 us
    ppermute x1, waiting for transfers between devices, body(): from_right = lax.ppermute(to_left, 'tile', down)  1.15 us
    unnamed x8, local copies, waits for them, and re-layouts  0.78 us
  transfers between devices with their start and end apart: 2, of which 1 were waited for; matrix products, arithmetic and copies ran while one was open for 0% of the time, Pallas kernels for 10%

commit v1 on v0

--- a/solution.py
+++ b/solution.py
@@ -65,17 +65,18 @@
     return to_right, to_left
 
 
-def joined_strip(own, edge, index, is_left):
+def joined_strip(own, edge, index, halo):
     part = own.shape[-1] // GROUPS
-    place = lane_index(own.shape) % part
-    edge = lane_roll(edge, -(index % 2) * (part // 2))
-    return jnp.where(place >= part - SWEEPS if is_left else place < SWEEPS, edge, own)
-
-
-def row_mirrored(value, start):
-    part = value.shape[-1] // GROUPS
-    group = group_index(value.shape, start)
-    return jnp.where(group % 2 == 0, lane_roll(value, -part), lane_roll(value, part))
+    return jnp.where(halo, lane_roll(edge, -(index % 2) * (part // 2)), own)
+
+
+def swap_sides(values, swapped):
+    first, second = values
+    return jnp.where(swapped, second, first), jnp.where(swapped, first, second)
+
+
+def first_is_left():
+    return lax.axis_index("tile") % 2 == 1
 
 
 def total(terms):
@@ -88,7 +89,7 @@
     return terms[0]
 
 
-def around(planes, level, row, start=None):
+def around(planes, level, row, even_group=None):
     levels, rows = len(planes), len(planes[level])
     here = planes[level][row]
     terms = [lane_roll(here, 1), lane_roll(here, -1)]
@@ -96,25 +97,26 @@
         terms.append(planes[level][row - 1])
     if row < rows - 1:
         terms.append(planes[level][row + 1])
-    elif start is not None:
-        terms.append(row_mirrored(here, start))
+    elif even_group is not None:
+        part = here.shape[-1] // GROUPS
+        terms.append(jnp.where(even_group, lane_roll(here, -part), lane_roll(here, part)))
     if level > 0:
         terms.append(planes[level - 1][row])
     if level < levels - 1:
         terms.append(planes[level + 1][row])
-    elif start is not None:
+    elif even_group is not None:
         terms.append(lane_roll(here, here.shape[-1] // 2))
     return total(terms)
 
 
-def sweep(source, target, keep_at, square_at, start=None):
+def sweep(source, target, keep_at, square_at):
     levels, rows = source.shape[0], source.shape[1]
     planes = [[source[level, row] for row in range(rows)] for level in range(levels)]
     for level in range(levels):
         for row in range(rows):
             target[level, row] = keep_at(level, row) * planes[level][row] + square_at(
                 level, row
-            ) * around(planes, level, row, start)
+            ) * around(planes, level, row)
 
 
 def anchor_kernel(out_ref):
@@ -128,17 +130,18 @@
     coeff_ref,
     anchor_ref,
     field_ref,
-    left_ref,
-    right_ref,
-    coeff_left_ref,
-    coeff_right_ref,
-    to_right_ref,
-    to_left_ref,
+    first_ref,
+    second_ref,
+    coeff_first_ref,
+    coeff_second_ref,
+    to_first_ref,
+    to_second_ref,
     grad_ref,
 ):
     members, terms, levels, rows, lanes = pert_ref.shape
     slab_rows = gathered_ref.shape[2]
-    strip_levels, strip_rows = left_ref.shape[:2]
+    strip_levels, strip_rows = first_ref.shape[:2]
+    left_first = jnp.broadcast_to(first_is_left(), (8, lanes))
     for slab in range(rows // slab_rows):
         owner = owner_ref[slab]
         for term in range(terms):
@@ -170,15 +173,19 @@
                 [field_ref[pl.ds((l * rows + r) * members, members), :] for l, r in cells]
             )
             coeff = own_strips([spread(coeff_ref[l, pl.ds(r, 1), :]) for l, r in cells])
-            left_ref[level, row], right_ref[level, row] = field
-            coeff_left_ref[pl.ds(index, 1), :] = coeff[0][0:1]
-            coeff_right_ref[pl.ds(index, 1), :] = coeff[1][0:1]
             fields.append(field[0])
             coeffs.append(coeff[0])
+            field = swap_sides(field[::-1], left_first)
+            coeff = swap_sides(coeff[::-1], left_first)
+            first_ref[level, row], second_ref[level, row] = field
+            coeff_first_ref[pl.ds(index, 1), :] = coeff[0][0:1]
+            coeff_second_ref[pl.ds(index, 1), :] = coeff[1][0:1]
     for pair in range(pairs):
         edges = packed_edges(fields[2 * pair], fields[2 * pair + 1])
         coeff_edges = packed_edges(coeffs[2 * pair], coeffs[2 * pair + 1])
-        for ref, edge, coeff_edge in zip((to_right_ref, to_left_ref), edges, coeff_edges):
+        edges = swap_sides(edges, left_first)
+        coeff_edges = swap_sides(coeff_edges, left_first)
+        for ref, edge, coeff_edge in zip((to_first_ref, to_second_ref), edges, coeff_edges):
             ref[pl.ds(pair * members, members), :] = edge
             ref[pl.ds(pairs * members + pair, 1), :] = coeff_edge[0:1]
 
@@ -189,7 +196,8 @@
     levels, rows, members, lanes = field_ref.shape
     terms = pert_ref.shape[1]
     width = lanes // levels
-    slot = lane_index((rows, lanes)) // width
+    shift = jnp.where(first_is_left(), 0, lanes - width)
+    slot = (lane_index((rows, lanes)) + shift) % lanes // width
 
     def pack_ends(member):
         for term in range(terms):
@@ -247,40 +255,45 @@
 def swept_strips(strip_ref, coeff_ref, edge_ref, is_left, keep_ref, square_ref):
     strip_levels, strip_rows, members, lanes = strip_ref.shape
     part = lanes // GROUPS
-    start = SWEEPS if is_left else part - SWEEPS
     pairs = strip_levels * strip_rows // 2
+    lane = lane_index((members, lanes))
+    even_group = (lane + jnp.where(is_left, SWEEPS, part - SWEEPS)) // part % 2 == 0
+    halo = (lane + jnp.where(is_left, SWEEPS, 0)) % part < SWEEPS
     planes, coeffs = [], []
     for level in range(strip_levels):
         plane, coeff_plane = [], []
         for row in range(strip_rows):
             index = level * strip_rows + row
             edge = edge_ref[pl.ds(index // 2 * members, members), :]
-            coeff_edge = spread(edge_ref[pl.ds(pairs * members + index // 2, 1), :])
-            plane.append(joined_strip(strip_ref[level, row], edge, index, is_left))
-            coeff_plane.append(
-                joined_strip(spread(coeff_ref[pl.ds(index, 1), :]), coeff_edge, index, is_left)
-            )
+            coeff_edge = spread(edge_ref[pl.ds(pairs * members + index // 2, 1), :], members)
+            plane.append(joined_strip(strip_ref[level, row], edge, index, halo))
+            coeff_own = spread(coeff_ref[pl.ds(index, 1), :], members)
+            coeff_plane.append(joined_strip(coeff_own, coeff_edge, index, halo))
         planes.append(plane)
         coeffs.append(coeff_plane)
     for level in range(strip_levels):
         for row in range(strip_rows):
             here = coeffs[level][row]
-            keep_ref[level, row] = 1.0 - here * around(coeffs, level, row, start)
+            keep_ref[level, row] = 1.0 - here * around(coeffs, level, row, even_group)
             square_ref[level, row] = here * here
     for _ in range(SWEEPS):
         planes = [
             [
                 keep_ref[level, row] * planes[level][row]
-                + square_ref[level, row] * around(planes, level, row, start)
+                + square_ref[level, row] * around(planes, level, row, even_group)
                 for row in range(strip_rows)
             ]
             for level in range(strip_levels)
         ]
     for level in range(strip_levels):
         for row in range(strip_rows):
-            coeff = spread(coeff_ref[pl.ds(level * strip_rows + row, 1), :])
+            coeff = spread(coeff_ref[pl.ds(level * strip_rows + row, 1), :], members)
             planes[level][row] = planes[level][row] / jnp.where(coeff > 0.0, coeff, 1.0)
     return planes
+
+
+def outer_lanes(shape, is_left):
+    return (lane_index(shape) + jnp.where(is_left, 0, SWEEPS)) % shape[-1] < SWEEPS
 
 
 def level_slots(levels):
@@ -293,13 +306,14 @@
 ):
     members, terms, levels, rows, lanes = pert_ref.shape
     part = lanes // GROUPS
-    planes = swept_strips(strip_ref, coeff_ref, edge_ref, True, keep_ref, square_ref)
-    lane = lane_index((members, lanes))
+    is_left = first_is_left()
+    planes = swept_strips(strip_ref, coeff_ref, edge_ref, is_left, keep_ref, square_ref)
+    outer = outer_lanes((members, lanes), is_left)
     for level, plane in enumerate(planes):
         for row, final in enumerate(plane):
             for g, (l, r) in enumerate(mirrors(level, row, levels, rows)):
                 local_ref[pl.ds((l * rows + r) * members, members), :] = jnp.where(
-                    lane < SWEEPS, lane_roll(final, -part * g), interior_ref[l, r]
+                    outer, lane_roll(final, -part * g), interior_ref[l, r]
                 )
 
     for level in range(levels):
@@ -331,9 +345,11 @@
     members, terms, rows, lanes = ends_ref.shape
     slab_rows, levels = out_ref.shape[2], out_ref.shape[3]
     part, half, width = lanes // GROUPS, lanes // 2, lanes // levels
-    planes = swept_strips(strip_ref, coeff_ref, edge_ref, False, keep_ref, square_ref)
+    is_left = jnp.logical_not(first_is_left())
+    planes = swept_strips(strip_ref, coeff_ref, edge_ref, is_left, keep_ref, square_ref)
     strip_levels, strip_rows = len(planes), len(planes[0])
-    slot = lane_index((members, lanes)) % half // width
+    shift = jnp.where(is_left, half - width, 0)
+    slot = (lane_index((members, lanes)) + shift) % half // width
     for row in range(strip_rows):
         for mirror in range(2):
             ends = None
@@ -343,13 +359,13 @@
             target = rows - 1 - row if mirror else row
             local_ref[pl.ds(target, members, stride=rows), :] = ends
     fields = [local_ref[pl.ds(member * rows, rows), :] for member in range(members)]
-    lane = lane_index((rows, lanes))
+    outer = outer_lanes((rows, lanes), is_left)
     for term in range(terms):
         added = total(ends_ref[member, term] * fields[member] for member in range(members))
         for index, level in enumerate(level_slots(levels)):
             place = pl.ds((term * levels + level) * rows, rows)
             sum_ref[place, :] = jnp.where(
-                lane >= lanes - SWEEPS, lane_roll(added, -width * (index + 1)), partial_ref[place, :]
+                outer, lane_roll(added, -width * (index + 1)), partial_ref[place, :]
             )
     for slab in range(rows // slab_rows):
         owner = owner_ref[slab]
@@ -393,8 +409,7 @@
     strip_levels, strip_rows = levels // 2, rows // 2
     strips = strip_levels * strip_rows
     wide_strip = (strip_levels, strip_rows, members, lanes)
-    coeff_wide_strip = (strip_levels, strip_rows, 8, lanes)
-    strip_scratch = [coeff_wide_strip, coeff_wide_strip]
+    strip_scratch = [wide_strip, wide_strip]
     coeff_strip = (strips, lanes)
     wide_field = (levels, rows, members, lanes)
     flat_field = (levels * rows * members, lanes)
@@ -408,7 +423,7 @@
     anchor = local_call(anchor_kernel, "anchor", [(8, lanes)], [], (), (), ANCHOR_WORK)
     gathered = lax.all_gather(slab, "member", axis=0, tiled=False)
 
-    field, left, right, coeff_left, coeff_right, to_right, to_left = local_call(
+    field, first, second, coeff_first, coeff_second, to_first, to_second = local_call(
         weigh_kernel,
         "weigh",
         [flat_field, wide_strip, wide_strip, coeff_strip, coeff_strip, edge_shape, edge_shape],
@@ -417,10 +432,14 @@
         (smem, vmem, vmem, vmem, vmem),
         2 * terms * members * cells,
     )
-    up = [(i, i + 1) for i in range(n_tile - 1)]
-    down = [(i + 1, i) for i in range(n_tile - 1)]
-    from_left = lax.ppermute(to_right, "tile", up)
-    from_right = lax.ppermute(to_left, "tile", down)
+    from_first, from_second = (
+        lax.ppermute(
+            edges,
+            "tile",
+            [pair for i in range(start, n_tile - 1, 2) for pair in ((i, i + 1), (i + 1, i))],
+        )
+        for start, edges in ((0, to_first), (1, to_second))
+    )
 
     interior, ends = local_call(
         interior_kernel,
@@ -436,7 +455,7 @@
         "partial",
         [grad_shape],
         [flat_field] + strip_scratch,
-        (pert, interior, left, coeff_left, from_left),
+        (pert, interior, first, coeff_first, from_first),
         (vmem,) * 5,
         2 * SWEEPS * members * cells,
     )
@@ -445,7 +464,7 @@
         "finish",
         [(n_member, terms, slab_rows, levels, lanes)],
         [(members * rows, lanes), grad_shape] + strip_scratch,
-        (slab_owner, ends, partial, right, coeff_right, from_right),
+        (slab_owner, ends, partial, second, coeff_second, from_second),
         (smem,) + (vmem,) * 5,
         2 * terms * members * cells,
     )

time: 35 us -> 32.7 us (0.934)
  the two profiles are of different devices: /device:TPU:0 before, /device:TPU:8 now
where the time goes in v1:
time: 32.7 us; the launch traced here: 32.5 us
  blocking collectives  19.6 us (60%)
  Pallas kernels  6.2 us (19%)
  starting transfers between devices  5.13 us (16%)
  local copies, waits for them, and re-layouts  0.76 us (2%)
  other arithmetic  0.64 us (2%)
    all_to_all x1, blocking collectives, body(): received = lax.all_to_all(sums, 'member', 0, 0, tiled=True)  10.2 us
    all_gather x1, blocking collectives, body(): gathered = lax.all_gather(slab, 'member', axis=0, tiled=False)  9.44 us
    pallas_call x5, Pallas kernels, local_call(): pl.pallas_call(kernel, out_shape=shapes[0] if single else shapes, in_spec...  6.2 us
    ppermute x2, starting transfers between devices, body(): lax.ppermute(edges, 'tile', [pair for i in range(start, n_tile - 1, 2) fo...  5.13 us
    unnamed x8, local copies, waits for them, and re-layouts  0.76 us
  transfers between devices with their start and end apart: 2, of which 0 were waited for; matrix products, arithmetic and copies ran while one was open for 0% of the time, Pallas kernels for 10%

profile of v1, /device:TPU:8, one launch (start us, length us, event | category | flops | bytes accessed | tf_op | source)
XLA Modules:
  0.0 32.5 jit_solution(2981394484197836578)
XLA Ops:
  0.0 0.0 copy-start.3
  0.0 0.0 copy-start.2
  0.0 0.0 copy-start.1
  0.0 0.0 copy-start
  0.0 0.7 %copy-done.3 = f32[2,5,8,1,128]{4,3,2,1,0:T(1,128)S(1)} copy-done((f32[2,5,8,1,128]{4,3,2,1,0:T(1,128)S(1)}, f32[2,5,8,1,128]{4,3,2,1,0:T(1,128)}, u32[]{:S(2)}) %copy-start.3) | copy-done | bytes 40984
  0.8 9.4 %all_gather.3.gathered_ref = f32[8,10,1,8,128]{4,3,2,1,0:T(8,128)S(1)} all-gather(f32[1,10,1,8,128]{4,3,2,1,0:T(8,128)S(1)} %bitcast.8), channel_id=1, replica_groups=mesh['member'=8,'tile'=4] {'member'}, dimensions={0}, use_global_device_ids=true | all-gather | bytes 368640 | tf_op jit(solution)/shard_map/all_gather | solution.py:424
  10.2 0.0 copy-done.2
  10.2 0.0 copy-done.1
  10.2 0.0 copy-done
  10.2 1.1 %weigh.1 = (f32[512,128]{1,0:T(8,128)S(1)}, f32[4,4,8,128]{3,2,1,0:T(8,128)S(1)}, f32[4,4,8,128]{3,2,1,0:T(8,128)S(1)}, f32[16,128]{1,0:T(8,128)S(1)}, f32[16,12...) custom-call(s32[8]{0:T(128)S(1)} %copy-done.2, f32[8,10,1,8,128]{4,3,2,1,0:T(8,128)S(1)} %all_gather.3.gathered_ref, ...), custom_call_target="tpu_custom_call" | custom-call | flops 1310720 | bytes 2158624 | tf_op jit(solution)/shard_map/weigh/pallas_call | solution.py:388
  11.3 0.5 %collective-permute-start = (f32[72,128]{1,0:T(8,128)S(1)}, f32[72,128]{1,0:T(8,128)S(1)}, u32[]{:S(2)}, u32[]{:S(2)}) collective-permute-start(f32[72,128]{1,0:T(8,128)S(1)} %get-tuple-element.19), channel_id=1, source_target_pairs={{0,1},{1,0},{2,3},{3,2},{4,5},{5,4},{6,7},{7,6},{8,9},{9,8},{10,11... | collective-permute-start | bytes 110600 | tf_op jit(solution)/shard_map/ppermute | solution.py:436
  11.8 4.6 %collective-permute-start.1 = (f32[72,128]{1,0:T(8,128)S(1)}, f32[72,128]{1,0:T(8,128)S(1)}, u32[]{:S(2)}, u32[]{:S(2)}) collective-permute-start(f32[72,128]{1,0:T(8,128)S(1)} %get-tuple-element.22), channel_id=1, source_target_pairs={{1,2},{2,1},{5,6},{6,5},{9,10},{10,9},{13,14},{14,13},{17,18},{18,... | collective-permute-start | bytes 110600 | tf_op jit(solution)/shard_map/ppermute | solution.py:436
  16.4 2.1 %interior.1 = (f32[8,8,8,128]{3,2,1,0:T(8,128)S(1)}, f32[8,10,8,128]{3,2,1,0:T(8,128)S(1)}) custom-call(f32[8,8,8,128]{3,2,1,0:T(8,128)S(1)} %bitcast.7, f32[8,8,128]{2,1,0:T(8,128)S(1)} %copy-done.1, bf16[8,10,8,8,128]{4,3,2,1,0:T(8,128)(2,1)S(1)} %bitcast.5), custom_call_target="tpu_custom_call" | custom-call | flops 5242880 | bytes 2195456 | tf_op jit(solution)/shard_map/interior/pallas_call | solution.py:388
  18.5 0.0 collective-permute-done.edge_ref
  18.5 1.3 %partial.1.partial_ref = f32[640,128]{1,0:T(8,128)S(1)} custom-call(bf16[8,10,8,8,128]{4,3,2,1,0:T(8,128)(2,1)S(1)} %bitcast.6, f32[8,8,8,128]{3,2,1,0:T(8,128)S(1)} %get-tuple-element.16.interior_ref, f32[4,4,8,128]{3,2,1,0:T(8,128)S(1)} %get-tuple-element.17.strip_ref, f32[16,128]{1,0:T(8,128)S(1)} %get-tuple-element.18.coeff_ref, ...), custom_call_target="tpu_custom_call" | custom-call | flops 1310720 | bytes 2011136 | tf_op jit(solution)/shard_map/partial/pallas_call | solution.py:388
  19.8 0.0 collective-permute-done.1.edge_ref
  19.8 1.8 %finish.1 = f32[8,10,1,8,128]{4,3,2,1,0:T(8,128)S(1)} custom-call(s32[8]{0:T(128)S(1)} %copy-done.2, f32[8,10,8,128]{3,2,1,0:T(8,128)S(1)} %get-tuple-element.15.ends_ref, f32[640,128]{1,0:T(8,128)S(1)} %partial.1.partial_ref, f32[4,4,8,128]{3,2,1,0:T(8,128)S(1)} %get-tuple-element.20.strip_ref, f32[16,128]{1,0:T(8,128)S(1)} %get-tuple-element.21.coeff_ref, ...), custom_call_target="tpu_custom_call" | custom-call | flops 1310720 | bytes 1093664 | tf_op jit(solution)/shard_map/finish/pallas_call | solution.py:388
  21.6 10.2 %all_to_all.5 = f32[8,10,1,8,128]{4,3,2,1,0:T(8,128)S(1)} all-to-all(f32[8,10,1,8,128]{4,3,2,1,0:T(8,128)S(1)} %finish.1), channel_id=1, replica_groups=mesh['member'=8,'tile'=4] {'member'}, dimensions={0} | all-to-all | bytes 655360 | tf_op jit(solution)/shard_map/all_to_all | solution.py:471
  31.8 0.6 %broadcast_multiply_fusion = f32[10,8,128]{2,1,0:T(8,128)} fusion(f32[10,8,128]{2,1,0:T(8,128)S(1)} %reduce_sum.9), kind=kLoop, calls=%fused_computation | loop fusion | flops 10240 | bytes 81920 | tf_op jit(solution)/shard_map/mul | solution.py:473
  (2 shorter events, 0.0 us)
Async XLA Ops:
  0.0 0.8 %copy-start.3 = (f32[2,5,8,1,128]{4,3,2,1,0:T(1,128)S(1)}, f32[2,5,8,1,128]{4,3,2,1,0:T(1,128)}, u32[]{:S(2)}) copy-start(f32[2,5,8,1,128]{4,3,2,1,0:T(1,128)} %param.5) | copy-start | bytes 122884
  0.0 10.2 %copy-start.2 = (s32[8]{0:T(128)S(1)}, s32[8]{0:T(128)}, u32[]{:S(2)}) copy-start(s32[8]{0:T(128)} %owner_ref.3) | copy-start | bytes 100
  0.0 10.2 %copy-start.1 = (f32[8,8,128]{2,1,0:T(8,128)S(1)}, f32[8,8,128]{2,1,0:T(8,128)}, u32[]{:S(2)}) copy-start(f32[8,8,128]{2,1,0:T(8,128)} %coeff_ref.3) | copy-start | bytes 98308
  0.0 10.2 %copy-start = (bf16[8,2,5,8,8,128]{5,4,3,2,1,0:T(8,128)(2,1)S(1)}, bf16[8,2,5,8,8,128]{5,4,3,2,1,0:T(8,128)(2,1)}, u32[]{:S(2)}) copy-start(bf16[8,2,5,8,8,128]{5,4,3,2,1,0:T(8,128)(2,1)} %param.4) | copy-start | bytes 3932164
  11.3 7.2 %collective-permute-start = (f32[72,128]{1,0:T(8,128)S(1)}, f32[72,128]{1,0:T(8,128)S(1)}, u32[]{:S(2)}, u32[]{:S(2)}) collective-permute-start(f32[72,128]{1,0:T(8,128)S(1)} %get-tuple-element.19), channel_id=1, source_target_pairs={{0,1},{1,0},{2,3},{3,2},{4,5},{5,4},{6,7},{7,6},{8,9},{9,8},{10,11... | collective-permute-start | bytes 110600 | tf_op jit(solution)/shard_map/ppermute | solution.py:436
  11.8 8.0 %collective-permute-start.1 = (f32[72,128]{1,0:T(8,128)S(1)}, f32[72,128]{1,0:T(8,128)S(1)}, u32[]{:S(2)}, u32[]{:S(2)}) collective-permute-start(f32[72,128]{1,0:T(8,128)S(1)} %get-tuple-element.22), channel_id=1, source_target_pairs={{1,2},{2,1},{5,6},{6,5},{9,10},{10,9},{13,14},{14,13},{17,18},{18,... | collective-permute-start | bytes 110600 | tf_op jit(solution)/shard_map/ppermute | solution.py:436

commit v2 on v1

--- a/solution.py
+++ b/solution.py
@@ -77,6 +77,23 @@
 
 def first_is_left():
     return lax.axis_index("tile") % 2 == 1
+
+
+def swap_pairs(start, n_member, n_tile):
+    pairs = []
+    for member in range(n_member):
+        for tile in range(n_tile):
+            other = tile + 1 if (tile - start) % 2 == 0 else tile - 1
+            if 0 <= other < n_tile:
+                pairs.append((member * n_tile + tile, member * n_tile + other))
+            elif n_member % 2 == 0:
+                pairs.append((member * n_tile + tile, (member ^ 1) * n_tile + tile))
+    return pairs
+
+
+def without_partner(is_left, n_tile):
+    tile = lax.axis_index("tile")
+    return jnp.where(is_left, tile == 0, tile == n_tile - 1)
 
 
 def total(terms):
@@ -253,6 +270,7 @@
 
 
 def swept_strips(strip_ref, coeff_ref, edge_ref, is_left, keep_ref, square_ref):
+    outside = without_partner(is_left, lax.axis_size("tile"))
     strip_levels, strip_rows, members, lanes = strip_ref.shape
     part = lanes // GROUPS
     pairs = strip_levels * strip_rows // 2
@@ -265,7 +283,9 @@
         for row in range(strip_rows):
             index = level * strip_rows + row
             edge = edge_ref[pl.ds(index // 2 * members, members), :]
-            coeff_edge = spread(edge_ref[pl.ds(pairs * members + index // 2, 1), :], members)
+            edge = jnp.where(outside, 0.0, edge)
+            coeff_edge = edge_ref[pl.ds(pairs * members + index // 2, 1), :]
+            coeff_edge = spread(jnp.where(outside, 0.0, coeff_edge), members)
             plane.append(joined_strip(strip_ref[level, row], edge, index, halo))
             coeff_own = spread(coeff_ref[pl.ds(index, 1), :], members)
             coeff_plane.append(joined_strip(coeff_own, coeff_edge, index, halo))
@@ -433,11 +453,7 @@
         2 * terms * members * cells,
     )
     from_first, from_second = (
-        lax.ppermute(
-            edges,
-            "tile",
-            [pair for i in range(start, n_tile - 1, 2) for pair in ((i, i + 1), (i + 1, i))],
-        )
+        lax.ppermute(edges, ("member", "tile"), swap_pairs(start, n_member, n_tile))
         for start, edges in ((0, to_first), (1, to_second))
     )
 

time: 32.7 us -> 30.9 us (0.945)
  the two profiles are of different devices: /device:TPU:8 before, /device:TPU:0 now
where the time goes in v2:
time: 30.9 us; the launch traced here: 30.7 us
  blocking collectives  21.1 us (68%)
  Pallas kernels  6.17 us (20%)
  starting transfers between devices  1.72 us (6%)
  local copies, waits for them, and re-layouts  0.78 us (3%)
  other arithmetic  0.64 us (2%)
    all_gather x1, blocking collectives, body(): gathered = lax.all_gather(slab, 'member', axis=0, tiled=False)  10.9 us
    all_to_all x1, blocking collectives, body(): received = lax.all_to_all(sums, 'member', 0, 0, tiled=True)  10.2 us
    pallas_call x5, Pallas kernels, local_call(): pl.pallas_call(kernel, out_shape=shapes[0] if single else shapes, in_spec...  6.17 us
    ppermute x2, starting transfers between devices, body(): lax.ppermute(edges, ('member', 'tile'), swap_pairs(start, n_member, n_tile))  1.72 us
    unnamed x8, local copies, waits for them, and re-layouts  0.78 us
    mul x1, other arithmetic, body(): owned = jnp.sum(received, axis=0) * norm_factor  0.62 us
  transfers between devices with their start and end apart: 2, of which 1 were waited for; matrix products, arithmetic and copies ran while one was open for 0% of the time, Pallas kernels for 11%

profile of v2, /device:TPU:0, one launch (start us, length us, event | category | flops | bytes accessed | tf_op | source)
XLA Modules:
  0.0 30.7 jit_solution(12261822769868550967)
XLA Ops:
  0.0 0.0 copy-start.3
  0.0 0.0 copy-start.2
  0.0 0.0 copy-start.1
  0.0 0.0 copy-start
  0.0 0.8 %copy-done.3 = f32[2,5,8,1,128]{4,3,2,1,0:T(1,128)S(1)} copy-done((f32[2,5,8,1,128]{4,3,2,1,0:T(1,128)S(1)}, f32[2,5,8,1,128]{4,3,2,1,0:T(1,128)}, u32[]{:S(2)}) %copy-start.3) | copy-done | bytes 40984
  0.8 10.9 %all_gather.3.gathered_ref = f32[8,10,1,8,128]{4,3,2,1,0:T(8,128)S(1)} all-gather(f32[1,10,1,8,128]{4,3,2,1,0:T(8,128)S(1)} %bitcast.8), channel_id=1, replica_groups=mesh['member'=8,'tile'=4] {'member'}, dimensions={0}, use_global_device_ids=true | all-gather | bytes 368640 | tf_op jit(solution)/shard_map/all_gather | solution.py:444
  11.7 0.0 copy-done.2
  11.7 0.0 copy-done.1
  11.7 0.0 copy-done
  11.7 1.1 %weigh.1 = (f32[512,128]{1,0:T(8,128)S(1)}, f32[4,4,8,128]{3,2,1,0:T(8,128)S(1)}, f32[4,4,8,128]{3,2,1,0:T(8,128)S(1)}, f32[16,128]{1,0:T(8,128)S(1)}, f32[16,12...) custom-call(s32[8]{0:T(128)S(1)} %copy-done.2, f32[8,10,1,8,128]{4,3,2,1,0:T(8,128)S(1)} %all_gather.3.gathered_ref, ...), custom_call_target="tpu_custom_call" | custom-call | flops 1310720 | bytes 2158624 | tf_op jit(solution)/shard_map/weigh/pallas_call | solution.py:408
  12.8 1.7 %collective-permute-start = (f32[72,128]{1,0:T(8,128)S(1)}, f32[72,128]{1,0:T(8,128)S(1)}, u32[]{:S(2)}, u32[]{:S(2)}) collective-permute-start(f32[72,128]{1,0:T(8,128)S(1)} %get-tuple-element.19), channel_id=1, source_target_pairs={{0,1},{1,0},{2,3},{3,2},{4,5},{5,4},{6,7},{7,6},{8,9},{9,8},{10,11... | collective-permute-start | bytes 110600 | tf_op jit(solution)/shard_map/ppermute | solution.py:456
  14.4 0.1 collective-permute-start.1
  14.5 2.0 %interior.1 = (f32[8,8,8,128]{3,2,1,0:T(8,128)S(1)}, f32[8,10,8,128]{3,2,1,0:T(8,128)S(1)}) custom-call(f32[8,8,8,128]{3,2,1,0:T(8,128)S(1)} %bitcast.7, f32[8,8,128]{2,1,0:T(8,128)S(1)} %copy-done.1, bf16[8,10,8,8,128]{4,3,2,1,0:T(8,128)(2,1)S(1)} %bitcast.5), custom_call_target="tpu_custom_call" | custom-call | flops 5242880 | bytes 2195456 | tf_op jit(solution)/shard_map/interior/pallas_call | solution.py:408
  16.5 0.3 collective-permute-done.edge_ref
  16.8 1.3 %partial.1.partial_ref = f32[640,128]{1,0:T(8,128)S(1)} custom-call(bf16[8,10,8,8,128]{4,3,2,1,0:T(8,128)(2,1)S(1)} %bitcast.6, f32[8,8,8,128]{3,2,1,0:T(8,128)S(1)} %get-tuple-element.16.interior_ref, f32[4,4,8,128]{3,2,1,0:T(8,128)S(1)} %get-tuple-element.17.strip_ref, f32[16,128]{1,0:T(8,128)S(1)} %get-tuple-element.18.coeff_ref, ...), custom_call_target="tpu_custom_call" | custom-call | flops 1310720 | bytes 2011136 | tf_op jit(solution)/shard_map/partial/pallas_call | solution.py:408
  18.1 0.0 collective-permute-done.1.edge_ref
  18.1 1.7 %finish.1 = f32[8,10,1,8,128]{4,3,2,1,0:T(8,128)S(1)} custom-call(s32[8]{0:T(128)S(1)} %copy-done.2, f32[8,10,8,128]{3,2,1,0:T(8,128)S(1)} %get-tuple-element.15.ends_ref, f32[640,128]{1,0:T(8,128)S(1)} %partial.1.partial_ref, f32[4,4,8,128]{3,2,1,0:T(8,128)S(1)} %get-tuple-element.20.strip_ref, f32[16,128]{1,0:T(8,128)S(1)} %get-tuple-element.21.coeff_ref, ...), custom_call_target="tpu_custom_call" | custom-call | flops 1310720 | bytes 1093664 | tf_op jit(solution)/shard_map/finish/pallas_call | solution.py:408
  19.9 10.2 %all_to_all.5 = f32[8,10,1,8,128]{4,3,2,1,0:T(8,128)S(1)} all-to-all(f32[8,10,1,8,128]{4,3,2,1,0:T(8,128)S(1)} %finish.1), channel_id=1, replica_groups=mesh['member'=8,'tile'=4] {'member'}, dimensions={0} | all-to-all | bytes 655360 | tf_op jit(solution)/shard_map/all_to_all | solution.py:487
  30.1 0.6 %broadcast_multiply_fusion = f32[10,8,128]{2,1,0:T(8,128)} fusion(f32[10,8,128]{2,1,0:T(8,128)S(1)} %reduce_sum.9), kind=kLoop, calls=%fused_computation | loop fusion | flops 10240 | bytes 81920 | tf_op jit(solution)/shard_map/mul | solution.py:489
  (2 shorter events, 0.0 us)
Async XLA Ops:
  0.0 0.8 %copy-start.3 = (f32[2,5,8,1,128]{4,3,2,1,0:T(1,128)S(1)}, f32[2,5,8,1,128]{4,3,2,1,0:T(1,128)}, u32[]{:S(2)}) copy-start(f32[2,5,8,1,128]{4,3,2,1,0:T(1,128)} %param.5) | copy-start | bytes 122884
  0.0 11.7 %copy-start.2 = (s32[8]{0:T(128)S(1)}, s32[8]{0:T(128)}, u32[]{:S(2)}) copy-start(s32[8]{0:T(128)} %owner_ref.3) | copy-start | bytes 100
  0.0 11.7 %copy-start.1 = (f32[8,8,128]{2,1,0:T(8,128)S(1)}, f32[8,8,128]{2,1,0:T(8,128)}, u32[]{:S(2)}) copy-start(f32[8,8,128]{2,1,0:T(8,128)} %coeff_ref.3) | copy-start | bytes 98308
  0.0 11.7 %copy-start = (bf16[8,2,5,8,8,128]{5,4,3,2,1,0:T(8,128)(2,1)S(1)}, bf16[8,2,5,8,8,128]{5,4,3,2,1,0:T(8,128)(2,1)}, u32[]{:S(2)}) copy-start(bf16[8,2,5,8,8,128]{5,4,3,2,1,0:T(8,128)(2,1)} %param.4) | copy-start | bytes 3932164
  12.8 4.0 %collective-permute-start = (f32[72,128]{1,0:T(8,128)S(1)}, f32[72,128]{1,0:T(8,128)S(1)}, u32[]{:S(2)}, u32[]{:S(2)}) collective-permute-start(f32[72,128]{1,0:T(8,128)S(1)} %get-tuple-element.19), channel_id=1, source_target_pairs={{0,1},{1,0},{2,3},{3,2},{4,5},{5,4},{6,7},{7,6},{8,9},{9,8},{10,11... | collective-permute-start | bytes 110600 | tf_op jit(solution)/shard_map/ppermute | solution.py:456
  14.4 3.7 %collective-permute-start.1 = (f32[72,128]{1,0:T(8,128)S(1)}, f32[72,128]{1,0:T(8,128)S(1)}, u32[]{:S(2)}, u32[]{:S(2)}) collective-permute-start(f32[72,128]{1,0:T(8,128)S(1)} %get-tuple-element.22), channel_id=1, source_target_pairs={{0,4},{1,2},{2,1},{3,7},{4,0},{5,6},{6,5},{7,3},{8,12},{9,10},{10,... | collective-permute-start | bytes 110600 | tf_op jit(solution)/shard_map/ppermute | solution.py:456

commit v3 on v2

--- a/solution.py
+++ b/solution.py
@@ -147,17 +147,17 @@
     coeff_ref,
     anchor_ref,
     field_ref,
-    first_ref,
-    second_ref,
-    coeff_first_ref,
-    coeff_second_ref,
+    left_ref,
+    right_ref,
+    coeff_left_ref,
+    coeff_right_ref,
     to_first_ref,
     to_second_ref,
     grad_ref,
 ):
     members, terms, levels, rows, lanes = pert_ref.shape
     slab_rows = gathered_ref.shape[2]
-    strip_levels, strip_rows = first_ref.shape[:2]
+    strip_levels, strip_rows = left_ref.shape[:2]
     left_first = jnp.broadcast_to(first_is_left(), (8, lanes))
     for slab in range(rows // slab_rows):
         owner = owner_ref[slab]
@@ -192,11 +192,9 @@
             coeff = own_strips([spread(coeff_ref[l, pl.ds(r, 1), :]) for l, r in cells])
             fields.append(field[0])
             coeffs.append(coeff[0])
-            field = swap_sides(field[::-1], left_first)
-            coeff = swap_sides(coeff[::-1], left_first)
-            first_ref[level, row], second_ref[level, row] = field
-            coeff_first_ref[pl.ds(index, 1), :] = coeff[0][0:1]
-            coeff_second_ref[pl.ds(index, 1), :] = coeff[1][0:1]
+            left_ref[level, row], right_ref[level, row] = field
+            coeff_left_ref[pl.ds(index, 1), :] = coeff[0][0:1]
+            coeff_right_ref[pl.ds(index, 1), :] = coeff[1][0:1]
     for pair in range(pairs):
         edges = packed_edges(fields[2 * pair], fields[2 * pair + 1])
         coeff_edges = packed_edges(coeffs[2 * pair], coeffs[2 * pair + 1])
@@ -208,23 +206,9 @@
 
 
 def interior_kernel(
-    field_ref, coeff_ref, pert_ref, out_ref, ends_ref, other_ref, keep_ref, square_ref, inverse_ref
+    field_ref, coeff_ref, out_ref, other_ref, keep_ref, square_ref, inverse_ref
 ):
     levels, rows, members, lanes = field_ref.shape
-    terms = pert_ref.shape[1]
-    width = lanes // levels
-    shift = jnp.where(first_is_left(), 0, lanes - width)
-    slot = (lane_index((rows, lanes)) + shift) % lanes // width
-
-    def pack_ends(member):
-        for term in range(terms):
-            ends = None
-            for index, level in enumerate(level_slots(levels)):
-                value = pert_ref[member, term, level].astype(jnp.float32)
-                moved = lane_roll(value, width * (index + 1))
-                ends = moved if ends is None else jnp.where(slot == index, moved, ends)
-            ends_ref[member, term] = ends
-
     row_index = lax.broadcasted_iota(jnp.int32, (rows, lanes), 0)
     for level in range(levels):
         here = coeff_ref[level]
@@ -251,89 +235,117 @@
     sweep(field_ref, other_ref, keep_at, square_at)
     sweep(other_ref, out_ref, keep_at, square_at)
 
-    pairs = SWEEPS // 2 - 1
-    share = members // pairs
-
     def pair(index, carry):
         sweep(out_ref, other_ref, keep_at, square_at)
         sweep(other_ref, out_ref, keep_at, square_at)
-        for extra in range(share):
-            pack_ends(index * share + extra)
         return carry
 
-    lax.fori_loop(0, pairs, pair, 0)
-    for member in range(pairs * share, members):
-        pack_ends(member)
+    lax.fori_loop(0, SWEEPS // 2 - 1, pair, 0)
     for level in range(levels):
         for row in range(rows):
             out_ref[level, row] = out_ref[level, row] * inverse_ref[level, pl.ds(row, 1), :]
 
 
-def swept_strips(strip_ref, coeff_ref, edge_ref, is_left, keep_ref, square_ref):
-    outside = without_partner(is_left, lax.axis_size("tile"))
-    strip_levels, strip_rows, members, lanes = strip_ref.shape
-    part = lanes // GROUPS
-    pairs = strip_levels * strip_rows // 2
-    lane = lane_index((members, lanes))
-    even_group = (lane + jnp.where(is_left, SWEEPS, part - SWEEPS)) // part % 2 == 0
-    halo = (lane + jnp.where(is_left, SWEEPS, 0)) % part < SWEEPS
-    planes, coeffs = [], []
-    for level in range(strip_levels):
-        plane, coeff_plane = [], []
-        for row in range(strip_rows):
-            index = level * strip_rows + row
-            edge = edge_ref[pl.ds(index // 2 * members, members), :]
-            edge = jnp.where(outside, 0.0, edge)
-            coeff_edge = edge_ref[pl.ds(pairs * members + index // 2, 1), :]
-            coeff_edge = spread(jnp.where(outside, 0.0, coeff_edge), members)
-            plane.append(joined_strip(strip_ref[level, row], edge, index, halo))
-            coeff_own = spread(coeff_ref[pl.ds(index, 1), :], members)
-            coeff_plane.append(joined_strip(coeff_own, coeff_edge, index, halo))
-        planes.append(plane)
-        coeffs.append(coeff_plane)
-    for level in range(strip_levels):
-        for row in range(strip_rows):
-            here = coeffs[level][row]
-            keep_ref[level, row] = 1.0 - here * around(coeffs, level, row, even_group)
-            square_ref[level, row] = here * here
-    for _ in range(SWEEPS):
-        planes = [
+class Strips:
+    def __init__(self, strip_ref, coeff_ref, edge_at, is_left, keep_ref, square_ref):
+        self.levels, self.rows, self.members, lanes = strip_ref.shape
+        self.coeff_ref, self.keep_ref, self.square_ref = coeff_ref, keep_ref, square_ref
+        part = lanes // GROUPS
+        pairs = self.levels * self.rows // 2
+        shape = (self.members, lanes)
+        self.even_group = group_index(shape, SWEEPS if is_left else part - SWEEPS) % 2 == 0
+        place = lane_index(shape) % part
+        halo = place >= part - SWEEPS if is_left else place < SWEEPS
+        self.planes, coeffs = [], []
+        for level in range(self.levels):
+            plane, coeff_plane = [], []
+            for row in range(self.rows):
+                index = level * self.rows + row
+                edge = edge_at(index // 2 * self.members, self.members)
+                coeff_edge = spread(edge_at(pairs * self.members + index // 2, 1), self.members)
+                plane.append(joined_strip(strip_ref[level, row], edge, index, halo))
+                coeff_plane.append(joined_strip(self.own_coeff(level, row), coeff_edge, index, halo))
+            self.planes.append(plane)
+            coeffs.append(coeff_plane)
+        for level in range(self.levels):
+            for row in range(self.rows):
+                here = coeffs[level][row]
+                keep_ref[level, row] = 1.0 - here * around(coeffs, level, row, self.even_group)
+                square_ref[level, row] = here * here
+
+    def own_coeff(self, level, row):
+        return spread(self.coeff_ref[pl.ds(level * self.rows + row, 1), :], self.members)
+
+    def step(self):
+        self.planes = [
             [
-                keep_ref[level, row] * planes[level][row]
-                + square_ref[level, row] * around(planes, level, row, even_group)
-                for row in range(strip_rows)
+                self.keep_ref[level, row] * self.planes[level][row]
+                + self.square_ref[level, row] * around(self.planes, level, row, self.even_group)
+                for row in range(self.rows)
             ]
-            for level in range(strip_levels)
+            for level in range(self.levels)
         ]
-    for level in range(strip_levels):
-        for row in range(strip_rows):
-            coeff = spread(coeff_ref[pl.ds(level * strip_rows + row, 1), :], members)
-            planes[level][row] = planes[level][row] / jnp.where(coeff > 0.0, coeff, 1.0)
-    return planes
-
-
-def outer_lanes(shape, is_left):
-    return (lane_index(shape) + jnp.where(is_left, 0, SWEEPS)) % shape[-1] < SWEEPS
-
-
-def level_slots(levels):
-    near = list(range(levels // 2))
-    return near + [levels - 1 - level for level in near]
-
-
-def partial_kernel(
-    pert_ref, interior_ref, strip_ref, coeff_ref, edge_ref, out_ref, local_ref, keep_ref, square_ref
+
+    def final(self, level, row):
+        coeff = self.own_coeff(level, row)
+        return self.planes[level][row] / jnp.where(coeff > 0.0, coeff, 1.0)
+
+
+def finish_kernel(
+    owner_ref,
+    pert_ref,
+    interior_ref,
+    left_ref,
+    right_ref,
+    coeff_left_ref,
+    coeff_right_ref,
+    from_first_ref,
+    from_second_ref,
+    out_ref,
+    local_ref,
+    sum_ref,
+    keep_left_ref,
+    square_left_ref,
+    keep_right_ref,
+    square_right_ref,
 ):
     members, terms, levels, rows, lanes = pert_ref.shape
+    slab_rows = out_ref.shape[2]
     part = lanes // GROUPS
-    is_left = first_is_left()
-    planes = swept_strips(strip_ref, coeff_ref, edge_ref, is_left, keep_ref, square_ref)
-    outer = outer_lanes((members, lanes), is_left)
-    for level, plane in enumerate(planes):
-        for row, final in enumerate(plane):
+    left_first = first_is_left()
+
+    def edge_reader(is_left):
+        outside = without_partner(is_left, lax.axis_size("tile"))
+
+        def edge_at(place, count):
+            first = from_first_ref[pl.ds(place, count), :]
+            second = from_second_ref[pl.ds(place, count), :]
+            edge = jnp.where(left_first == is_left, first, second)
+            return jnp.where(outside, 0.0, edge)
+
+        return edge_at
+
+    left = Strips(
+        left_ref, coeff_left_ref, edge_reader(True), True, keep_left_ref, square_left_ref
+    )
+    right = Strips(
+        right_ref, coeff_right_ref, edge_reader(False), False, keep_right_ref, square_right_ref
+    )
+    for _ in range(SWEEPS):
+        left.step()
+        right.step()
+    lane = lane_index((members, lanes))
+    for level in range(left.levels):
+        for row in range(left.rows):
+            left_end, right_end = left.final(level, row), right.final(level, row)
             for g, (l, r) in enumerate(mirrors(level, row, levels, rows)):
+                ends = jnp.where(
+                    lane < lanes // 2,
+                    lane_roll(left_end, -part * g),
+                    lane_roll(right_end, -part * g),
+                )
                 local_ref[pl.ds((l * rows + r) * members, members), :] = jnp.where(
-                    outer, lane_roll(final, -part * g), interior_ref[l, r]
+                    (lane < SWEEPS) | (lane >= lanes - SWEEPS), ends, interior_ref[l, r]
                 )
 
     for level in range(levels):
@@ -343,49 +355,9 @@
             for member in range(members)
         ]
         for term in range(terms):
-            out_ref[pl.ds(term * levels * rows + base, rows), :] = total(
+            sum_ref[pl.ds(term * levels * rows + base, rows), :] = total(
                 pert_ref[member, term, level].astype(jnp.float32) * fields[member]
                 for member in range(members)
-            )
-
-
-def finish_kernel(
-    owner_ref,
-    ends_ref,
-    partial_ref,
-    strip_ref,
-    coeff_ref,
-    edge_ref,
-    out_ref,
-    local_ref,
-    sum_ref,
-    keep_ref,
-    square_ref,
-):
-    members, terms, rows, lanes = ends_ref.shape
-    slab_rows, levels = out_ref.shape[2], out_ref.shape[3]
-    part, half, width = lanes // GROUPS, lanes // 2, lanes // levels
-    is_left = jnp.logical_not(first_is_left())
-    planes = swept_strips(strip_ref, coeff_ref, edge_ref, is_left, keep_ref, square_ref)
-    strip_levels, strip_rows = len(planes), len(planes[0])
-    shift = jnp.where(is_left, half - width, 0)
-    slot = (lane_index((members, lanes)) + shift) % half // width
-    for row in range(strip_rows):
-        for mirror in range(2):
-            ends = None
-            for level in range(strip_levels):
-                moved = lane_roll(planes[level][row], width * (level + 1) - part * mirror)
-                ends = moved if ends is None else jnp.where(slot == level, moved, ends)
-            target = rows - 1 - row if mirror else row
-            local_ref[pl.ds(target, members, stride=rows), :] = ends
-    fields = [local_ref[pl.ds(member * rows, rows), :] for member in range(members)]
-    outer = outer_lanes((rows, lanes), is_left)
-    for term in range(terms):
-        added = total(ends_ref[member, term] * fields[member] for member in range(members))
-        for index, level in enumerate(level_slots(levels)):
-            place = pl.ds((term * levels + level) * rows, rows)
-            sum_ref[place, :] = jnp.where(
-                outer, lane_roll(added, -width * (index + 1)), partial_ref[place, :]
             )
     for slab in range(rows // slab_rows):
         owner = owner_ref[slab]
@@ -429,7 +401,6 @@
     strip_levels, strip_rows = levels // 2, rows // 2
     strips = strip_levels * strip_rows
     wide_strip = (strip_levels, strip_rows, members, lanes)
-    strip_scratch = [wide_strip, wide_strip]
     coeff_strip = (strips, lanes)
     wide_field = (levels, rows, members, lanes)
     flat_field = (levels * rows * members, lanes)
@@ -443,7 +414,7 @@
     anchor = local_call(anchor_kernel, "anchor", [(8, lanes)], [], (), (), ANCHOR_WORK)
     gathered = lax.all_gather(slab, "member", axis=0, tiled=False)
 
-    field, first, second, coeff_first, coeff_second, to_first, to_second = local_call(
+    field, left, right, coeff_left, coeff_right, to_first, to_second = local_call(
         weigh_kernel,
         "weigh",
         [flat_field, wide_strip, wide_strip, coeff_strip, coeff_strip, edge_shape, edge_shape],
@@ -457,31 +428,32 @@
         for start, edges in ((0, to_first), (1, to_second))
     )
 
-    interior, ends = local_call(
+    interior = local_call(
         interior_kernel,
         "interior",
-        [wide_field, (members, terms, rows, lanes)],
+        [wide_field],
         [wide_field, field_coeff, field_coeff, field_coeff],
-        (field.reshape(wide_field), diffusivity, pert),
-        (vmem,) * 3,
+        (field.reshape(wide_field), diffusivity),
+        (vmem,) * 2,
         8 * SWEEPS * members * cells,
-    )
-    partial = local_call(
-        partial_kernel,
-        "partial",
-        [grad_shape],
-        [flat_field] + strip_scratch,
-        (pert, interior, first, coeff_first, from_first),
-        (vmem,) * 5,
-        2 * SWEEPS * members * cells,
     )
     sums = local_call(
         finish_kernel,
         "finish",
         [(n_member, terms, slab_rows, levels, lanes)],
-        [(members * rows, lanes), grad_shape] + strip_scratch,
-        (slab_owner, ends, partial, second, coeff_second, from_second),
-        (smem,) + (vmem,) * 5,
+        [flat_field, grad_shape] + [wide_strip] * 4,
+        (
+            slab_owner,
+            pert,
+            interior,
+            left,
+            right,
+            coeff_left,
+            coeff_right,
+            from_first,
+            from_second,
+        ),
+        (smem,) + (vmem,) * 8,
         2 * terms * members * cells,
     )
     received = lax.all_to_all(sums, "member", 0, 0, tiled=True)

time: 30.9 us -> 30.3 us (0.981)
  Pallas kernels: 6.17 us -> 5.16 us
    pallas_call x5 -> x4, Pallas kernels: 6.17 us -> 5.16 us  [local_call(): pl.pallas_call(kernel, out_shape=shapes[0] if single else shapes, in_spec...]
  transfers between devices with their start and end apart: 2 -> 2, of which waited for: 1 -> 1; matrix products, arithmetic and copies ran while one was open for 0% -> 0% of each run, Pallas kernels for 11% -> 6%
where the time goes in v3:
time: 30.3 us; the launch traced here: 30 us
  blocking collectives  21.1 us (70%)
  Pallas kernels  5.16 us (17%)
  starting transfers between devices  1.72 us (6%)
  local copies, waits for them, and re-layouts  0.78 us (3%)
  other arithmetic  0.64 us (2%)
  waiting for transfers between devices  0.54 us (2%)
    all_gather x1, blocking collectives, body(): gathered = lax.all_gather(slab, 'member', axis=0, tiled=False)  10.9 us
    all_to_all x1, blocking collectives, body(): received = lax.all_to_all(sums, 'member', 0, 0, tiled=True)  10.2 us
    pallas_call x4, Pallas kernels, local_call(): pl.pallas_call(kernel, out_shape=shapes[0] if single else shapes, in_spec...  5.16 us
    ppermute x2, starting transfers between devices, body(): lax.ppermute(edges, ('member', 'tile'), swap_pairs(start, n_member, n_tile))  1.72 us
    unnamed x8, local copies, waits for them, and re-layouts  0.78 us
    mul x1, other arithmetic, body(): owned = jnp.sum(received, axis=0) * norm_factor  0.62 us
  transfers between devices with their start and end apart: 2, of which 1 were waited for; matrix products, arithmetic and copies ran while one was open for 0% of the time, Pallas kernels for 6%

profile of v3, /device:TPU:0, one launch (start us, length us, event | category | flops | bytes accessed | tf_op | source)
XLA Modules:
  0.0 30.0 jit_solution(1146733097380908165)
XLA Ops:
  0.0 0.0 copy-start.3
  0.0 0.0 copy-start.2
  0.0 0.0 copy-start.1
  0.0 0.0 copy-start
  0.0 0.8 %copy-done.3 = f32[2,5,8,1,128]{4,3,2,1,0:T(1,128)S(1)} copy-done((f32[2,5,8,1,128]{4,3,2,1,0:T(1,128)S(1)}, f32[2,5,8,1,128]{4,3,2,1,0:T(1,128)}, u32[]{:S(2)}) %copy-start.3) | copy-done | bytes 40984
  0.8 10.9 %all_gather.3.gathered_ref = f32[8,10,1,8,128]{4,3,2,1,0:T(8,128)S(1)} all-gather(f32[1,10,1,8,128]{4,3,2,1,0:T(8,128)S(1)} %bitcast.7), channel_id=1, replica_groups=mesh['member'=8,'tile'=4] {'member'}, dimensions={0}, use_global_device_ids=true | all-gather | bytes 368640 | tf_op jit(solution)/shard_map/all_gather | solution.py:415
  11.7 0.0 copy-done.2
  11.7 0.0 copy-done.1
  11.7 0.0 copy-done
  11.7 1.1 %weigh.1 = (f32[512,128]{1,0:T(8,128)S(1)}, f32[4,4,8,128]{3,2,1,0:T(8,128)S(1)}, f32[4,4,8,128]{3,2,1,0:T(8,128)S(1)}, f32[16,128]{1,0:T(8,128)S(1)}, f32[16,12...) custom-call(s32[8]{0:T(128)S(1)} %copy-done.2, f32[8,10,1,8,128]{4,3,2,1,0:T(8,128)S(1)} %all_gather.3.gathered_ref, ...), custom_call_target="tpu_custom_call" | custom-call | flops 1310720 | bytes 2158624 | tf_op jit(solution)/shard_map/weigh/pallas_call | solution.py:380
  12.8 1.7 %collective-permute-start = (f32[72,128]{1,0:T(8,128)S(1)}, f32[72,128]{1,0:T(8,128)S(1)}, u32[]{:S(2)}, u32[]{:S(2)}) collective-permute-start(f32[72,128]{1,0:T(8,128)S(1)} %get-tuple-element.17), channel_id=1, source_target_pairs={{0,1},{1,0},{2,3},{3,2},{4,5},{5,4},{6,7},{7,6},{8,9},{9,8},{10,11... | collective-permute-start | bytes 110600 | tf_op jit(solution)/shard_map/ppermute | solution.py:427
  14.4 0.1 collective-permute-start.1
  14.5 1.8 %interior.1.interior_ref = f32[8,8,8,128]{3,2,1,0:T(8,128)S(1)} custom-call(f32[8,8,8,128]{3,2,1,0:T(8,128)S(1)} %bitcast.6, f32[8,8,128]{2,1,0:T(8,128)S(1)} %copy-done.1), custom_call_target="tpu_custom_call" | custom-call | flops 5242880 | bytes 557056 | tf_op jit(solution)/shard_map/interior/pallas_call | solution.py:380
  16.3 0.5 %collective-permute-done.from_first_ref = f32[72,128]{1,0:T(8,128)S(1)} collective-permute-done((f32[72,128]{1,0:T(8,128)S(1)}, f32[72,128]{1,0:T(8,128)S(1)}, u32[]{:S(2)}, u32[]{:S(2)}) %collective-permute-start) | collective-permute-done | bytes 36896 | tf_op jit(solution)/shard_map/ppermute | solution.py:427
  16.8 0.0 collective-permute-done.1.from_second_ref
  16.8 2.3 %finish.1 = f32[8,10,1,8,128]{4,3,2,1,0:T(8,128)S(1)} custom-call(s32[8]{0:T(128)S(1)} %copy-done.2, bf16[8,10,8,8,128]{4,3,2,1,0:T(8,128)(2,1)S(1)} %bitcast.5, f32[8,8,8,128]{3,2,1,0:T(8,128)S(1)} %interior.1.interior_ref, f32[4,4,8,128]{3,2,1,0:T(8,128)S(1)} %get-tuple-element.13.left_ref, f32[4,4,8,128]{3,2,1,0:T(8,128)S(1)} %get-tuple-element.14.right_ref, ...), custom_call_target="tpu_custom_call" | custom-call | flops 1310720 | bytes 2121760 | tf_op jit(solution)/shard_map/finish/pallas_call | solution.py:380
  19.1 10.2 %all_to_all.5 = f32[8,10,1,8,128]{4,3,2,1,0:T(8,128)S(1)} all-to-all(f32[8,10,1,8,128]{4,3,2,1,0:T(8,128)S(1)} %finish.1), channel_id=1, replica_groups=mesh['member'=8,'tile'=4] {'member'}, dimensions={0} | all-to-all | bytes 655360 | tf_op jit(solution)/shard_map/all_to_all | solution.py:459
  29.3 0.6 %broadcast_multiply_fusion = f32[10,8,128]{2,1,0:T(8,128)} fusion(f32[10,8,128]{2,1,0:T(8,128)S(1)} %reduce_sum.9), kind=kLoop, calls=%fused_computation | loop fusion | flops 10240 | bytes 81920 | tf_op jit(solution)/shard_map/mul | solution.py:461
  (2 shorter events, 0.0 us)
Async XLA Ops:
  0.0 0.8 %copy-start.3 = (f32[2,5,8,1,128]{4,3,2,1,0:T(1,128)S(1)}, f32[2,5,8,1,128]{4,3,2,1,0:T(1,128)}, u32[]{:S(2)}) copy-start(f32[2,5,8,1,128]{4,3,2,1,0:T(1,128)} %param.5) | copy-start | bytes 122884
  0.0 11.7 %copy-start.2 = (s32[8]{0:T(128)S(1)}, s32[8]{0:T(128)}, u32[]{:S(2)}) copy-start(s32[8]{0:T(128)} %owner_ref.3) | copy-start | bytes 100
  0.0 11.7 %copy-start.1 = (f32[8,8,128]{2,1,0:T(8,128)S(1)}, f32[8,8,128]{2,1,0:T(8,128)}, u32[]{:S(2)}) copy-start(f32[8,8,128]{2,1,0:T(8,128)} %coeff_ref.3) | copy-start | bytes 98308
  0.0 11.7 %copy-start = (bf16[8,2,5,8,8,128]{5,4,3,2,1,0:T(8,128)(2,1)S(1)}, bf16[8,2,5,8,8,128]{5,4,3,2,1,0:T(8,128)(2,1)}, u32[]{:S(2)}) copy-start(bf16[8,2,5,8,8,128]{5,4,3,2,1,0:T(8,128)(2,1)} %param.4) | copy-start | bytes 3932164
  12.8 4.0 %collective-permute-start = (f32[72,128]{1,0:T(8,128)S(1)}, f32[72,128]{1,0:T(8,128)S(1)}, u32[]{:S(2)}, u32[]{:S(2)}) collective-permute-start(f32[72,128]{1,0:T(8,128)S(1)} %get-tuple-element.17), channel_id=1, source_target_pairs={{0,1},{1,0},{2,3},{3,2},{4,5},{5,4},{6,7},{7,6},{8,9},{9,8},{10,11... | collective-permute-start | bytes 110600 | tf_op jit(solution)/shard_map/ppermute | solution.py:427
  14.4 2.4 %collective-permute-start.1 = (f32[72,128]{1,0:T(8,128)S(1)}, f32[72,128]{1,0:T(8,128)S(1)}, u32[]{:S(2)}, u32[]{:S(2)}) collective-permute-start(f32[72,128]{1,0:T(8,128)S(1)} %get-tuple-element.18), channel_id=1, source_target_pairs={{0,4},{1,2},{2,1},{3,7},{4,0},{5,6},{6,5},{7,3},{8,12},{9,10},{10,... | collective-permute-start | bytes 110600 | tf_op jit(solution)/shard_map/ppermute | solution.py:427

commit v4 on v3

--- a/solution.py
+++ b/solution.py
@@ -9,6 +9,7 @@
 
 SWEEPS = 10
 GROUPS = 4
+BLOCK = 16
 ANCHOR_WORK = 10**10
 VMEM_LIMIT = 16 * 1024 * 1024
 
@@ -155,7 +156,8 @@
     to_second_ref,
     grad_ref,
 ):
-    members, terms, levels, rows, lanes = pert_ref.shape
+    members, terms, _, lanes = pert_ref.shape
+    levels, rows, _ = coeff_ref.shape
     slab_rows = gathered_ref.shape[2]
     strip_levels, strip_rows = left_ref.shape[:2]
     left_first = jnp.broadcast_to(first_is_left(), (8, lanes))
@@ -168,15 +170,15 @@
                     owner, term, inner
                 ]
 
-    for level in range(levels):
-        base = level * rows
-        coeff = coeff_ref[level]
+    for start in range(0, levels * rows, BLOCK):
+        block = pl.ds(start, BLOCK)
+        coeff = jnp.concatenate([coeff_ref[l] for l in range(levels)], axis=0)[start : start + BLOCK]
         gradients = [
-            coeff * grad_ref[pl.ds(term * levels * rows + base, rows), :] for term in range(terms)
+            coeff * grad_ref[pl.ds(term * levels * rows + start, BLOCK), :] for term in range(terms)
         ]
         for member in range(members):
-            field_ref[pl.ds(base * members + member, rows, stride=members), :] = total(
-                pert_ref[member, term, level].astype(jnp.float32) * gradients[term]
+            field_ref[pl.ds(start * members + member, BLOCK, stride=members), :] = total(
+                pert_ref[member, term, block, :].astype(jnp.float32) * gradients[term]
                 for term in range(terms)
             )
 
@@ -309,7 +311,8 @@
     keep_right_ref,
     square_right_ref,
 ):
-    members, terms, levels, rows, lanes = pert_ref.shape
+    members, terms, _, lanes = pert_ref.shape
+    levels, rows = interior_ref.shape[:2]
     slab_rows = out_ref.shape[2]
     part = lanes // GROUPS
     left_first = first_is_left()
@@ -348,15 +351,15 @@
                     (lane < SWEEPS) | (lane >= lanes - SWEEPS), ends, interior_ref[l, r]
                 )
 
-    for level in range(levels):
-        base = level * rows
+    for start in range(0, levels * rows, BLOCK):
+        block = pl.ds(start, BLOCK)
         fields = [
-            local_ref[pl.ds(base * members + member, rows, stride=members), :]
+            local_ref[pl.ds(start * members + member, BLOCK, stride=members), :]
             for member in range(members)
         ]
         for term in range(terms):
-            sum_ref[pl.ds(term * levels * rows + base, rows), :] = total(
-                pert_ref[member, term, level].astype(jnp.float32) * fields[member]
+            sum_ref[pl.ds(term * levels * rows + start, BLOCK), :] = total(
+                pert_ref[member, term, block, :].astype(jnp.float32) * fields[member]
                 for member in range(members)
             )
     for slab in range(rows // slab_rows):
@@ -409,7 +412,7 @@
     grad_shape = (terms * levels * rows, lanes)
     vmem, smem = pltpu.VMEM, pltpu.SMEM
 
-    pert = perturbations.reshape(members, terms, levels, rows, lanes)
+    pert = perturbations.reshape(members, terms, levels * rows, lanes)
     slab = gradient_store.reshape(terms, levels, slab_rows, lanes).swapaxes(1, 2)
     anchor = local_call(anchor_kernel, "anchor", [(8, lanes)], [], (), (), ANCHOR_WORK)
     gathered = lax.all_gather(slab, "member", axis=0, tiled=False)

time: 30.3 us -> 30.3 us (level)
  no operation moved by 1% of the time
where the time goes in v4:
time: 30.3 us; the launch traced here: 30 us
  blocking collectives  21.1 us (70%)
  Pallas kernels  5.21 us (17%)
  starting transfers between devices  1.72 us (6%)
  local copies, waits for them, and re-layouts  0.78 us (3%)
  other arithmetic  0.64 us (2%)
  waiting for transfers between devices  0.54 us (2%)
    all_gather x1, blocking collectives, body(): gathered = lax.all_gather(slab, 'member', axis=0, tiled=False)  10.9 us
    all_to_all x1, blocking collectives, body(): received = lax.all_to_all(sums, 'member', 0, 0, tiled=True)  10.2 us
    pallas_call x4, Pallas kernels, local_call(): pl.pallas_call(kernel, out_shape=shapes[0] if single else shapes, in_spec...  5.21 us
    ppermute x2, starting transfers between devices, body(): lax.ppermute(edges, ('member', 'tile'), swap_pairs(start, n_member, n_tile))  1.72 us
    unnamed x8, local copies, waits for them, and re-layouts  0.78 us
    mul x1, other arithmetic, body(): owned = jnp.sum(received, axis=0) * norm_factor  0.62 us
  transfers between devices with their start and end apart: 2, of which 1 were waited for; matrix products, arithmetic and copies ran while one was open for 0% of the time, Pallas kernels for 6%

profile of v4, /device:TPU:0, one launch (start us, length us, event | category | flops | bytes accessed | tf_op | source)
XLA Modules:
  0.0 30.0 jit_solution(11020164595583037056)
XLA Ops:
  0.0 0.0 copy-start.3
  0.0 0.0 copy-start.2
  0.0 0.0 copy-start.1
  0.0 0.0 copy-start
  0.0 0.8 %copy-done.3 = f32[2,5,8,1,128]{4,3,2,1,0:T(1,128)S(1)} copy-done((f32[2,5,8,1,128]{4,3,2,1,0:T(1,128)S(1)}, f32[2,5,8,1,128]{4,3,2,1,0:T(1,128)}, u32[]{:S(2)}) %copy-start.3) | copy-done | bytes 40984
  0.8 10.9 %all_gather.3.gathered_ref = f32[8,10,1,8,128]{4,3,2,1,0:T(8,128)S(1)} all-gather(f32[1,10,1,8,128]{4,3,2,1,0:T(8,128)S(1)} %bitcast.7), channel_id=1, replica_groups=mesh['member'=8,'tile'=4] {'member'}, dimensions={0}, use_global_device_ids=true | all-gather | bytes 368640 | tf_op jit(solution)/shard_map/all_gather | solution.py:418
  11.7 0.0 copy-done.2
  11.7 0.0 copy-done.1
  11.7 0.0 copy-done
  11.7 1.1 %weigh.1 = (f32[512,128]{1,0:T(8,128)S(1)}, f32[4,4,8,128]{3,2,1,0:T(8,128)S(1)}, f32[4,4,8,128]{3,2,1,0:T(8,128)S(1)}, f32[16,128]{1,0:T(8,128)S(1)}, f32[16,12...) custom-call(s32[8]{0:T(128)S(1)} %copy-done.2, f32[8,10,1,8,128]{4,3,2,1,0:T(8,128)S(1)} %all_gather.3.gathered_ref, ...), custom_call_target="tpu_custom_call" | custom-call | flops 1310720 | bytes 2158624 | tf_op jit(solution)/shard_map/weigh/pallas_call | solution.py:383
  12.8 1.7 %collective-permute-start = (f32[72,128]{1,0:T(8,128)S(1)}, f32[72,128]{1,0:T(8,128)S(1)}, u32[]{:S(2)}, u32[]{:S(2)}) collective-permute-start(f32[72,128]{1,0:T(8,128)S(1)} %get-tuple-element.17), channel_id=1, source_target_pairs={{0,1},{1,0},{2,3},{3,2},{4,5},{5,4},{6,7},{7,6},{8,9},{9,8},{10,11... | collective-permute-start | bytes 110600 | tf_op jit(solution)/shard_map/ppermute | solution.py:430
  14.5 0.1 collective-permute-start.1
  14.5 1.8 %interior.1.interior_ref = f32[8,8,8,128]{3,2,1,0:T(8,128)S(1)} custom-call(f32[8,8,8,128]{3,2,1,0:T(8,128)S(1)} %bitcast.6, f32[8,8,128]{2,1,0:T(8,128)S(1)} %copy-done.1), custom_call_target="tpu_custom_call" | custom-call | flops 5242880 | bytes 557056 | tf_op jit(solution)/shard_map/interior/pallas_call | solution.py:383
  16.3 0.5 %collective-permute-done.from_first_ref = f32[72,128]{1,0:T(8,128)S(1)} collective-permute-done((f32[72,128]{1,0:T(8,128)S(1)}, f32[72,128]{1,0:T(8,128)S(1)}, u32[]{:S(2)}, u32[]{:S(2)}) %collective-permute-start) | collective-permute-done | bytes 36896 | tf_op jit(solution)/shard_map/ppermute | solution.py:430
  16.8 0.0 collective-permute-done.1.from_second_ref
  16.8 2.3 %finish.1 = f32[8,10,1,8,128]{4,3,2,1,0:T(8,128)S(1)} custom-call(s32[8]{0:T(128)S(1)} %copy-done.2, bf16[8,10,64,128]{3,2,1,0:T(8,128)(2,1)S(1)} %bitcast.5, f32[8,8,8,128]{3,2,1,0:T(8,128)S(1)} %interior.1.interior_ref, f32[4,4,8,128]{3,2,1,0:T(8,128)S(1)} %get-tuple-element.13.left_ref, f32[4,4,8,128]{3,2,1,0:T(8,128)S(1)} %get-tuple-element.14.right_ref, ...), custom_call_target="tpu_custom_call" | custom-call | flops 1310720 | bytes 2121760 | tf_op jit(solution)/shard_map/finish/pallas_call | solution.py:383
  19.2 10.2 %all_to_all.5 = f32[8,10,1,8,128]{4,3,2,1,0:T(8,128)S(1)} all-to-all(f32[8,10,1,8,128]{4,3,2,1,0:T(8,128)S(1)} %finish.1), channel_id=1, replica_groups=mesh['member'=8,'tile'=4] {'member'}, dimensions={0} | all-to-all | bytes 655360 | tf_op jit(solution)/shard_map/all_to_all | solution.py:462
  29.4 0.6 %broadcast_multiply_fusion = f32[10,8,128]{2,1,0:T(8,128)} fusion(f32[10,8,128]{2,1,0:T(8,128)S(1)} %reduce_sum.9), kind=kLoop, calls=%fused_computation | loop fusion | flops 10240 | bytes 81920 | tf_op jit(solution)/shard_map/mul | solution.py:464
  (2 shorter events, 0.0 us)
Async XLA Ops:
  0.0 0.8 %copy-start.3 = (f32[2,5,8,1,128]{4,3,2,1,0:T(1,128)S(1)}, f32[2,5,8,1,128]{4,3,2,1,0:T(1,128)}, u32[]{:S(2)}) copy-start(f32[2,5,8,1,128]{4,3,2,1,0:T(1,128)} %param.5) | copy-start | bytes 122884
  0.0 11.7 %copy-start.2 = (s32[8]{0:T(128)S(1)}, s32[8]{0:T(128)}, u32[]{:S(2)}) copy-start(s32[8]{0:T(128)} %owner_ref.3) | copy-start | bytes 100
  0.0 11.7 %copy-start.1 = (f32[8,8,128]{2,1,0:T(8,128)S(1)}, f32[8,8,128]{2,1,0:T(8,128)}, u32[]{:S(2)}) copy-start(f32[8,8,128]{2,1,0:T(8,128)} %coeff_ref.3) | copy-start | bytes 98308
  0.0 11.7 %copy-start = (bf16[8,2,5,8,8,128]{5,4,3,2,1,0:T(8,128)(2,1)S(1)}, bf16[8,2,5,8,8,128]{5,4,3,2,1,0:T(8,128)(2,1)}, u32[]{:S(2)}) copy-start(bf16[8,2,5,8,8,128]{5,4,3,2,1,0:T(8,128)(2,1)} %param.4) | copy-start | bytes 3932164
  12.8 4.0 %collective-permute-start = (f32[72,128]{1,0:T(8,128)S(1)}, f32[72,128]{1,0:T(8,128)S(1)}, u32[]{:S(2)}, u32[]{:S(2)}) collective-permute-start(f32[72,128]{1,0:T(8,128)S(1)} %get-tuple-element.17), channel_id=1, source_target_pairs={{0,1},{1,0},{2,3},{3,2},{4,5},{5,4},{6,7},{7,6},{8,9},{9,8},{10,11... | collective-permute-start | bytes 110600 | tf_op jit(solution)/shard_map/ppermute | solution.py:430
  14.5 2.4 %collective-permute-start.1 = (f32[72,128]{1,0:T(8,128)S(1)}, f32[72,128]{1,0:T(8,128)S(1)}, u32[]{:S(2)}, u32[]{:S(2)}) collective-permute-start(f32[72,128]{1,0:T(8,128)S(1)} %get-tuple-element.18), channel_id=1, source_target_pairs={{0,4},{1,2},{2,1},{3,7},{4,0},{5,6},{6,5},{7,3},{8,12},{9,10},{10,... | collective-permute-start | bytes 110600 | tf_op jit(solution)/shard_map/ppermute | solution.py:430

commit v5 on v3

--- a/solution.py
+++ b/solution.py
@@ -153,6 +153,7 @@
     coeff_right_ref,
     to_first_ref,
     to_second_ref,
+    wide_ref,
     grad_ref,
 ):
     members, terms, levels, rows, lanes = pert_ref.shape
@@ -175,10 +176,12 @@
             coeff * grad_ref[pl.ds(term * levels * rows + base, rows), :] for term in range(terms)
         ]
         for member in range(members):
-            field_ref[pl.ds(base * members + member, rows, stride=members), :] = total(
-                pert_ref[member, term, level].astype(jnp.float32) * gradients[term]
-                for term in range(terms)
-            )
+            pieces = []
+            for term in range(terms):
+                wide = pert_ref[member, term, level].astype(jnp.float32)
+                wide_ref[member, term, level] = wide
+                pieces.append(wide * gradients[term])
+            field_ref[pl.ds(base * members + member, rows, stride=members), :] = total(pieces)
 
     pairs = strip_levels * strip_rows // 2
     fields, coeffs = [], []
@@ -356,7 +359,7 @@
         ]
         for term in range(terms):
             sum_ref[pl.ds(term * levels * rows + base, rows), :] = total(
-                pert_ref[member, term, level].astype(jnp.float32) * fields[member]
+                pert_ref[member, term, level] * fields[member]
                 for member in range(members)
             )
     for slab in range(rows // slab_rows):
@@ -414,10 +417,11 @@
     anchor = local_call(anchor_kernel, "anchor", [(8, lanes)], [], (), (), ANCHOR_WORK)
     gathered = lax.all_gather(slab, "member", axis=0, tiled=False)
 
-    field, left, right, coeff_left, coeff_right, to_first, to_second = local_call(
+    field, left, right, coeff_left, coeff_right, to_first, to_second, wide = local_call(
         weigh_kernel,
         "weigh",
-        [flat_field, wide_strip, wide_strip, coeff_strip, coeff_strip, edge_shape, edge_shape],
+        [flat_field, wide_strip, wide_strip, coeff_strip, coeff_strip, edge_shape, edge_shape]
+        + [pert.shape],
         [grad_shape],
         (slab_owner, gathered, pert, diffusivity, anchor),
         (smem, vmem, vmem, vmem, vmem),
@@ -444,7 +448,7 @@
         [flat_field, grad_shape] + [wide_strip] * 4,
         (
             slab_owner,
-            pert,
+            wide,
             interior,
             left,
             right,

time: 30.3 us -> 30.3 us (level)
  no operation moved by 1% of the time
where the time goes in v5:
time: 30.3 us; the launch traced here: 30 us
  blocking collectives  21.1 us (70%)
  Pallas kernels  5.15 us (17%)
  starting transfers between devices  1.72 us (6%)
  local copies, waits for them, and re-layouts  0.78 us (3%)
  other arithmetic  0.64 us (2%)
  waiting for transfers between devices  0.57 us (2%)
    all_gather x1, blocking collectives, body(): gathered = lax.all_gather(slab, 'member', axis=0, tiled=False)  10.9 us
    all_to_all x1, blocking collectives, body(): received = lax.all_to_all(sums, 'member', 0, 0, tiled=True)  10.2 us
    pallas_call x4, Pallas kernels, local_call(): pl.pallas_call(kernel, out_shape=shapes[0] if single else shapes, in_spec...  5.15 us
    ppermute x2, starting transfers between devices, body(): lax.ppermute(edges, ('member', 'tile'), swap_pairs(start, n_member, n_tile))  1.72 us
    unnamed x8, local copies, waits for them, and re-layouts  0.78 us
    mul x1, other arithmetic, body(): owned = jnp.sum(received, axis=0) * norm_factor  0.62 us
  transfers between devices with their start and end apart: 2, of which 1 were waited for; matrix products, arithmetic and copies ran while one was open for 0% of the time, Pallas kernels for 6%

profile of v5, /device:TPU:0, one launch (start us, length us, event | category | flops | bytes accessed | tf_op | source)
XLA Modules:
  0.0 30.0 jit_solution(16173402620015561331)
XLA Ops:
  0.0 0.0 copy-start.3
  0.0 0.0 copy-start.2
  0.0 0.0 copy-start.1
  0.0 0.0 copy-start
  0.0 0.8 %copy-done.3 = f32[2,5,8,1,128]{4,3,2,1,0:T(1,128)S(1)} copy-done((f32[2,5,8,1,128]{4,3,2,1,0:T(1,128)S(1)}, f32[2,5,8,1,128]{4,3,2,1,0:T(1,128)}, u32[]{:S(2)}) %copy-start.3) | copy-done | bytes 40984
  0.8 10.9 %all_gather.3.gathered_ref = f32[8,10,1,8,128]{4,3,2,1,0:T(8,128)S(1)} all-gather(f32[1,10,1,8,128]{4,3,2,1,0:T(8,128)S(1)} %bitcast.6), channel_id=1, replica_groups=mesh['member'=8,'tile'=4] {'member'}, dimensions={0}, use_global_device_ids=true | all-gather | bytes 368640 | tf_op jit(solution)/shard_map/all_gather | solution.py:418
  11.7 0.0 copy-done.2
  11.7 0.0 copy-done.1
  11.7 0.0 copy-done
  11.7 1.2 %weigh.1 = (f32[512,128]{1,0:T(8,128)S(1)}, f32[4,4,8,128]{3,2,1,0:T(8,128)S(1)}, f32[4,4,8,128]{3,2,1,0:T(8,128)S(1)}, f32[16,128]{1,0:T(8,128)S(1)}, f32[16,12...) custom-call(s32[8]{0:T(128)S(1)} %copy-done.2, ...), custom_call_target="tpu_custom_call" | custom-call | flops 1310720 | bytes 4780064 | tf_op jit(solution)/shard_map/weigh/pallas_call | solution.py:383
  12.9 1.7 %collective-permute-start = (f32[72,128]{1,0:T(8,128)S(1)}, f32[72,128]{1,0:T(8,128)S(1)}, u32[]{:S(2)}, u32[]{:S(2)}) collective-permute-start(f32[72,128]{1,0:T(8,128)S(1)} %get-tuple-element.19), channel_id=1, source_target_pairs={{0,1},{1,0},{2,3},{3,2},{4,5},{5,4},{6,7},{7,6},{8,9},{9,8},{10,11... | collective-permute-start | bytes 110600 | tf_op jit(solution)/shard_map/ppermute | solution.py:431
  14.6 0.1 collective-permute-start.1
  14.6 1.7 %interior.1.interior_ref = f32[8,8,8,128]{3,2,1,0:T(8,128)S(1)} custom-call(f32[8,8,8,128]{3,2,1,0:T(8,128)S(1)} %bitcast.5, f32[8,8,128]{2,1,0:T(8,128)S(1)} %copy-done.1), custom_call_target="tpu_custom_call" | custom-call | flops 5242880 | bytes 557056 | tf_op jit(solution)/shard_map/interior/pallas_call | solution.py:383
  16.4 0.6 %collective-permute-done.from_first_ref = f32[72,128]{1,0:T(8,128)S(1)} collective-permute-done((f32[72,128]{1,0:T(8,128)S(1)}, f32[72,128]{1,0:T(8,128)S(1)}, u32[]{:S(2)}, u32[]{:S(2)}) %collective-permute-start) | collective-permute-done | bytes 36896 | tf_op jit(solution)/shard_map/ppermute | solution.py:431
  17.0 0.0 collective-permute-done.1.from_second_ref
  17.0 2.2 %finish.1 = f32[8,10,1,8,128]{4,3,2,1,0:T(8,128)S(1)} custom-call(s32[8]{0:T(128)S(1)} %copy-done.2, f32[8,10,8,8,128]{4,3,2,1,0:T(8,128)S(1)} %get-tuple-element.13.pert_ref, f32[8,8,8,128]{3,2,1,0:T(8,128)S(1)} %interior.1.interior_ref, f32[4,4,8,128]{3,2,1,0:T(8,128)S(1)} %get-tuple-element.15.left_ref, f32[4,4,8,128]{3,2,1,0:T(8,128)S(1)} %get-tuple-element.16.right_ref, ...), custom_call_target="tpu_custom_call" | custom-call | flops 1310720 | bytes 3432480 | tf_op jit(solution)/shard_map/finish/pallas_call | solution.py:383
  19.1 10.2 %all_to_all.5 = f32[8,10,1,8,128]{4,3,2,1,0:T(8,128)S(1)} all-to-all(f32[8,10,1,8,128]{4,3,2,1,0:T(8,128)S(1)} %finish.1), channel_id=1, replica_groups=mesh['member'=8,'tile'=4] {'member'}, dimensions={0} | all-to-all | bytes 655360 | tf_op jit(solution)/shard_map/all_to_all | solution.py:463
  29.4 0.6 %broadcast_multiply_fusion = f32[10,8,128]{2,1,0:T(8,128)} fusion(f32[10,8,128]{2,1,0:T(8,128)S(1)} %reduce_sum.9), kind=kLoop, calls=%fused_computation | loop fusion | flops 10240 | bytes 81920 | tf_op jit(solution)/shard_map/mul | solution.py:465
  (2 shorter events, 0.0 us)
Async XLA Ops:
  0.0 0.8 %copy-start.3 = (f32[2,5,8,1,128]{4,3,2,1,0:T(1,128)S(1)}, f32[2,5,8,1,128]{4,3,2,1,0:T(1,128)}, u32[]{:S(2)}) copy-start(f32[2,5,8,1,128]{4,3,2,1,0:T(1,128)} %param.5) | copy-start | bytes 122884
  0.0 11.7 %copy-start.2 = (s32[8]{0:T(128)S(1)}, s32[8]{0:T(128)}, u32[]{:S(2)}) copy-start(s32[8]{0:T(128)} %owner_ref.3) | copy-start | bytes 100
  0.0 11.7 %copy-start.1 = (f32[8,8,128]{2,1,0:T(8,128)S(1)}, f32[8,8,128]{2,1,0:T(8,128)}, u32[]{:S(2)}) copy-start(f32[8,8,128]{2,1,0:T(8,128)} %coeff_ref.3) | copy-start | bytes 98308
  0.0 11.7 %copy-start = (bf16[8,2,5,8,8,128]{5,4,3,2,1,0:T(8,128)(2,1)S(1)}, bf16[8,2,5,8,8,128]{5,4,3,2,1,0:T(8,128)(2,1)}, u32[]{:S(2)}) copy-start(bf16[8,2,5,8,8,128]{5,4,3,2,1,0:T(8,128)(2,1)} %param.4) | copy-start | bytes 3932164
  12.9 4.0 %collective-permute-start = (f32[72,128]{1,0:T(8,128)S(1)}, f32[72,128]{1,0:T(8,128)S(1)}, u32[]{:S(2)}, u32[]{:S(2)}) collective-permute-start(f32[72,128]{1,0:T(8,128)S(1)} %get-tuple-element.19), channel_id=1, source_target_pairs={{0,1},{1,0},{2,3},{3,2},{4,5},{5,4},{6,7},{7,6},{8,9},{9,8},{10,11... | collective-permute-start | bytes 110600 | tf_op jit(solution)/shard_map/ppermute | solution.py:431
  14.6 2.4 %collective-permute-start.1 = (f32[72,128]{1,0:T(8,128)S(1)}, f32[72,128]{1,0:T(8,128)S(1)}, u32[]{:S(2)}, u32[]{:S(2)}) collective-permute-start(f32[72,128]{1,0:T(8,128)S(1)} %get-tuple-element.20), channel_id=1, source_target_pairs={{0,4},{1,2},{2,1},{3,7},{4,0},{5,6},{6,5},{7,3},{8,12},{9,10},{10,... | collective-permute-start | bytes 110600 | tf_op jit(solution)/shard_map/ppermute | solution.py:431

commit v6 on v3

--- a/solution.py
+++ b/solution.py
@@ -94,6 +94,19 @@
 def without_partner(is_left, n_tile):
     tile = lax.axis_index("tile")
     return jnp.where(is_left, tile == 0, tile == n_tile - 1)
+
+
+def is_outer():
+    tile = lax.axis_index("tile")
+    return (tile == 0) | ((tile == lax.axis_size("tile") - 1) & first_is_left())
+
+
+def early_is_left():
+    return jnp.logical_xor(is_outer(), first_is_left())
+
+
+def outer_lanes(shape, is_left):
+    return (lane_index(shape) + jnp.where(is_left, 0, SWEEPS)) % shape[-1] < SWEEPS
 
 
 def total(terms):
@@ -206,7 +219,19 @@
 
 
 def interior_kernel(
-    field_ref, coeff_ref, out_ref, other_ref, keep_ref, square_ref, inverse_ref
+    field_ref,
+    coeff_ref,
+    left_ref,
+    right_ref,
+    coeff_left_ref,
+    coeff_right_ref,
+    out_ref,
+    outer_ref,
+    other_ref,
+    keep_ref,
+    square_ref,
+    strip_keep_ref,
+    strip_square_ref,
 ):
     levels, rows, members, lanes = field_ref.shape
     row_index = lax.broadcasted_iota(jnp.int32, (rows, lanes), 0)
@@ -222,15 +247,17 @@
             beside.append(coeff_ref[level - 1])
         if level < levels - 1:
             beside.append(coeff_ref[level + 1])
-        keep_ref[level] = 1.0 - here * total(beside)
-        square_ref[level] = here * here
-        inverse_ref[level] = 1.0 / here
+        keep = 1.0 - here * total(beside)
+        square = here * here
+        for row in range(rows):
+            keep_ref[level, row] = spread(keep[row : row + 1], members)
+            square_ref[level, row] = spread(square[row : row + 1], members)
 
     def keep_at(level, row):
-        return keep_ref[level, pl.ds(row, 1), :]
+        return keep_ref[level, row]
 
     def square_at(level, row):
-        return square_ref[level, pl.ds(row, 1), :]
+        return square_ref[level, row]
 
     sweep(field_ref, other_ref, keep_at, square_at)
     sweep(other_ref, out_ref, keep_at, square_at)
@@ -242,59 +269,112 @@
 
     lax.fori_loop(0, SWEEPS // 2 - 1, pair, 0)
     for level in range(levels):
+        inverse = 1.0 / coeff_ref[level]
         for row in range(rows):
-            out_ref[level, row] = out_ref[level, row] * inverse_ref[level, pl.ds(row, 1), :]
-
-
-class Strips:
-    def __init__(self, strip_ref, coeff_ref, edge_at, is_left, keep_ref, square_ref):
-        self.levels, self.rows, self.members, lanes = strip_ref.shape
-        self.coeff_ref, self.keep_ref, self.square_ref = coeff_ref, keep_ref, square_ref
-        part = lanes // GROUPS
-        pairs = self.levels * self.rows // 2
-        shape = (self.members, lanes)
-        self.even_group = group_index(shape, SWEEPS if is_left else part - SWEEPS) % 2 == 0
-        place = lane_index(shape) % part
-        halo = place >= part - SWEEPS if is_left else place < SWEEPS
-        self.planes, coeffs = [], []
-        for level in range(self.levels):
-            plane, coeff_plane = [], []
-            for row in range(self.rows):
-                index = level * self.rows + row
-                edge = edge_at(index // 2 * self.members, self.members)
-                coeff_edge = spread(edge_at(pairs * self.members + index // 2, 1), self.members)
-                plane.append(joined_strip(strip_ref[level, row], edge, index, halo))
-                coeff_plane.append(joined_strip(self.own_coeff(level, row), coeff_edge, index, halo))
-            self.planes.append(plane)
-            coeffs.append(coeff_plane)
-        for level in range(self.levels):
-            for row in range(self.rows):
-                here = coeffs[level][row]
-                keep_ref[level, row] = 1.0 - here * around(coeffs, level, row, self.even_group)
-                square_ref[level, row] = here * here
-
-    def own_coeff(self, level, row):
-        return spread(self.coeff_ref[pl.ds(level * self.rows + row, 1), :], self.members)
-
-    def step(self):
-        self.planes = [
+            out_ref[level, row] = out_ref[level, row] * spread(inverse[row : row + 1], members)
+
+    @pl.when(is_outer())
+    def _():
+        strips = left_ref, right_ref, coeff_left_ref, coeff_right_ref
+        edge_at = lambda place, count: jnp.zeros((count, lanes), jnp.float32)
+        planes = swept_strips(strips, edge_at, early_is_left(), strip_keep_ref, strip_square_ref)
+        store_planes(outer_ref, planes)
+
+
+def swept_strips(strips, edge_at, is_left, keep_ref, square_ref):
+    left_ref, right_ref, coeff_left_ref, coeff_right_ref = strips
+    levels, rows, members, lanes = left_ref.shape
+    outside = without_partner(is_left, lax.axis_size("tile"))
+    part = lanes // GROUPS
+    pairs = levels * rows // 2
+    lane = lane_index((members, lanes))
+    even_group = (lane + jnp.where(is_left, SWEEPS, part - SWEEPS)) // part % 2 == 0
+    halo = (lane + jnp.where(is_left, SWEEPS, 0)) % part < SWEEPS
+
+    def own_coeff(level, row):
+        place = pl.ds(level * rows + row, 1)
+        return spread(jnp.where(is_left, coeff_left_ref[place, :], coeff_right_ref[place, :]), members)
+
+    planes, coeffs = [], []
+    for level in range(levels):
+        plane, coeff_plane = [], []
+        for row in range(rows):
+            index = level * rows + row
+            edge = jnp.where(outside, 0.0, edge_at(index // 2 * members, members))
+            coeff_edge = jnp.where(outside, 0.0, edge_at(pairs * members + index // 2, 1))
+            own = jnp.where(is_left, left_ref[level, row], right_ref[level, row])
+            plane.append(joined_strip(own, edge, index, halo))
+            coeff_plane.append(
+                joined_strip(own_coeff(level, row), spread(coeff_edge, members), index, halo)
+            )
+        planes.append(plane)
+        coeffs.append(coeff_plane)
+    for level in range(levels):
+        for row in range(rows):
+            here = coeffs[level][row]
+            keep_ref[level, row] = 1.0 - here * around(coeffs, level, row, even_group)
+            square_ref[level, row] = here * here
+    for _ in range(SWEEPS):
+        planes = [
             [
-                self.keep_ref[level, row] * self.planes[level][row]
-                + self.square_ref[level, row] * around(self.planes, level, row, self.even_group)
-                for row in range(self.rows)
+                keep_ref[level, row] * planes[level][row]
+                + square_ref[level, row] * around(planes, level, row, even_group)
+                for row in range(rows)
             ]
-            for level in range(self.levels)
+            for level in range(levels)
         ]
-
-    def final(self, level, row):
-        coeff = self.own_coeff(level, row)
-        return self.planes[level][row] / jnp.where(coeff > 0.0, coeff, 1.0)
+    for level in range(levels):
+        for row in range(rows):
+            coeff = own_coeff(level, row)
+            planes[level][row] = planes[level][row] / jnp.where(coeff > 0.0, coeff, 1.0)
+    return planes
+
+
+def store_planes(ref, planes):
+    for level, plane in enumerate(planes):
+        for row, value in enumerate(plane):
+            ref[level, row] = value
+
+
+def early_kernel(
+    interior_ref,
+    outer_ref,
+    left_ref,
+    right_ref,
+    coeff_left_ref,
+    coeff_right_ref,
+    edge_ref,
+    out_ref,
+    swept_ref,
+    keep_ref,
+    square_ref,
+):
+    levels, rows, members, lanes = interior_ref.shape
+    part = lanes // GROUPS
+    is_left = early_is_left()
+
+    @pl.when(is_outer())
+    def _():
+        swept_ref[...] = outer_ref[...]
+
+    @pl.when(jnp.logical_not(is_outer()))
+    def _():
+        strips = left_ref, right_ref, coeff_left_ref, coeff_right_ref
+        edge_at = lambda place, count: edge_ref[pl.ds(place, count), :]
+        store_planes(swept_ref, swept_strips(strips, edge_at, is_left, keep_ref, square_ref))
+
+    ends = outer_lanes((members, lanes), is_left)
+    for level in range(swept_ref.shape[0]):
+        for row in range(swept_ref.shape[1]):
+            final = swept_ref[level, row]
+            for g, (l, r) in enumerate(mirrors(level, row, levels, rows)):
+                out_ref[l, r] = jnp.where(ends, lane_roll(final, -part * g), interior_ref[l, r])
 
 
 def finish_kernel(
     owner_ref,
     pert_ref,
-    interior_ref,
+    partial_ref,
     left_ref,
     right_ref,
     coeff_left_ref,
@@ -304,48 +384,27 @@
     out_ref,
     local_ref,
     sum_ref,
-    keep_left_ref,
-    square_left_ref,
-    keep_right_ref,
-    square_right_ref,
+    keep_ref,
+    square_ref,
 ):
     members, terms, levels, rows, lanes = pert_ref.shape
     slab_rows = out_ref.shape[2]
     part = lanes // GROUPS
-    left_first = first_is_left()
-
-    def edge_reader(is_left):
-        outside = without_partner(is_left, lax.axis_size("tile"))
-
-        def edge_at(place, count):
-            first = from_first_ref[pl.ds(place, count), :]
-            second = from_second_ref[pl.ds(place, count), :]
-            edge = jnp.where(left_first == is_left, first, second)
-            return jnp.where(outside, 0.0, edge)
-
-        return edge_at
-
-    left = Strips(
-        left_ref, coeff_left_ref, edge_reader(True), True, keep_left_ref, square_left_ref
-    )
-    right = Strips(
-        right_ref, coeff_right_ref, edge_reader(False), False, keep_right_ref, square_right_ref
-    )
-    for _ in range(SWEEPS):
-        left.step()
-        right.step()
-    lane = lane_index((members, lanes))
-    for level in range(left.levels):
-        for row in range(left.rows):
-            left_end, right_end = left.final(level, row), right.final(level, row)
+    is_left = jnp.logical_not(early_is_left())
+    outer = is_outer()
+
+    def edge_at(place, count):
+        place = pl.ds(place, count)
+        return jnp.where(outer, from_first_ref[place, :], from_second_ref[place, :])
+
+    strips = left_ref, right_ref, coeff_left_ref, coeff_right_ref
+    planes = swept_strips(strips, edge_at, is_left, keep_ref, square_ref)
+    ends = outer_lanes((members, lanes), is_left)
+    for level, plane in enumerate(planes):
+        for row, final in enumerate(plane):
             for g, (l, r) in enumerate(mirrors(level, row, levels, rows)):
-                ends = jnp.where(
-                    lane < lanes // 2,
-                    lane_roll(left_end, -part * g),
-                    lane_roll(right_end, -part * g),
-                )
                 local_ref[pl.ds((l * rows + r) * members, members), :] = jnp.where(
-                    (lane < SWEEPS) | (lane >= lanes - SWEEPS), ends, interior_ref[l, r]
+                    ends, lane_roll(final, -part * g), partial_ref[l, r]
                 )
 
     for level in range(levels):
@@ -428,31 +487,31 @@
         for start, edges in ((0, to_first), (1, to_second))
     )
 
-    interior = local_call(
+    strips = (left, right, coeff_left, coeff_right)
+    interior, outer = local_call(
         interior_kernel,
         "interior",
+        [wide_field, wide_strip],
+        [wide_field] * 3 + [wide_strip] * 2,
+        (field.reshape(wide_field), diffusivity) + strips,
+        (vmem,) * 6,
+        8 * SWEEPS * members * cells,
+    )
+    partial = local_call(
+        early_kernel,
+        "early_strips",
         [wide_field],
-        [wide_field, field_coeff, field_coeff, field_coeff],
-        (field.reshape(wide_field), diffusivity),
-        (vmem,) * 2,
-        8 * SWEEPS * members * cells,
+        [wide_strip] * 3,
+        (interior, outer) + strips + (from_first,),
+        (vmem,) * 7,
+        2 * SWEEPS * members * cells,
     )
     sums = local_call(
         finish_kernel,
         "finish",
         [(n_member, terms, slab_rows, levels, lanes)],
-        [flat_field, grad_shape] + [wide_strip] * 4,
-        (
-            slab_owner,
-            pert,
-            interior,
-            left,
-            right,
-            coeff_left,
-            coeff_right,
-            from_first,
-            from_second,
-        ),
+        [flat_field, grad_shape] + [wide_strip] * 2,
+        (slab_owner, pert, partial) + strips + (from_first, from_second),
         (smem,) + (vmem,) * 8,
         2 * terms * members * cells,
     )

time: 30.3 us -> 30.5 us (level)
  Pallas kernels: 5.16 us -> 5.97 us
  waiting for transfers between devices: 0.54 us -> 0.01 us
    pallas_call x4 -> x5, Pallas kernels: 5.16 us -> 5.97 us  [local_call(): pl.pallas_call(kernel, out_shape=shapes[0] if single else shapes, in_spec...]
    ppermute x2, waiting for transfers between devices: 0.54 us -> 0.01 us  [body(): lax.ppermute(edges, ('member', 'tile'), swap_pairs(start, n_member, n_tile))]
  transfers between devices with their start and end apart: 2 -> 2, of which waited for: 1 -> 0; matrix products, arithmetic and copies ran while one was open for 0% -> 0% of each run, Pallas kernels for 6% -> 9%
where the time goes in v6:
time: 30.5 us; the launch traced here: 30.3 us
  blocking collectives  21.1 us (69%)
  Pallas kernels  5.97 us (20%)
  starting transfers between devices  1.72 us (6%)
  local copies, waits for them, and re-layouts  0.78 us (3%)
  other arithmetic  0.64 us (2%)
    all_gather x1, blocking collectives, body(): gathered = lax.all_gather(slab, 'member', axis=0, tiled=False)  10.9 us
    all_to_all x1, blocking collectives, body(): received = lax.all_to_all(sums, 'member', 0, 0, tiled=True)  10.3 us
    pallas_call x5, Pallas kernels, local_call(): pl.pallas_call(kernel, out_shape=shapes[0] if single else shapes, in_spec...  5.97 us
    ppermute x2, starting transfers between devices, body(): lax.ppermute(edges, ('member', 'tile'), swap_pairs(start, n_member, n_tile))  1.72 us
    unnamed x8, local copies, waits for them, and re-layouts  0.78 us
    mul x1, other arithmetic, body(): owned = jnp.sum(received, axis=0) * norm_factor  0.62 us
  transfers between devices with their start and end apart: 2, of which 0 were waited for; matrix products, arithmetic and copies ran while one was open for 0% of the time, Pallas kernels for 9%

profile of v6, /device:TPU:0, one launch (start us, length us, event | category | flops | bytes accessed | tf_op | source)
XLA Modules:
  0.0 30.3 jit_solution(13006757740853935009)
XLA Ops:
  0.0 0.0 copy-start.3
  0.0 0.0 copy-start.2
  0.0 0.0 copy-start.1
  0.0 0.0 copy-start
  0.0 0.8 %copy-done.3 = f32[2,5,8,1,128]{4,3,2,1,0:T(1,128)S(1)} copy-done((f32[2,5,8,1,128]{4,3,2,1,0:T(1,128)S(1)}, f32[2,5,8,1,128]{4,3,2,1,0:T(1,128)}, u32[]{:S(2)}) %copy-start.3) | copy-done | bytes 40984
  0.8 10.9 %all_gather.3.gathered_ref = f32[8,10,1,8,128]{4,3,2,1,0:T(8,128)S(1)} all-gather(f32[1,10,1,8,128]{4,3,2,1,0:T(8,128)S(1)} %bitcast.7), channel_id=1, replica_groups=mesh['member'=8,'tile'=4] {'member'}, dimensions={0}, use_global_device_ids=true | all-gather | bytes 368640 | tf_op jit(solution)/shard_map/all_gather | solution.py:474
  11.7 0.0 copy-done.2
  11.7 0.0 copy-done.1
  11.7 0.0 copy-done
  11.7 1.1 %weigh.1 = (f32[512,128]{1,0:T(8,128)S(1)}, f32[4,4,8,128]{3,2,1,0:T(8,128)S(1)}, f32[4,4,8,128]{3,2,1,0:T(8,128)S(1)}, f32[16,128]{1,0:T(8,128)S(1)}, f32[16,12...) custom-call(s32[8]{0:T(128)S(1)} %copy-done.2, f32[8,10,1,8,128]{4,3,2,1,0:T(8,128)S(1)} %all_gather.3.gathered_ref, ...), custom_call_target="tpu_custom_call" | custom-call | flops 1310720 | bytes 2158624 | tf_op jit(solution)/shard_map/weigh/pallas_call | solution.py:439
  12.8 1.7 %collective-permute-start = (f32[72,128]{1,0:T(8,128)S(1)}, f32[72,128]{1,0:T(8,128)S(1)}, u32[]{:S(2)}, u32[]{:S(2)}) collective-permute-start(f32[72,128]{1,0:T(8,128)S(1)} %get-tuple-element.21), channel_id=1, source_target_pairs={{0,1},{1,0},{2,3},{3,2},{4,5},{5,4},{6,7},{7,6},{8,9},{9,8},{10,11... | collective-permute-start | bytes 110600 | tf_op jit(solution)/shard_map/ppermute | solution.py:486
  14.4 0.1 collective-permute-start.1
  14.5 2.7 %interior.1 = (f32[8,8,8,128]{3,2,1,0:T(8,128)S(1)}, f32[4,4,8,128]{3,2,1,0:T(8,128)S(1)}) custom-call(f32[8,8,8,128]{3,2,1,0:T(8,128)S(1)} %bitcast.6, f32[8,8,128]{2,1,0:T(8,128)S(1)} %copy-done.1, f32[4,4,8,128]{3,2,1,0:T(8,128)S(1)} %get-tuple-element.15.left_ref, f32[4,4,8,128]{3,2,1,0:T(8,128)S(1)} %get-tuple-element.16.right_ref, ...), custom_call_target="tpu_custom_call" | custom-call | flops 5242880 | bytes 770048 | tf_op jit(solution)/shard_map/interior/pallas_call | solution.py:439
  17.2 0.0 collective-permute-done.edge_ref.from_first_ref
  17.2 0.1 early_strips.1.partial_ref
  17.4 0.0 collective-permute-done.1.from_second_ref
  17.4 2.0 %finish.1 = f32[8,10,1,8,128]{4,3,2,1,0:T(8,128)S(1)} custom-call(s32[8]{0:T(128)S(1)} %copy-done.2, bf16[8,10,8,8,128]{4,3,2,1,0:T(8,128)(2,1)S(1)} %bitcast.5, f32[8,8,8,128]{3,2,1,0:T(8,128)S(1)} %early_strips.1.partial_ref, f32[4,4,8,128]{3,2,1,0:T(8,128)S(1)} %get-tuple-element.15.left_ref, f32[4,4,8,128]{3,2,1,0:T(8,128)S(1)} %get-tuple-element.16.right_ref, ...), custom_call_target="tpu_custom_call" | custom-call | flops 1310720 | bytes 2121760 | tf_op jit(solution)/shard_map/finish/pallas_call | solution.py:439
  19.4 10.3 %all_to_all.5 = f32[8,10,1,8,128]{4,3,2,1,0:T(8,128)S(1)} all-to-all(f32[8,10,1,8,128]{4,3,2,1,0:T(8,128)S(1)} %finish.1), channel_id=1, replica_groups=mesh['member'=8,'tile'=4] {'member'}, dimensions={0} | all-to-all | bytes 655360 | tf_op jit(solution)/shard_map/all_to_all | solution.py:518
  29.7 0.6 %broadcast_multiply_fusion = f32[10,8,128]{2,1,0:T(8,128)} fusion(f32[10,8,128]{2,1,0:T(8,128)S(1)} %reduce_sum.9), kind=kLoop, calls=%fused_computation | loop fusion | flops 10240 | bytes 81920 | tf_op jit(solution)/shard_map/mul | solution.py:520
  (2 shorter events, 0.0 us)
Async XLA Ops:
  0.0 0.8 %copy-start.3 = (f32[2,5,8,1,128]{4,3,2,1,0:T(1,128)S(1)}, f32[2,5,8,1,128]{4,3,2,1,0:T(1,128)}, u32[]{:S(2)}) copy-start(f32[2,5,8,1,128]{4,3,2,1,0:T(1,128)} %param.5) | copy-start | bytes 122884
  0.0 11.7 %copy-start.2 = (s32[8]{0:T(128)S(1)}, s32[8]{0:T(128)}, u32[]{:S(2)}) copy-start(s32[8]{0:T(128)} %owner_ref.3) | copy-start | bytes 100
  0.0 11.7 %copy-start.1 = (f32[8,8,128]{2,1,0:T(8,128)S(1)}, f32[8,8,128]{2,1,0:T(8,128)}, u32[]{:S(2)}) copy-start(f32[8,8,128]{2,1,0:T(8,128)} %coeff_ref.3) | copy-start | bytes 98308
  0.0 11.7 %copy-start = (bf16[8,2,5,8,8,128]{5,4,3,2,1,0:T(8,128)(2,1)S(1)}, bf16[8,2,5,8,8,128]{5,4,3,2,1,0:T(8,128)(2,1)}, u32[]{:S(2)}) copy-start(bf16[8,2,5,8,8,128]{5,4,3,2,1,0:T(8,128)(2,1)} %param.4) | copy-start | bytes 3932164
  12.8 4.4 %collective-permute-start = (f32[72,128]{1,0:T(8,128)S(1)}, f32[72,128]{1,0:T(8,128)S(1)}, u32[]{:S(2)}, u32[]{:S(2)}) collective-permute-start(f32[72,128]{1,0:T(8,128)S(1)} %get-tuple-element.21), channel_id=1, source_target_pairs={{0,1},{1,0},{2,3},{3,2},{4,5},{5,4},{6,7},{7,6},{8,9},{9,8},{10,11... | collective-permute-start | bytes 110600 | tf_op jit(solution)/shard_map/ppermute | solution.py:486
  14.4 2.9 %collective-permute-start.1 = (f32[72,128]{1,0:T(8,128)S(1)}, f32[72,128]{1,0:T(8,128)S(1)}, u32[]{:S(2)}, u32[]{:S(2)}) collective-permute-start(f32[72,128]{1,0:T(8,128)S(1)} %get-tuple-element.22), channel_id=1, source_target_pairs={{0,4},{1,2},{2,1},{3,7},{4,0},{5,6},{6,5},{7,3},{8,12},{9,10},{10,... | collective-permute-start | bytes 110600 | tf_op jit(solution)/shard_map/ppermute | solution.py:486

commit v7 on v3

--- a/solution.py
+++ b/solution.py
@@ -94,6 +94,10 @@
 def without_partner(is_left, n_tile):
     tile = lax.axis_index("tile")
     return jnp.where(is_left, tile == 0, tile == n_tile - 1)
+
+
+def exchanged(values):
+    return jnp.swapaxes(jnp.stack(values, axis=0), 0, 1)
 
 
 def total(terms):
@@ -159,26 +163,23 @@
     slab_rows = gathered_ref.shape[2]
     strip_levels, strip_rows = left_ref.shape[:2]
     left_first = jnp.broadcast_to(first_is_left(), (8, lanes))
-    for slab in range(rows // slab_rows):
-        owner = owner_ref[slab]
-        for term in range(terms):
-            for inner in range(slab_rows):
-                row = slab * slab_rows + inner
-                grad_ref[pl.ds(term * levels * rows + row, levels, stride=rows), :] = gathered_ref[
-                    owner, term, inner
-                ]
+    owners = [owner_ref[slab] for slab in range(rows // slab_rows)]
+    for term in range(terms):
+        found = [gathered_ref[owner, term, inner] for owner in owners for inner in range(slab_rows)]
+        grad_ref[term] = exchanged(found)
 
     for level in range(levels):
-        base = level * rows
         coeff = coeff_ref[level]
-        gradients = [
-            coeff * grad_ref[pl.ds(term * levels * rows + base, rows), :] for term in range(terms)
-        ]
-        for member in range(members):
-            field_ref[pl.ds(base * members + member, rows, stride=members), :] = total(
-                pert_ref[member, term, level].astype(jnp.float32) * gradients[term]
-                for term in range(terms)
-            )
+        gradients = [coeff * grad_ref[term, level] for term in range(terms)]
+        field_ref[level] = exchanged(
+            [
+                total(
+                    pert_ref[member, term, level].astype(jnp.float32) * gradients[term]
+                    for term in range(terms)
+                )
+                for member in range(members)
+            ]
+        )
 
     pairs = strip_levels * strip_rows // 2
     fields, coeffs = [], []
@@ -187,7 +188,7 @@
             index = level * strip_rows + row
             cells = mirrors(level, row, levels, rows)
             field = own_strips(
-                [field_ref[pl.ds((l * rows + r) * members, members), :] for l, r in cells]
+                [field_ref[l, r] for l, r in cells]
             )
             coeff = own_strips([spread(coeff_ref[l, pl.ds(r, 1), :]) for l, r in cells])
             fields.append(field[0])
@@ -344,29 +345,23 @@
                     lane_roll(left_end, -part * g),
                     lane_roll(right_end, -part * g),
                 )
-                local_ref[pl.ds((l * rows + r) * members, members), :] = jnp.where(
+                local_ref[l, r] = jnp.where(
                     (lane < SWEEPS) | (lane >= lanes - SWEEPS), ends, interior_ref[l, r]
                 )
 
     for level in range(levels):
-        base = level * rows
-        fields = [
-            local_ref[pl.ds(base * members + member, rows, stride=members), :]
-            for member in range(members)
-        ]
+        fields = exchanged([local_ref[level, row] for row in range(rows)])
         for term in range(terms):
-            sum_ref[pl.ds(term * levels * rows + base, rows), :] = total(
+            sum_ref[term, level] = total(
                 pert_ref[member, term, level].astype(jnp.float32) * fields[member]
                 for member in range(members)
             )
-    for slab in range(rows // slab_rows):
-        owner = owner_ref[slab]
-        for term in range(terms):
+    owners = [owner_ref[slab] for slab in range(rows // slab_rows)]
+    for term in range(terms):
+        found = exchanged([sum_ref[term, level] for level in range(levels)])
+        for slab, owner in enumerate(owners):
             for inner in range(slab_rows):
-                row = slab * slab_rows + inner
-                out_ref[owner, term, inner] = sum_ref[
-                    pl.ds(term * levels * rows + row, levels, stride=rows), :
-                ]
+                out_ref[owner, term, inner] = found[slab * slab_rows + inner]
 
 
 def local_call(kernel, name, outs, scratch, operands, places, work):
@@ -403,10 +398,9 @@
     wide_strip = (strip_levels, strip_rows, members, lanes)
     coeff_strip = (strips, lanes)
     wide_field = (levels, rows, members, lanes)
-    flat_field = (levels * rows * members, lanes)
     field_coeff = (levels, rows, lanes)
     edge_shape = (strips // 2 * (members + 1), lanes)
-    grad_shape = (terms * levels * rows, lanes)
+    grad_shape = (terms, levels, rows, lanes)
     vmem, smem = pltpu.VMEM, pltpu.SMEM
 
     pert = perturbations.reshape(members, terms, levels, rows, lanes)
@@ -417,7 +411,7 @@
     field, left, right, coeff_left, coeff_right, to_first, to_second = local_call(
         weigh_kernel,
         "weigh",
-        [flat_field, wide_strip, wide_strip, coeff_strip, coeff_strip, edge_shape, edge_shape],
+        [wide_field, wide_strip, wide_strip, coeff_strip, coeff_strip, edge_shape, edge_shape],
         [grad_shape],
         (slab_owner, gathered, pert, diffusivity, anchor),
         (smem, vmem, vmem, vmem, vmem),
@@ -433,7 +427,7 @@
         "interior",
         [wide_field],
         [wide_field, field_coeff, field_coeff, field_coeff],
-        (field.reshape(wide_field), diffusivity),
+        (field, diffusivity),
         (vmem,) * 2,
         8 * SWEEPS * members * cells,
     )
@@ -441,7 +435,7 @@
         finish_kernel,
         "finish",
         [(n_member, terms, slab_rows, levels, lanes)],
-        [flat_field, grad_shape] + [wide_strip] * 4,
+        [wide_field, grad_shape] + [wide_strip] * 4,
         (
             slab_owner,
             pert,

time: 30.3 us -> 30.3 us (level)
  no operation moved by 1% of the time
where the time goes in v7:
time: 30.3 us; the launch traced here: 30 us
  blocking collectives  21.1 us (70%)
  Pallas kernels  5.15 us (17%)
  starting transfers between devices  1.72 us (6%)
  local copies, waits for them, and re-layouts  0.78 us (3%)
  other arithmetic  0.64 us (2%)
  waiting for transfers between devices  0.54 us (2%)
    all_gather x1, blocking collectives, body(): gathered = lax.all_gather(slab, 'member', axis=0, tiled=False)  10.9 us
    all_to_all x1, blocking collectives, body(): received = lax.all_to_all(sums, 'member', 0, 0, tiled=True)  10.2 us
    pallas_call x4, Pallas kernels, local_call(): pl.pallas_call(kernel, out_shape=shapes[0] if single else shapes, in_spec...  5.15 us
    ppermute x2, starting transfers between devices, body(): lax.ppermute(edges, ('member', 'tile'), swap_pairs(start, n_member, n_tile))  1.72 us
    unnamed x8, local copies, waits for them, and re-layouts  0.78 us
    mul x1, other arithmetic, body(): owned = jnp.sum(received, axis=0) * norm_factor  0.62 us
  transfers between devices with their start and end apart: 2, of which 1 were waited for; matrix products, arithmetic and copies ran while one was open for 0% of the time, Pallas kernels for 6%

profile of v7, /device:TPU:0, one launch (start us, length us, event | category | flops | bytes accessed | tf_op | source)
XLA Modules:
  0.0 30.0 jit_solution(3086585027025804038)
XLA Ops:
  0.0 0.0 copy-start.3
  0.0 0.0 copy-start.2
  0.0 0.0 copy-start.1
  0.0 0.0 copy-start
  0.0 0.8 %copy-done.3 = f32[2,5,8,1,128]{4,3,2,1,0:T(1,128)S(1)} copy-done((f32[2,5,8,1,128]{4,3,2,1,0:T(1,128)S(1)}, f32[2,5,8,1,128]{4,3,2,1,0:T(1,128)}, u32[]{:S(2)}) %copy-start.3) | copy-done | bytes 40984
  0.8 10.9 %all_gather.3.gathered_ref = f32[8,10,1,8,128]{4,3,2,1,0:T(8,128)S(1)} all-gather(f32[1,10,1,8,128]{4,3,2,1,0:T(8,128)S(1)} %bitcast.5), channel_id=1, replica_groups=mesh['member'=8,'tile'=4] {'member'}, dimensions={0}, use_global_device_ids=true | all-gather | bytes 368640 | tf_op jit(solution)/shard_map/all_gather | solution.py:409
  11.7 0.0 copy-done.2
  11.7 0.0 copy-done.1
  11.7 0.0 copy-done
  11.7 1.1 %weigh.1 = (f32[8,8,8,128]{3,2,1,0:T(8,128)S(1)}, f32[4,4,8,128]{3,2,1,0:T(8,128)S(1)}, f32[4,4,8,128]{3,2,1,0:T(8,128)S(1)}, f32[16,128]{1,0:T(8,128)S(1)}, f32...) custom-call(s32[8]{0:T(128)S(1)} %copy-done.2, ...), custom_call_target="tpu_custom_call" | custom-call | flops 1310720 | bytes 2158624 | tf_op jit(solution)/shard_map/weigh/pallas_call | solution.py:375
  12.8 1.7 %collective-permute-start = (f32[72,128]{1,0:T(8,128)S(1)}, f32[72,128]{1,0:T(8,128)S(1)}, u32[]{:S(2)}, u32[]{:S(2)}) collective-permute-start(f32[72,128]{1,0:T(8,128)S(1)} %get-tuple-element.17), channel_id=1, source_target_pairs={{0,1},{1,0},{2,3},{3,2},{4,5},{5,4},{6,7},{7,6},{8,9},{9,8},{10,11... | collective-permute-start | bytes 110600 | tf_op jit(solution)/shard_map/ppermute | solution.py:421
  14.4 0.1 collective-permute-start.1
  14.5 1.8 %interior.1.interior_ref = f32[8,8,8,128]{3,2,1,0:T(8,128)S(1)} custom-call(f32[8,8,8,128]{3,2,1,0:T(8,128)S(1)} %get-tuple-element.12.field_ref, f32[8,8,128]{2,1,0:T(8,128)S(1)} %copy-done.1), custom_call_target="tpu_custom_call" | custom-call | flops 5242880 | bytes 557056 | tf_op jit(solution)/shard_map/interior/pallas_call | solution.py:375
  16.3 0.5 %collective-permute-done.from_first_ref = f32[72,128]{1,0:T(8,128)S(1)} collective-permute-done((f32[72,128]{1,0:T(8,128)S(1)}, f32[72,128]{1,0:T(8,128)S(1)}, u32[]{:S(2)}, u32[]{:S(2)}) %collective-permute-start) | collective-permute-done | bytes 36896 | tf_op jit(solution)/shard_map/ppermute | solution.py:421
  16.8 0.0 collective-permute-done.1.from_second_ref
  16.8 2.3 %finish.1 = f32[8,10,1,8,128]{4,3,2,1,0:T(8,128)S(1)} custom-call(s32[8]{0:T(128)S(1)} %copy-done.2, bf16[8,10,8,8,128]{4,3,2,1,0:T(8,128)(2,1)S(1)} %bitcast.4, f32[8,8,8,128]{3,2,1,0:T(8,128)S(1)} %interior.1.interior_ref, f32[4,4,8,128]{3,2,1,0:T(8,128)S(1)} %get-tuple-element.13.left_ref, f32[4,4,8,128]{3,2,1,0:T(8,128)S(1)} %get-tuple-element.14.right_ref, ...), custom_call_target="tpu_custom_call" | custom-call | flops 1310720 | bytes 2121760 | tf_op jit(solution)/shard_map/finish/pallas_call | solution.py:375
  19.1 10.2 %all_to_all.5 = f32[8,10,1,8,128]{4,3,2,1,0:T(8,128)S(1)} all-to-all(f32[8,10,1,8,128]{4,3,2,1,0:T(8,128)S(1)} %finish.1), channel_id=1, replica_groups=mesh['member'=8,'tile'=4] {'member'}, dimensions={0} | all-to-all | bytes 655360 | tf_op jit(solution)/shard_map/all_to_all | solution.py:453
  29.3 0.6 %broadcast_multiply_fusion = f32[10,8,128]{2,1,0:T(8,128)} fusion(f32[10,8,128]{2,1,0:T(8,128)S(1)} %reduce_sum.9), kind=kLoop, calls=%fused_computation | loop fusion | flops 10240 | bytes 81920 | tf_op jit(solution)/shard_map/mul | solution.py:455
  (2 shorter events, 0.0 us)
Async XLA Ops:
  0.0 0.8 %copy-start.3 = (f32[2,5,8,1,128]{4,3,2,1,0:T(1,128)S(1)}, f32[2,5,8,1,128]{4,3,2,1,0:T(1,128)}, u32[]{:S(2)}) copy-start(f32[2,5,8,1,128]{4,3,2,1,0:T(1,128)} %param.5) | copy-start | bytes 122884
  0.0 11.7 %copy-start.2 = (s32[8]{0:T(128)S(1)}, s32[8]{0:T(128)}, u32[]{:S(2)}) copy-start(s32[8]{0:T(128)} %owner_ref.3) | copy-start | bytes 100
  0.0 11.7 %copy-start.1 = (f32[8,8,128]{2,1,0:T(8,128)S(1)}, f32[8,8,128]{2,1,0:T(8,128)}, u32[]{:S(2)}) copy-start(f32[8,8,128]{2,1,0:T(8,128)} %coeff_ref.3) | copy-start | bytes 98308
  0.0 11.7 %copy-start = (bf16[8,2,5,8,8,128]{5,4,3,2,1,0:T(8,128)(2,1)S(1)}, bf16[8,2,5,8,8,128]{5,4,3,2,1,0:T(8,128)(2,1)}, u32[]{:S(2)}) copy-start(bf16[8,2,5,8,8,128]{5,4,3,2,1,0:T(8,128)(2,1)} %param.4) | copy-start | bytes 3932164
  12.8 4.0 %collective-permute-start = (f32[72,128]{1,0:T(8,128)S(1)}, f32[72,128]{1,0:T(8,128)S(1)}, u32[]{:S(2)}, u32[]{:S(2)}) collective-permute-start(f32[72,128]{1,0:T(8,128)S(1)} %get-tuple-element.17), channel_id=1, source_target_pairs={{0,1},{1,0},{2,3},{3,2},{4,5},{5,4},{6,7},{7,6},{8,9},{9,8},{10,11... | collective-permute-start | bytes 110600 | tf_op jit(solution)/shard_map/ppermute | solution.py:421
  14.4 2.4 %collective-permute-start.1 = (f32[72,128]{1,0:T(8,128)S(1)}, f32[72,128]{1,0:T(8,128)S(1)}, u32[]{:S(2)}, u32[]{:S(2)}) collective-permute-start(f32[72,128]{1,0:T(8,128)S(1)} %get-tuple-element.18), channel_id=1, source_target_pairs={{0,4},{1,2},{2,1},{3,7},{4,0},{5,6},{6,5},{7,3},{8,12},{9,10},{10,... | collective-permute-start | bytes 110600 | tf_op jit(solution)/shard_map/ppermute | solution.py:421

commit v8 on v3

--- a/solution.py
+++ b/solution.py
@@ -158,9 +158,14 @@
     members, terms, levels, rows, lanes = pert_ref.shape
     slab_rows = gathered_ref.shape[2]
     strip_levels, strip_rows = left_ref.shape[:2]
+    owner_row = owner_ref[...].astype(jnp.float32)
+    place = lane_index(owner_row.shape)
+    owners = [
+        jnp.sum(jnp.where(place == slab, owner_row, 0.0)).astype(jnp.int32)
+        for slab in range(rows // slab_rows)
+    ]
     left_first = jnp.broadcast_to(first_is_left(), (8, lanes))
-    for slab in range(rows // slab_rows):
-        owner = owner_ref[slab]
+    for slab, owner in enumerate(owners):
         for term in range(terms):
             for inner in range(slab_rows):
                 row = slab * slab_rows + inner
@@ -292,7 +297,7 @@
 
 
 def finish_kernel(
-    owner_ref,
+    owner_hbm,
     pert_ref,
     interior_ref,
     left_ref,
@@ -308,11 +313,15 @@
     square_left_ref,
     keep_right_ref,
     square_right_ref,
+    owner_ref,
+    owner_sem,
 ):
     members, terms, levels, rows, lanes = pert_ref.shape
     slab_rows = out_ref.shape[2]
     part = lanes // GROUPS
     left_first = first_is_left()
+    owner_copy = pltpu.make_async_copy(owner_hbm, owner_ref, owner_sem)
+    owner_copy.start()
 
     def edge_reader(is_left):
         outside = without_partner(is_left, lax.axis_size("tile"))
@@ -359,6 +368,7 @@
                 pert_ref[member, term, level].astype(jnp.float32) * fields[member]
                 for member in range(members)
             )
+    owner_copy.wait()
     for slab in range(rows // slab_rows):
         owner = owner_ref[slab]
         for term in range(terms):
@@ -407,7 +417,7 @@
     field_coeff = (levels, rows, lanes)
     edge_shape = (strips // 2 * (members + 1), lanes)
     grad_shape = (terms * levels * rows, lanes)
-    vmem, smem = pltpu.VMEM, pltpu.SMEM
+    vmem = pltpu.VMEM
 
     pert = perturbations.reshape(members, terms, levels, rows, lanes)
     slab = gradient_store.reshape(terms, levels, slab_rows, lanes).swapaxes(1, 2)
@@ -419,8 +429,8 @@
         "weigh",
         [flat_field, wide_strip, wide_strip, coeff_strip, coeff_strip, edge_shape, edge_shape],
         [grad_shape],
-        (slab_owner, gathered, pert, diffusivity, anchor),
-        (smem, vmem, vmem, vmem, vmem),
+        (slab_owner.reshape(1, -1), gathered, pert, diffusivity, anchor),
+        (vmem,) * 5,
         2 * terms * members * cells,
     )
     from_first, from_second = (
@@ -441,9 +451,11 @@
         finish_kernel,
         "finish",
         [(n_member, terms, slab_rows, levels, lanes)],
-        [flat_field, grad_shape] + [wide_strip] * 4,
+        [flat_field, grad_shape]
+        + [wide_strip] * 4
+        + [pltpu.SMEM(slab_owner.shape, slab_owner.dtype), pltpu.SemaphoreType.DMA],
         (
-            slab_owner,
+            pltpu.with_memory_space_constraint(slab_owner, pltpu.HBM),
             pert,
             interior,
             left,
@@ -453,7 +465,7 @@
             from_first,
             from_second,
         ),
-        (smem,) + (vmem,) * 8,
+        (pltpu.HBM,) + (vmem,) * 8,
         2 * terms * members * cells,
     )
     received = lax.all_to_all(sums, "member", 0, 0, tiled=True)

time: 30.3 us -> 29.2 us (0.964)
  Pallas kernels: 5.16 us -> 4.05 us
    pallas_call x4, Pallas kernels: 5.16 us -> 4.05 us  [local_call(): pl.pallas_call(kernel, out_shape=shapes[0] if single else shapes, in_spec...]
where the time goes in v8:
time: 29.2 us; the launch traced here: 28.9 us
  blocking collectives  21.1 us (72%)
  Pallas kernels  4.05 us (14%)
  starting transfers between devices  1.71 us (6%)
  local copies, waits for them, and re-layouts  0.78 us (3%)
  other arithmetic  0.64 us (2%)
  waiting for transfers between devices  0.57 us (2%)
    all_gather x1, blocking collectives, body(): gathered = lax.all_gather(slab, 'member', axis=0, tiled=False)  10.9 us
    all_to_all x1, blocking collectives, body(): received = lax.all_to_all(sums, 'member', 0, 0, tiled=True)  10.2 us
    pallas_call x4, Pallas kernels, local_call(): pl.pallas_call(kernel, out_shape=shapes[0] if single else shapes, in_spec...  4.05 us
    ppermute x2, starting transfers between devices, body(): lax.ppermute(edges, ('member', 'tile'), swap_pairs(start, n_member, n_tile))  1.71 us
    unnamed x8, local copies, waits for them, and re-layouts  0.78 us
    mul x1, other arithmetic, body(): owned = jnp.sum(received, axis=0) * norm_factor  0.62 us
  transfers between devices with their start and end apart: 2, of which 1 were waited for; matrix products, arithmetic and copies ran while one was open for 0% of the time, Pallas kernels for 6%

profile of v8, /device:TPU:0, one launch (start us, length us, event | category | flops | bytes accessed | tf_op | source)
XLA Modules:
  0.0 28.9 jit_solution(14954631394194337565)
XLA Ops:
  0.0 0.0 copy-start.3
  0.0 0.0 copy-start.1
  0.0 0.0 copy-start.2
  0.0 0.0 copy-start
  0.0 0.8 %copy-done.3 = f32[2,5,8,1,128]{4,3,2,1,0:T(1,128)S(1)} copy-done((f32[2,5,8,1,128]{4,3,2,1,0:T(1,128)S(1)}, f32[2,5,8,1,128]{4,3,2,1,0:T(1,128)}, u32[]{:S(2)}) %copy-start.3) | copy-done | bytes 40984
  0.8 10.9 %all_gather.3.gathered_ref = f32[8,10,1,8,128]{4,3,2,1,0:T(8,128)S(1)} all-gather(f32[1,10,1,8,128]{4,3,2,1,0:T(8,128)S(1)} %bitcast.9), channel_id=1, replica_groups=mesh['member'=8,'tile'=4] {'member'}, dimensions={0}, use_global_device_ids=true | all-gather | bytes 368640 | tf_op jit(solution)/shard_map/all_gather | solution.py:425
  11.7 0.0 copy-done.1
  11.7 0.0 copy-done.2
  11.7 0.0 copy-done
  11.7 0.7 %weigh.1 = (f32[512,128]{1,0:T(8,128)S(1)}, f32[4,4,8,128]{3,2,1,0:T(8,128)S(1)}, f32[4,4,8,128]{3,2,1,0:T(8,128)S(1)}, f32[16,128]{1,0:T(8,128)S(1)}, f32[16,12...) custom-call(s32[1,8]{1,0:T(1,128)S(1)} %bitcast.8, f32[8,10,1,8,128]{4,3,2,1,0:T(8,128)S(1)} %all_gather.3.gathered_ref, ...), custom_call_target="tpu_custom_call" | custom-call | flops 1310720 | bytes 2158624 | tf_op jit(solution)/shard_map/weigh/pallas_call | solution.py:390
  12.4 1.6 %collective-permute-start = (f32[72,128]{1,0:T(8,128)S(1)}, f32[72,128]{1,0:T(8,128)S(1)}, u32[]{:S(2)}, u32[]{:S(2)}) collective-permute-start(f32[72,128]{1,0:T(8,128)S(1)} %get-tuple-element.17), channel_id=1, source_target_pairs={{0,1},{1,0},{2,3},{3,2},{4,5},{5,4},{6,7},{7,6},{8,9},{9,8},{10,11... | collective-permute-start | bytes 110600 | tf_op jit(solution)/shard_map/ppermute | solution.py:437
  14.0 0.1 collective-permute-start.1
  14.1 1.7 %interior.1.interior_ref = f32[8,8,8,128]{3,2,1,0:T(8,128)S(1)} custom-call(f32[8,8,8,128]{3,2,1,0:T(8,128)S(1)} %bitcast.7, f32[8,8,128]{2,1,0:T(8,128)S(1)} %copy-done.1), custom_call_target="tpu_custom_call" | custom-call | flops 5242880 | bytes 557056 | tf_op jit(solution)/shard_map/interior/pallas_call | solution.py:390
  15.8 0.6 %collective-permute-done.from_first_ref = f32[72,128]{1,0:T(8,128)S(1)} collective-permute-done((f32[72,128]{1,0:T(8,128)S(1)}, f32[72,128]{1,0:T(8,128)S(1)}, u32[]{:S(2)}, u32[]{:S(2)}) %collective-permute-start) | collective-permute-done | bytes 36896 | tf_op jit(solution)/shard_map/ppermute | solution.py:437
  16.4 0.0 collective-permute-done.1.from_second_ref
  16.4 1.6 %finish.1 = f32[8,10,1,8,128]{4,3,2,1,0:T(8,128)S(1)} custom-call(s32[8]{0:T(128)} %owner_hbm.1, bf16[8,10,8,8,128]{4,3,2,1,0:T(8,128)(2,1)S(1)} %bitcast.6, f32[8,8,8,128]{3,2,1,0:T(8,128)S(1)} %interior.1.interior_ref, f32[4,4,8,128]{3,2,1,0:T(8,128)S(1)} %get-tuple-element.13.left_ref, f32[4,4,8,128]{3,2,1,0:T(8,128)S(1)} %get-tuple-element.14.right_ref, ...), custom_call_target="tpu_custom_call" | custom-call | flops 1310720 | bytes 2121760 | tf_op jit(solution)/shard_map/finish/pallas_call | solution.py:390
  18.0 10.2 %all_to_all.5 = f32[8,10,1,8,128]{4,3,2,1,0:T(8,128)S(1)} all-to-all(f32[8,10,1,8,128]{4,3,2,1,0:T(8,128)S(1)} %finish.1), channel_id=1, replica_groups=mesh['member'=8,'tile'=4] {'member'}, dimensions={0} | all-to-all | bytes 655360 | tf_op jit(solution)/shard_map/all_to_all | solution.py:471
  28.3 0.6 %broadcast_multiply_fusion = f32[10,8,128]{2,1,0:T(8,128)} fusion(f32[10,8,128]{2,1,0:T(8,128)S(1)} %reduce_sum.9), kind=kLoop, calls=%fused_computation | loop fusion | flops 10240 | bytes 81920 | tf_op jit(solution)/shard_map/mul | solution.py:473
  (2 shorter events, 0.0 us)
Async XLA Ops:
  0.0 0.8 %copy-start.3 = (f32[2,5,8,1,128]{4,3,2,1,0:T(1,128)S(1)}, f32[2,5,8,1,128]{4,3,2,1,0:T(1,128)}, u32[]{:S(2)}) copy-start(f32[2,5,8,1,128]{4,3,2,1,0:T(1,128)} %param.5) | copy-start | bytes 122884
  0.0 11.7 %copy-start.1 = (f32[8,8,128]{2,1,0:T(8,128)S(1)}, f32[8,8,128]{2,1,0:T(8,128)}, u32[]{:S(2)}) copy-start(f32[8,8,128]{2,1,0:T(8,128)} %coeff_ref.3) | copy-start | bytes 98308
  0.0 11.7 %copy-start.2 = (s32[8]{0:T(128)S(1)}, s32[8]{0:T(128)}, u32[]{:S(2)}) copy-start(s32[8]{0:T(128)} %owner_hbm.1) | copy-start | bytes 100
  0.0 11.7 %copy-start = (bf16[8,2,5,8,8,128]{5,4,3,2,1,0:T(8,128)(2,1)S(1)}, bf16[8,2,5,8,8,128]{5,4,3,2,1,0:T(8,128)(2,1)}, u32[]{:S(2)}) copy-start(bf16[8,2,5,8,8,128]{5,4,3,2,1,0:T(8,128)(2,1)} %param.4) | copy-start | bytes 3932164
  12.4 4.0 %collective-permute-start = (f32[72,128]{1,0:T(8,128)S(1)}, f32[72,128]{1,0:T(8,128)S(1)}, u32[]{:S(2)}, u32[]{:S(2)}) collective-permute-start(f32[72,128]{1,0:T(8,128)S(1)} %get-tuple-element.17), channel_id=1, source_target_pairs={{0,1},{1,0},{2,3},{3,2},{4,5},{5,4},{6,7},{7,6},{8,9},{9,8},{10,11... | collective-permute-start | bytes 110600 | tf_op jit(solution)/shard_map/ppermute | solution.py:437
  14.0 2.4 %collective-permute-start.1 = (f32[72,128]{1,0:T(8,128)S(1)}, f32[72,128]{1,0:T(8,128)S(1)}, u32[]{:S(2)}, u32[]{:S(2)}) collective-permute-start(f32[72,128]{1,0:T(8,128)S(1)} %get-tuple-element.18), channel_id=1, source_target_pairs={{0,4},{1,2},{2,1},{3,7},{4,0},{5,6},{6,5},{7,3},{8,12},{9,10},{10,... | collective-permute-start | bytes 110600 | tf_op jit(solution)/shard_map/ppermute | solution.py:437

commit v9 on v8

--- a/solution.py
+++ b/solution.py
@@ -9,6 +9,7 @@
 
 SWEEPS = 10
 GROUPS = 4
+ROUNDS = 3
 ANCHOR_WORK = 10**10
 VMEM_LIMIT = 16 * 1024 * 1024
 
@@ -70,22 +71,22 @@
     return jnp.where(halo, lane_roll(edge, -(index % 2) * (part // 2)), own)
 
 
-def swap_sides(values, swapped):
-    first, second = values
-    return jnp.where(swapped, second, first), jnp.where(swapped, first, second)
-
-
-def first_is_left():
-    return lax.axis_index("tile") % 2 == 1
-
-
-def swap_pairs(start, n_member, n_tile):
+def right_round():
+    return lax.axis_index("tile") % ROUNDS
+
+
+def left_round():
+    return (lax.axis_index("tile") + ROUNDS - 1) % ROUNDS
+
+
+def swap_pairs(turn, n_member, n_tile):
     pairs = []
     for member in range(n_member):
         for tile in range(n_tile):
-            other = tile + 1 if (tile - start) % 2 == 0 else tile - 1
-            if 0 <= other < n_tile:
-                pairs.append((member * n_tile + tile, member * n_tile + other))
+            if tile % ROUNDS == turn and tile + 1 < n_tile:
+                pairs.append((member * n_tile + tile, member * n_tile + tile + 1))
+            elif tile > 0 and (tile - 1) % ROUNDS == turn:
+                pairs.append((member * n_tile + tile, member * n_tile + tile - 1))
             elif n_member % 2 == 0:
                 pairs.append((member * n_tile + tile, (member ^ 1) * n_tile + tile))
     return pairs
@@ -151,10 +152,9 @@
     right_ref,
     coeff_left_ref,
     coeff_right_ref,
-    to_first_ref,
-    to_second_ref,
-    grad_ref,
+    *rest,
 ):
+    edge_refs, (grad_ref,) = rest[:ROUNDS], rest[ROUNDS:]
     members, terms, levels, rows, lanes = pert_ref.shape
     slab_rows = gathered_ref.shape[2]
     strip_levels, strip_rows = left_ref.shape[:2]
@@ -164,7 +164,6 @@
         jnp.sum(jnp.where(place == slab, owner_row, 0.0)).astype(jnp.int32)
         for slab in range(rows // slab_rows)
     ]
-    left_first = jnp.broadcast_to(first_is_left(), (8, lanes))
     for slab, owner in enumerate(owners):
         for term in range(terms):
             for inner in range(slab_rows):
@@ -203,11 +202,10 @@
     for pair in range(pairs):
         edges = packed_edges(fields[2 * pair], fields[2 * pair + 1])
         coeff_edges = packed_edges(coeffs[2 * pair], coeffs[2 * pair + 1])
-        edges = swap_sides(edges, left_first)
-        coeff_edges = swap_sides(coeff_edges, left_first)
-        for ref, edge, coeff_edge in zip((to_first_ref, to_second_ref), edges, coeff_edges):
-            ref[pl.ds(pair * members, members), :] = edge
-            ref[pl.ds(pairs * members + pair, 1), :] = coeff_edge[0:1]
+        for turn, ref in enumerate(edge_refs):
+            to_right = jnp.broadcast_to(right_round() == turn, (8, lanes))
+            ref[pl.ds(pair * members, members), :] = jnp.where(to_right, *edges)
+            ref[pl.ds(pairs * members + pair, 1), :] = jnp.where(to_right, *coeff_edges)[0:1]
 
 
 def interior_kernel(
@@ -304,32 +302,25 @@
     right_ref,
     coeff_left_ref,
     coeff_right_ref,
-    from_first_ref,
-    from_second_ref,
-    out_ref,
-    local_ref,
-    sum_ref,
-    keep_left_ref,
-    square_left_ref,
-    keep_right_ref,
-    square_right_ref,
-    owner_ref,
-    owner_sem,
+    *rest,
 ):
+    edge_refs, rest = rest[:ROUNDS], rest[ROUNDS:]
+    out_ref, local_ref, sum_ref, keep_left_ref, square_left_ref = rest[:5]
+    keep_right_ref, square_right_ref, owner_ref, owner_sem = rest[5:]
     members, terms, levels, rows, lanes = pert_ref.shape
     slab_rows = out_ref.shape[2]
     part = lanes // GROUPS
-    left_first = first_is_left()
     owner_copy = pltpu.make_async_copy(owner_hbm, owner_ref, owner_sem)
     owner_copy.start()
 
     def edge_reader(is_left):
         outside = without_partner(is_left, lax.axis_size("tile"))
+        turn = left_round() if is_left else right_round()
 
         def edge_at(place, count):
-            first = from_first_ref[pl.ds(place, count), :]
-            second = from_second_ref[pl.ds(place, count), :]
-            edge = jnp.where(left_first == is_left, first, second)
+            edge = edge_refs[0][pl.ds(place, count), :]
+            for index in range(1, ROUNDS):
+                edge = jnp.where(turn == index, edge_refs[index][pl.ds(place, count), :], edge)
             return jnp.where(outside, 0.0, edge)
 
         return edge_at
@@ -424,19 +415,20 @@
     anchor = local_call(anchor_kernel, "anchor", [(8, lanes)], [], (), (), ANCHOR_WORK)
     gathered = lax.all_gather(slab, "member", axis=0, tiled=False)
 
-    field, left, right, coeff_left, coeff_right, to_first, to_second = local_call(
+    field, left, right, coeff_left, coeff_right, *edges = local_call(
         weigh_kernel,
         "weigh",
-        [flat_field, wide_strip, wide_strip, coeff_strip, coeff_strip, edge_shape, edge_shape],
+        [flat_field, wide_strip, wide_strip, coeff_strip, coeff_strip]
+        + [edge_shape] * ROUNDS,
         [grad_shape],
         (slab_owner.reshape(1, -1), gathered, pert, diffusivity, anchor),
         (vmem,) * 5,
         2 * terms * members * cells,
     )
-    from_first, from_second = (
-        lax.ppermute(edges, ("member", "tile"), swap_pairs(start, n_member, n_tile))
-        for start, edges in ((0, to_first), (1, to_second))
-    )
+    edges = [
+        lax.ppermute(values, ("member", "tile"), swap_pairs(turn, n_member, n_tile))
+        for turn, values in enumerate(edges)
+    ]
 
     interior = local_call(
         interior_kernel,
@@ -462,10 +454,9 @@
             right,
             coeff_left,
             coeff_right,
-            from_first,
-            from_second,
+            *edges,
         ),
-        (pltpu.HBM,) + (vmem,) * 8,
+        (pltpu.HBM,) + (vmem,) * (6 + ROUNDS),
         2 * terms * members * cells,
     )
     received = lax.all_to_all(sums, "member", 0, 0, tiled=True)

time: 29.2 us -> 29.1 us (level)
  starting transfers between devices: 1.71 us -> 2.16 us
  waiting for transfers between devices: 0.57 us -> 0.13 us
    ppermute x2 -> x3, starting transfers between devices: 1.71 us -> 2.16 us  [body(): lax.ppermute(values, ('member', 'tile'), swap_pairs(turn, n_member, n_tile))]
    ppermute x2 -> x3, waiting for transfers between devices: 0.57 us -> 0.13 us  [body(): lax.ppermute(values, ('member', 'tile'), swap_pairs(turn, n_member, n_tile))]
  transfers between devices with their start and end apart: 2 -> 3, of which waited for: 1 -> 1; matrix products, arithmetic and copies ran while one was open for 0% -> 0% of each run, Pallas kernels for 6% -> 6%
where the time goes in v9:
time: 29.1 us; the launch traced here: 28.9 us
  blocking collectives  21.1 us (73%)
  Pallas kernels  4.1 us (14%)
  starting transfers between devices  2.16 us (7%)
  local copies, waits for them, and re-layouts  0.78 us (3%)
  other arithmetic  0.64 us (2%)
    all_gather x1, blocking collectives, body(): gathered = lax.all_gather(slab, 'member', axis=0, tiled=False)  10.9 us
    all_to_all x1, blocking collectives, body(): received = lax.all_to_all(sums, 'member', 0, 0, tiled=True)  10.2 us
    pallas_call x4, Pallas kernels, local_call(): pl.pallas_call(kernel, out_shape=shapes[0] if single else shapes, in_spec...  4.1 us
    ppermute x3, starting transfers between devices, body(): lax.ppermute(values, ('member', 'tile'), swap_pairs(turn, n_member, n_tile))  2.16 us
    unnamed x8, local copies, waits for them, and re-layouts  0.78 us
    mul x1, other arithmetic, body(): owned = jnp.sum(received, axis=0) * norm_factor  0.62 us
  transfers between devices with their start and end apart: 3, of which 1 were waited for; matrix products, arithmetic and copies ran while one was open for 0% of the time, Pallas kernels for 6%

profile of v9, /device:TPU:0, one launch (start us, length us, event | category | flops | bytes accessed | tf_op | source)
XLA Modules:
  0.0 28.9 jit_solution(13576467055398461409)
XLA Ops:
  0.0 0.0 copy-start.3
  0.0 0.0 copy-start.1
  0.0 0.0 copy-start.2
  0.0 0.0 copy-start
  0.0 0.8 %copy-done.3 = f32[2,5,8,1,128]{4,3,2,1,0:T(1,128)S(1)} copy-done((f32[2,5,8,1,128]{4,3,2,1,0:T(1,128)S(1)}, f32[2,5,8,1,128]{4,3,2,1,0:T(1,128)}, u32[]{:S(2)}) %copy-start.3) | copy-done | bytes 40984
  0.8 10.9 %all_gather.3.gathered_ref = f32[8,10,1,8,128]{4,3,2,1,0:T(8,128)S(1)} all-gather(f32[1,10,1,8,128]{4,3,2,1,0:T(8,128)S(1)} %bitcast.9), channel_id=1, replica_groups=mesh['member'=8,'tile'=4] {'member'}, dimensions={0}, use_global_device_ids=true | all-gather | bytes 368640 | tf_op jit(solution)/shard_map/all_gather | solution.py:416
  11.7 0.0 copy-done.1
  11.7 0.0 copy-done.2
  11.7 0.0 copy-done
  11.7 0.7 %weigh.1 = (f32[512,128]{1,0:T(8,128)S(1)}, f32[4,4,8,128]{3,2,1,0:T(8,128)S(1)}, f32[4,4,8,128]{3,2,1,0:T(8,128)S(1)}, f32[16,128]{1,0:T(8,128)S(1)}, f32[16,12...) custom-call(s32[1,8]{1,0:T(1,128)S(1)} %bitcast.8, ...), custom_call_target="tpu_custom_call" | custom-call | flops 1310720 | bytes 2195488 | tf_op jit(solution)/shard_map/weigh/pallas_call | solution.py:381
  12.4 1.6 %collective-permute-start = (f32[72,128]{1,0:T(8,128)S(1)}, f32[72,128]{1,0:T(8,128)S(1)}, u32[]{:S(2)}, u32[]{:S(2)}) collective-permute-start(f32[72,128]{1,0:T(8,128)S(1)} %get-tuple-element.18), channel_id=1, source_target_pairs={{0,1},{1,0},{2,6},{3,7},{4,5},{5,4},{6,2},{7,3},{8,9},{9,8},{10,14... | collective-permute-start | bytes 110600 | tf_op jit(solution)/shard_map/ppermute | solution.py:429
  14.0 0.1 collective-permute-start.1
  14.1 0.4 %collective-permute-start.2 = (f32[72,128]{1,0:T(8,128)S(1)}, f32[72,128]{1,0:T(8,128)S(1)}, u32[]{:S(2)}, u32[]{:S(2)}) collective-permute-start(f32[72,128]{1,0:T(8,128)S(1)} %get-tuple-element.20), channel_id=1, source_target_pairs={{0,4},{1,5},{2,3},{3,2},{4,0},{5,1},{6,7},{7,6},{8,12},{9,13},{10,... | collective-permute-start | bytes 110600 | tf_op jit(solution)/shard_map/ppermute | solution.py:429
  14.5 1.7 %interior.1.interior_ref = f32[8,8,8,128]{3,2,1,0:T(8,128)S(1)} custom-call(f32[8,8,8,128]{3,2,1,0:T(8,128)S(1)} %bitcast.7, f32[8,8,128]{2,1,0:T(8,128)S(1)} %copy-done.1), custom_call_target="tpu_custom_call" | custom-call | flops 5242880 | bytes 557056 | tf_op jit(solution)/shard_map/interior/pallas_call | solution.py:381
  16.3 0.1 collective-permute-done.rest_0_
  16.4 0.0 collective-permute-done.1.rest_1_
  16.4 0.0 collective-permute-done.2.rest_2_
  16.4 1.7 %finish.1 = f32[8,10,1,8,128]{4,3,2,1,0:T(8,128)S(1)} custom-call(s32[8]{0:T(128)} %owner_hbm.1, bf16[8,10,8,8,128]{4,3,2,1,0:T(8,128)(2,1)S(1)} %bitcast.6, f32[8,8,8,128]{3,2,1,0:T(8,128)S(1)} %interior.1.interior_ref, f32[4,4,8,128]{3,2,1,0:T(8,128)S(1)} %get-tuple-element.14.left_ref, f32[4,4,8,128]{3,2,1,0:T(8,128)S(1)} %get-tuple-element.15.right_ref, ...), custom_call_target="tpu_custom_call" | custom-call | flops 1310720 | bytes 2158624 | tf_op jit(solution)/shard_map/finish/pallas_call | solution.py:381
  18.1 10.2 %all_to_all.5 = f32[8,10,1,8,128]{4,3,2,1,0:T(8,128)S(1)} all-to-all(f32[8,10,1,8,128]{4,3,2,1,0:T(8,128)S(1)} %finish.1), channel_id=1, replica_groups=mesh['member'=8,'tile'=4] {'member'}, dimensions={0} | all-to-all | bytes 655360 | tf_op jit(solution)/shard_map/all_to_all | solution.py:462
  28.3 0.6 %broadcast_multiply_fusion = f32[10,8,128]{2,1,0:T(8,128)} fusion(f32[10,8,128]{2,1,0:T(8,128)S(1)} %reduce_sum.9), kind=kLoop, calls=%fused_computation | loop fusion | flops 10240 | bytes 81920 | tf_op jit(solution)/shard_map/mul | solution.py:464
  (2 shorter events, 0.0 us)
Async XLA Ops:
  0.0 0.8 %copy-start.3 = (f32[2,5,8,1,128]{4,3,2,1,0:T(1,128)S(1)}, f32[2,5,8,1,128]{4,3,2,1,0:T(1,128)}, u32[]{:S(2)}) copy-start(f32[2,5,8,1,128]{4,3,2,1,0:T(1,128)} %param.5) | copy-start | bytes 122884
  0.0 11.7 %copy-start.1 = (f32[8,8,128]{2,1,0:T(8,128)S(1)}, f32[8,8,128]{2,1,0:T(8,128)}, u32[]{:S(2)}) copy-start(f32[8,8,128]{2,1,0:T(8,128)} %coeff_ref.3) | copy-start | bytes 98308
  0.0 11.7 %copy-start.2 = (s32[8]{0:T(128)S(1)}, s32[8]{0:T(128)}, u32[]{:S(2)}) copy-start(s32[8]{0:T(128)} %owner_hbm.1) | copy-start | bytes 100
  0.0 11.7 %copy-start = (bf16[8,2,5,8,8,128]{5,4,3,2,1,0:T(8,128)(2,1)S(1)}, bf16[8,2,5,8,8,128]{5,4,3,2,1,0:T(8,128)(2,1)}, u32[]{:S(2)}) copy-start(bf16[8,2,5,8,8,128]{5,4,3,2,1,0:T(8,128)(2,1)} %param.4) | copy-start | bytes 3932164
  12.4 4.0 %collective-permute-start = (f32[72,128]{1,0:T(8,128)S(1)}, f32[72,128]{1,0:T(8,128)S(1)}, u32[]{:S(2)}, u32[]{:S(2)}) collective-permute-start(f32[72,128]{1,0:T(8,128)S(1)} %get-tuple-element.18), channel_id=1, source_target_pairs={{0,1},{1,0},{2,6},{3,7},{4,5},{5,4},{6,2},{7,3},{8,9},{9,8},{10,14... | collective-permute-start | bytes 110600 | tf_op jit(solution)/shard_map/ppermute | solution.py:429
  14.0 2.4 %collective-permute-start.1 = (f32[72,128]{1,0:T(8,128)S(1)}, f32[72,128]{1,0:T(8,128)S(1)}, u32[]{:S(2)}, u32[]{:S(2)}) collective-permute-start(f32[72,128]{1,0:T(8,128)S(1)} %get-tuple-element.19), channel_id=1, source_target_pairs={{0,4},{1,2},{2,1},{3,7},{4,0},{5,6},{6,5},{7,3},{8,12},{9,10},{10,... | collective-permute-start | bytes 110600 | tf_op jit(solution)/shard_map/ppermute | solution.py:429
  14.1 2.3 %collective-permute-start.2 = (f32[72,128]{1,0:T(8,128)S(1)}, f32[72,128]{1,0:T(8,128)S(1)}, u32[]{:S(2)}, u32[]{:S(2)}) collective-permute-start(f32[72,128]{1,0:T(8,128)S(1)} %get-tuple-element.20), channel_id=1, source_target_pairs={{0,4},{1,5},{2,3},{3,2},{4,0},{5,1},{6,7},{7,6},{8,12},{9,13},{10,... | collective-permute-start | bytes 110600 | tf_op jit(solution)/shard_map/ppermute | solution.py:429

commit v10 on v9

--- a/solution.py
+++ b/solution.py
@@ -10,7 +10,7 @@
 SWEEPS = 10
 GROUPS = 4
 ROUNDS = 3
-ANCHOR_WORK = 10**10
+ANCHOR_WORK = 5 * 10**6
 VMEM_LIMIT = 16 * 1024 * 1024
 
 

time: 29.1 us -> 31.6 us (1.086)
  local copies, waits for them, and re-layouts: 0.78 us -> 2.74 us
    unnamed x8 -> x10, local copies, waits for them, and re-layouts: 0.78 us -> 2.74 us
    all_gather x1, blocking collectives: 10.9 us -> 11.2 us  [body(): gathered = lax.all_gather(slab, 'member', axis=0, tiled=False)]
where the time goes in v10:
time: 31.6 us; the launch traced here: 31.2 us
  blocking collectives  21.4 us (68%)
  Pallas kernels  4.1 us (13%)
  local copies, waits for them, and re-layouts  2.74 us (9%)
  starting transfers between devices  2.14 us (7%)
  other arithmetic  0.64 us (2%)
    all_gather x1, blocking collectives, body(): gathered = lax.all_gather(slab, 'member', axis=0, tiled=False)  11.2 us
    all_to_all x1, blocking collectives, body(): received = lax.all_to_all(sums, 'member', 0, 0, tiled=True)  10.2 us
    pallas_call x4, Pallas kernels, local_call(): pl.pallas_call(kernel, out_shape=shapes[0] if single else shapes, in_spec...  4.1 us
    unnamed x10, local copies, waits for them, and re-layouts  2.74 us
    ppermute x3, starting transfers between devices, body(): lax.ppermute(values, ('member', 'tile'), swap_pairs(turn, n_member, n_tile))  2.14 us
  transfers between devices with their start and end apart: 3, of which 1 were waited for; matrix products, arithmetic and copies ran while one was open for 0% of the time, Pallas kernels for 6%

profile of v10, /device:TPU:0, one launch (start us, length us, event | category | flops | bytes accessed | tf_op | source)
XLA Modules:
  0.0 31.2 jit_solution(16235096291258293859)
XLA Ops:
  0.0 0.0 copy-start.3
  0.0 11.2 %all_gather.3.gathered_ref = f32[8,10,1,8,128]{4,3,2,1,0:T(8,128)S(1)} all-gather(f32[1,10,1,8,128]{4,3,2,1,0:T(8,128)} %bitcast.9), channel_id=1, replica_groups=mesh['member'=8,'tile'=4] {'member'}, dimensions={0}, use_global_device_ids=true | all-gather | bytes 368640 | tf_op jit(solution)/shard_map/all_gather | solution.py:416
  11.3 0.0 copy-start
  11.3 1.3 %copy-done = bf16[8,2,5,8,8,128]{5,4,3,2,1,0:T(8,128)(2,1)S(1)} copy-done((bf16[8,2,5,8,8,128]{5,4,3,2,1,0:T(8,128)(2,1)S(1)}, bf16[8,2,5,8,8,128]{5,4,3,2,1,0:T(8,128)(2,1)}, u32[]{:S(2)}) %copy-start) | copy-done | bytes 1310744
  12.6 0.0 copy-start.2
  12.6 0.8 %copy-done.2 = f32[8,8,128]{2,1,0:T(8,128)S(1)} copy-done((f32[8,8,128]{2,1,0:T(8,128)S(1)}, f32[8,8,128]{2,1,0:T(8,128)}, u32[]{:S(2)}) %copy-start.2) | copy-done | bytes 32792
  13.3 0.0 copy-start.4
  13.3 0.7 %copy-done.4 = s32[8]{0:T(128)S(1)} copy-done((s32[8]{0:T(128)S(1)}, s32[8]{0:T(128)}, u32[]{:S(2)}) %copy-start.4) | copy-done | bytes 56
  14.0 0.0 copy-start.1
  14.0 0.7 %weigh.1 = (f32[512,128]{1,0:T(8,128)S(1)}, f32[4,4,8,128]{3,2,1,0:T(8,128)S(1)}, f32[4,4,8,128]{3,2,1,0:T(8,128)S(1)}, f32[16,128]{1,0:T(8,128)S(1)}, f32[16,12...) custom-call(s32[1,8]{1,0:T(1,128)S(1)} %bitcast.8, ...), custom_call_target="tpu_custom_call" | custom-call | flops 1310720 | bytes 2195488 | tf_op jit(solution)/shard_map/weigh/pallas_call | solution.py:381
  14.7 1.6 %collective-permute-start = (f32[72,128]{1,0:T(8,128)S(1)}, f32[72,128]{1,0:T(8,128)S(1)}, u32[]{:S(2)}, u32[]{:S(2)}) collective-permute-start(f32[72,128]{1,0:T(8,128)S(1)} %get-tuple-element.18), channel_id=1, source_target_pairs={{0,1},{1,0},{2,6},{3,7},{4,5},{5,4},{6,2},{7,3},{8,9},{9,8},{10,14... | collective-permute-start | bytes 110600 | tf_op jit(solution)/shard_map/ppermute | solution.py:429
  16.3 0.1 collective-permute-start.1
  16.4 0.4 %collective-permute-start.2 = (f32[72,128]{1,0:T(8,128)S(1)}, f32[72,128]{1,0:T(8,128)S(1)}, u32[]{:S(2)}, u32[]{:S(2)}) collective-permute-start(f32[72,128]{1,0:T(8,128)S(1)} %get-tuple-element.20), channel_id=1, source_target_pairs={{0,4},{1,5},{2,3},{3,2},{4,0},{5,1},{6,7},{7,6},{8,12},{9,13},{10,... | collective-permute-start | bytes 110600 | tf_op jit(solution)/shard_map/ppermute | solution.py:429
  16.8 0.0 copy-done.3
  16.8 1.7 %interior.1.interior_ref = f32[8,8,8,128]{3,2,1,0:T(8,128)S(1)} custom-call(f32[8,8,8,128]{3,2,1,0:T(8,128)S(1)} %bitcast.7, f32[8,8,128]{2,1,0:T(8,128)S(1)} %copy-done.3), custom_call_target="tpu_custom_call" | custom-call | flops 5242880 | bytes 557056 | tf_op jit(solution)/shard_map/interior/pallas_call | solution.py:381
  18.6 0.1 collective-permute-done.rest_0_
  18.7 0.0 collective-permute-done.1.rest_1_
  18.7 0.0 collective-permute-done.2.rest_2_
  18.7 0.0 copy-done.1
  18.7 1.7 %finish.1 = f32[8,10,1,8,128]{4,3,2,1,0:T(8,128)S(1)} custom-call(s32[8]{0:T(128)} %owner_hbm.1, bf16[8,10,8,8,128]{4,3,2,1,0:T(8,128)(2,1)S(1)} %bitcast.6, f32[8,8,8,128]{3,2,1,0:T(8,128)S(1)} %interior.1.interior_ref, f32[4,4,8,128]{3,2,1,0:T(8,128)S(1)} %get-tuple-element.14.left_ref, f32[4,4,8,128]{3,2,1,0:T(8,128)S(1)} %get-tuple-element.15.right_ref, ...), custom_call_target="tpu_custom_call" | custom-call | flops 1310720 | bytes 2158624 | tf_op jit(solution)/shard_map/finish/pallas_call | solution.py:381
  20.4 10.2 %all_to_all.5 = f32[8,10,1,8,128]{4,3,2,1,0:T(8,128)S(1)} all-to-all(f32[8,10,1,8,128]{4,3,2,1,0:T(8,128)S(1)} %finish.1), channel_id=1, replica_groups=mesh['member'=8,'tile'=4] {'member'}, dimensions={0} | all-to-all | bytes 655360 | tf_op jit(solution)/shard_map/all_to_all | solution.py:462
  30.6 0.6 %broadcast_multiply_fusion = f32[10,8,128]{2,1,0:T(8,128)} fusion(f32[10,8,128]{2,1,0:T(8,128)S(1)} %reduce_sum.9), kind=kLoop, calls=%fused_computation | loop fusion | flops 10240 | bytes 81920 | tf_op jit(solution)/shard_map/mul | solution.py:464
  (2 shorter events, 0.0 us)
Async XLA Ops:
  0.0 16.8 %copy-start.3 = (f32[8,8,128]{2,1,0:T(8,128)S(1)}, f32[8,8,128]{2,1,0:T(8,128)}, u32[]{:S(2)}) copy-start(f32[8,8,128]{2,1,0:T(8,128)} %coeff_ref.3) | copy-start | bytes 98308
  11.3 1.3 %copy-start = (bf16[8,2,5,8,8,128]{5,4,3,2,1,0:T(8,128)(2,1)S(1)}, bf16[8,2,5,8,8,128]{5,4,3,2,1,0:T(8,128)(2,1)}, u32[]{:S(2)}) copy-start(bf16[8,2,5,8,8,128]{5,4,3,2,1,0:T(8,128)(2,1)} %param.4) | copy-start | bytes 3932164
  12.6 0.8 %copy-start.2 = (f32[8,8,128]{2,1,0:T(8,128)S(1)}, f32[8,8,128]{2,1,0:T(8,128)}, u32[]{:S(2)}) copy-start(f32[8,8,128]{2,1,0:T(8,128)} %coeff_ref.3) | copy-start | bytes 98308
  13.3 0.7 %copy-start.4 = (s32[8]{0:T(128)S(1)}, s32[8]{0:T(128)}, u32[]{:S(2)}) copy-start(s32[8]{0:T(128)} %owner_hbm.1) | copy-start | bytes 100
  14.0 4.7 %copy-start.1 = (bf16[8,2,5,8,8,128]{5,4,3,2,1,0:T(8,128)(2,1)S(1)}, bf16[8,2,5,8,8,128]{5,4,3,2,1,0:T(8,128)(2,1)}, u32[]{:S(2)}) copy-start(bf16[8,2,5,8,8,128]{5,4,3,2,1,0:T(8,128)(2,1)} %param.4) | copy-start | bytes 3932164
  14.7 4.0 %collective-permute-start = (f32[72,128]{1,0:T(8,128)S(1)}, f32[72,128]{1,0:T(8,128)S(1)}, u32[]{:S(2)}, u32[]{:S(2)}) collective-permute-start(f32[72,128]{1,0:T(8,128)S(1)} %get-tuple-element.18), channel_id=1, source_target_pairs={{0,1},{1,0},{2,6},{3,7},{4,5},{5,4},{6,2},{7,3},{8,9},{9,8},{10,14... | collective-permute-start | bytes 110600 | tf_op jit(solution)/shard_map/ppermute | solution.py:429
  16.3 2.4 %collective-permute-start.1 = (f32[72,128]{1,0:T(8,128)S(1)}, f32[72,128]{1,0:T(8,128)S(1)}, u32[]{:S(2)}, u32[]{:S(2)}) collective-permute-start(f32[72,128]{1,0:T(8,128)S(1)} %get-tuple-element.19), channel_id=1, source_target_pairs={{0,4},{1,2},{2,1},{3,7},{4,0},{5,6},{6,5},{7,3},{8,12},{9,10},{10,... | collective-permute-start | bytes 110600 | tf_op jit(solution)/shard_map/ppermute | solution.py:429
  16.4 2.3 %collective-permute-start.2 = (f32[72,128]{1,0:T(8,128)S(1)}, f32[72,128]{1,0:T(8,128)S(1)}, u32[]{:S(2)}, u32[]{:S(2)}) collective-permute-start(f32[72,128]{1,0:T(8,128)S(1)} %get-tuple-element.20), channel_id=1, source_target_pairs={{0,4},{1,5},{2,3},{3,2},{4,0},{5,1},{6,7},{7,6},{8,12},{9,13},{10,... | collective-permute-start | bytes 110600 | tf_op jit(solution)/shard_map/ppermute | solution.py:429

commit v11 on v9

--- a/solution.py
+++ b/solution.py
@@ -209,9 +209,21 @@
 
 
 def interior_kernel(
-    field_ref, coeff_ref, out_ref, other_ref, keep_ref, square_ref, inverse_ref
+    field_ref,
+    coeff_ref,
+    coeff_left_ref,
+    coeff_right_ref,
+    out_ref,
+    inverse_left_ref,
+    inverse_right_ref,
+    other_ref,
+    keep_ref,
+    square_ref,
+    inverse_ref,
 ):
     levels, rows, members, lanes = field_ref.shape
+    for ref, inverse in ((coeff_left_ref, inverse_left_ref), (coeff_right_ref, inverse_right_ref)):
+        inverse[...] = 1.0 / jnp.where(ref[...] > 0.0, ref[...], 1.0)
     row_index = lax.broadcasted_iota(jnp.int32, (rows, lanes), 0)
     for level in range(levels):
         here = coeff_ref[level]
@@ -250,8 +262,9 @@
 
 
 class Strips:
-    def __init__(self, strip_ref, coeff_ref, edge_at, is_left, keep_ref, square_ref):
+    def __init__(self, strip_ref, coeff_ref, inverse_ref, edge_at, is_left, keep_ref, square_ref):
         self.levels, self.rows, self.members, lanes = strip_ref.shape
+        self.inverse_ref = inverse_ref
         self.coeff_ref, self.keep_ref, self.square_ref = coeff_ref, keep_ref, square_ref
         part = lanes // GROUPS
         pairs = self.levels * self.rows // 2
@@ -290,8 +303,8 @@
         ]
 
     def final(self, level, row):
-        coeff = self.own_coeff(level, row)
-        return self.planes[level][row] / jnp.where(coeff > 0.0, coeff, 1.0)
+        inverse = self.inverse_ref[pl.ds(level * self.rows + row, 1), :]
+        return self.planes[level][row] * spread(inverse, self.members)
 
 
 def finish_kernel(
@@ -302,6 +315,8 @@
     right_ref,
     coeff_left_ref,
     coeff_right_ref,
+    inverse_left_ref,
+    inverse_right_ref,
     *rest,
 ):
     edge_refs, rest = rest[:ROUNDS], rest[ROUNDS:]
@@ -326,10 +341,10 @@
         return edge_at
 
     left = Strips(
-        left_ref, coeff_left_ref, edge_reader(True), True, keep_left_ref, square_left_ref
+        left_ref, coeff_left_ref, inverse_left_ref, edge_reader(True), True, keep_left_ref, square_left_ref
     )
     right = Strips(
-        right_ref, coeff_right_ref, edge_reader(False), False, keep_right_ref, square_right_ref
+        right_ref, coeff_right_ref, inverse_right_ref, edge_reader(False), False, keep_right_ref, square_right_ref
     )
     for _ in range(SWEEPS):
         left.step()
@@ -430,13 +445,13 @@
         for turn, values in enumerate(edges)
     ]
 
-    interior = local_call(
+    interior, inverse_left, inverse_right = local_call(
         interior_kernel,
         "interior",
-        [wide_field],
+        [wide_field, coeff_strip, coeff_strip],
         [wide_field, field_coeff, field_coeff, field_coeff],
-        (field.reshape(wide_field), diffusivity),
-        (vmem,) * 2,
+        (field.reshape(wide_field), diffusivity, coeff_left, coeff_right),
+        (vmem,) * 4,
         8 * SWEEPS * members * cells,
     )
     sums = local_call(
@@ -454,9 +469,11 @@
             right,
             coeff_left,
             coeff_right,
+            inverse_left,
+            inverse_right,
             *edges,
         ),
-        (pltpu.HBM,) + (vmem,) * (6 + ROUNDS),
+        (pltpu.HBM,) + (vmem,) * (8 + ROUNDS),
         2 * terms * members * cells,
     )
     received = lax.all_to_all(sums, "member", 0, 0, tiled=True)

time: 29.1 us -> 29.3 us (level)
  no operation moved by 1% of the time
where the time goes in v11:
time: 29.3 us; the launch traced here: 29.1 us
  blocking collectives  21.1 us (72%)
  Pallas kernels  4.28 us (15%)
  starting transfers between devices  2.16 us (7%)
  local copies, waits for them, and re-layouts  0.78 us (3%)
  other arithmetic  0.64 us (2%)
    all_gather x1, blocking collectives, body(): gathered = lax.all_gather(slab, 'member', axis=0, tiled=False)  10.9 us
    all_to_all x1, blocking collectives, body(): received = lax.all_to_all(sums, 'member', 0, 0, tiled=True)  10.2 us
    pallas_call x4, Pallas kernels, local_call(): pl.pallas_call(kernel, out_shape=shapes[0] if single else shapes, in_spec...  4.28 us
    ppermute x3, starting transfers between devices, body(): lax.ppermute(values, ('member', 'tile'), swap_pairs(turn, n_member, n_tile))  2.16 us
    unnamed x8, local copies, waits for them, and re-layouts  0.78 us
    mul x1, other arithmetic, body(): owned = jnp.sum(received, axis=0) * norm_factor  0.62 us
  transfers between devices with their start and end apart: 3, of which 1 were waited for; matrix products, arithmetic and copies ran while one was open for 0% of the time, Pallas kernels for 6%

profile of v11, /device:TPU:0, one launch (start us, length us, event | category | flops | bytes accessed | tf_op | source)
XLA Modules:
  0.0 29.1 jit_solution(17932517817395178395)
XLA Ops:
  0.0 0.0 copy-start.3
  0.0 0.0 copy-start.1
  0.0 0.0 copy-start.2
  0.0 0.0 copy-start
  0.0 0.8 %copy-done.3 = f32[2,5,8,1,128]{4,3,2,1,0:T(1,128)S(1)} copy-done((f32[2,5,8,1,128]{4,3,2,1,0:T(1,128)S(1)}, f32[2,5,8,1,128]{4,3,2,1,0:T(1,128)}, u32[]{:S(2)}) %copy-start.3) | copy-done | bytes 40984
  0.8 10.9 %all_gather.3.gathered_ref = f32[8,10,1,8,128]{4,3,2,1,0:T(8,128)S(1)} all-gather(f32[1,10,1,8,128]{4,3,2,1,0:T(8,128)S(1)} %bitcast.9), channel_id=1, replica_groups=mesh['member'=8,'tile'=4] {'member'}, dimensions={0}, use_global_device_ids=true | all-gather | bytes 368640 | tf_op jit(solution)/shard_map/all_gather | solution.py:431
  11.7 0.0 copy-done.1
  11.7 0.0 copy-done.2
  11.7 0.0 copy-done
  11.7 0.7 %weigh.1 = (f32[512,128]{1,0:T(8,128)S(1)}, f32[4,4,8,128]{3,2,1,0:T(8,128)S(1)}, f32[4,4,8,128]{3,2,1,0:T(8,128)S(1)}, f32[16,128]{1,0:T(8,128)S(1)}, f32[16,12...) custom-call(s32[1,8]{1,0:T(1,128)S(1)} %bitcast.8, ...), custom_call_target="tpu_custom_call" | custom-call | flops 1310720 | bytes 2195488 | tf_op jit(solution)/shard_map/weigh/pallas_call | solution.py:396
  12.4 1.6 %collective-permute-start = (f32[72,128]{1,0:T(8,128)S(1)}, f32[72,128]{1,0:T(8,128)S(1)}, u32[]{:S(2)}, u32[]{:S(2)}) collective-permute-start(f32[72,128]{1,0:T(8,128)S(1)} %get-tuple-element.24), channel_id=1, source_target_pairs={{0,1},{1,0},{2,6},{3,7},{4,5},{5,4},{6,2},{7,3},{8,9},{9,8},{10,14... | collective-permute-start | bytes 110600 | tf_op jit(solution)/shard_map/ppermute | solution.py:444
  14.0 0.1 collective-permute-start.1
  14.1 0.4 %collective-permute-start.2 = (f32[72,128]{1,0:T(8,128)S(1)}, f32[72,128]{1,0:T(8,128)S(1)}, u32[]{:S(2)}, u32[]{:S(2)}) collective-permute-start(f32[72,128]{1,0:T(8,128)S(1)} %get-tuple-element.26), channel_id=1, source_target_pairs={{0,4},{1,5},{2,3},{3,2},{4,0},{5,1},{6,7},{7,6},{8,12},{9,13},{10,... | collective-permute-start | bytes 110600 | tf_op jit(solution)/shard_map/ppermute | solution.py:444
  14.5 1.7 %interior.1 = (f32[8,8,8,128]{3,2,1,0:T(8,128)S(1)}, f32[16,128]{1,0:T(8,128)S(1)}, f32[16,128]{1,0:T(8,128)S(1)}) custom-call(f32[8,8,8,128]{3,2,1,0:T(8,128)S(1)} %bitcast.7, f32[8,8,128]{2,1,0:T(8,128)S(1)} %copy-done.1, f32[16,128]{1,0:T(8,128)S(1)} %get-tuple-element.17.coeff_left_ref, f32[16,128]{1,0:T(8,128)S(1)} %get-tuple-element.18.coeff_right_ref), custom_call_target="tpu_custom_call" | custom-call | flops 5242880 | bytes 589824 | tf_op jit(solution)/shard_map/interior/pallas_call | solution.py:396
  16.3 0.1 collective-permute-done.rest_0_
  16.4 0.0 collective-permute-done.1.rest_1_
  16.4 0.0 collective-permute-done.2.rest_2_
  16.4 1.8 %finish.1 = f32[8,10,1,8,128]{4,3,2,1,0:T(8,128)S(1)} custom-call(s32[8]{0:T(128)} %owner_hbm.1, bf16[8,10,8,8,128]{4,3,2,1,0:T(8,128)(2,1)S(1)} %bitcast.6, f32[8,8,8,128]{3,2,1,0:T(8,128)S(1)} %get-tuple-element.19.interior_ref, f32[4,4,8,128]{3,2,1,0:T(8,128)S(1)} %get-tuple-element.20.left_ref, f32[4,4,8,128]{3,2,1,0:T(8,128)S(1)} %get-tuple-element.21.right_ref, ...), custom_call_target="tpu_custom_call" | custom-call | flops 1310720 | bytes 2175008 | tf_op jit(solution)/shard_map/finish/pallas_call | solution.py:396
  18.3 10.2 %all_to_all.5 = f32[8,10,1,8,128]{4,3,2,1,0:T(8,128)S(1)} all-to-all(f32[8,10,1,8,128]{4,3,2,1,0:T(8,128)S(1)} %finish.1), channel_id=1, replica_groups=mesh['member'=8,'tile'=4] {'member'}, dimensions={0} | all-to-all | bytes 655360 | tf_op jit(solution)/shard_map/all_to_all | solution.py:479
  28.5 0.6 %broadcast_multiply_fusion = f32[10,8,128]{2,1,0:T(8,128)} fusion(f32[10,8,128]{2,1,0:T(8,128)S(1)} %reduce_sum.9), kind=kLoop, calls=%fused_computation | loop fusion | flops 10240 | bytes 81920 | tf_op jit(solution)/shard_map/mul | solution.py:481
  (2 shorter events, 0.0 us)
Async XLA Ops:
  0.0 0.8 %copy-start.3 = (f32[2,5,8,1,128]{4,3,2,1,0:T(1,128)S(1)}, f32[2,5,8,1,128]{4,3,2,1,0:T(1,128)}, u32[]{:S(2)}) copy-start(f32[2,5,8,1,128]{4,3,2,1,0:T(1,128)} %param.5) | copy-start | bytes 122884
  0.0 11.7 %copy-start.1 = (f32[8,8,128]{2,1,0:T(8,128)S(1)}, f32[8,8,128]{2,1,0:T(8,128)}, u32[]{:S(2)}) copy-start(f32[8,8,128]{2,1,0:T(8,128)} %coeff_ref.3) | copy-start | bytes 98308
  0.0 11.7 %copy-start.2 = (s32[8]{0:T(128)S(1)}, s32[8]{0:T(128)}, u32[]{:S(2)}) copy-start(s32[8]{0:T(128)} %owner_hbm.1) | copy-start | bytes 100
  0.0 11.7 %copy-start = (bf16[8,2,5,8,8,128]{5,4,3,2,1,0:T(8,128)(2,1)S(1)}, bf16[8,2,5,8,8,128]{5,4,3,2,1,0:T(8,128)(2,1)}, u32[]{:S(2)}) copy-start(bf16[8,2,5,8,8,128]{5,4,3,2,1,0:T(8,128)(2,1)} %param.4) | copy-start | bytes 3932164
  12.4 4.0 %collective-permute-start = (f32[72,128]{1,0:T(8,128)S(1)}, f32[72,128]{1,0:T(8,128)S(1)}, u32[]{:S(2)}, u32[]{:S(2)}) collective-permute-start(f32[72,128]{1,0:T(8,128)S(1)} %get-tuple-element.24), channel_id=1, source_target_pairs={{0,1},{1,0},{2,6},{3,7},{4,5},{5,4},{6,2},{7,3},{8,9},{9,8},{10,14... | collective-permute-start | bytes 110600 | tf_op jit(solution)/shard_map/ppermute | solution.py:444
  14.0 2.4 %collective-permute-start.1 = (f32[72,128]{1,0:T(8,128)S(1)}, f32[72,128]{1,0:T(8,128)S(1)}, u32[]{:S(2)}, u32[]{:S(2)}) collective-permute-start(f32[72,128]{1,0:T(8,128)S(1)} %get-tuple-element.25), channel_id=1, source_target_pairs={{0,4},{1,2},{2,1},{3,7},{4,0},{5,6},{6,5},{7,3},{8,12},{9,10},{10,... | collective-permute-start | bytes 110600 | tf_op jit(solution)/shard_map/ppermute | solution.py:444
  14.1 2.3 %collective-permute-start.2 = (f32[72,128]{1,0:T(8,128)S(1)}, f32[72,128]{1,0:T(8,128)S(1)}, u32[]{:S(2)}, u32[]{:S(2)}) collective-permute-start(f32[72,128]{1,0:T(8,128)S(1)} %get-tuple-element.26), channel_id=1, source_target_pairs={{0,4},{1,5},{2,3},{3,2},{4,0},{5,1},{6,7},{7,6},{8,12},{9,13},{10,... | collective-permute-start | bytes 110600 | tf_op jit(solution)/shard_map/ppermute | solution.py:444
